TPU v7x, 32 devices: a whole 2x2x4 slice. The times are simulated.
32 devices in a mesh: gx: 8 (over z, x), gy: 2 (over core), gz: 2 (over y).
Axes of the slice: x: 2, y: 2, z: 4, core: 2. Of those that a mesh axis runs over, the one named last changes fastest.
Arguments:
- e_start: float32 [3, 64, 32, 256], P(None, 'gx', 'gy', 'gz'), may hold values from -6 to 6
- h_start: float32 [3, 64, 32, 256], P(None, 'gx', 'gy', 'gz'), may hold values from -6 to 6
- inv_perm: float32 [3, 64, 32, 256], P(None, 'gx', 'gy', 'gz'), may hold values from 0.25 to 1
- adj_seed: float32 [3, 64, 32, 256], P(None, 'gx', 'gy', 'gz'), may hold values from -6 to 6
- region_ids: int32 [64, 32, 256], P('gx', 'gy', 'gz'), may hold values from 0 to 255, as said below
Outputs:
- e_final: float32 [3, 64, 32, 256], P(None, 'gx', 'gy', 'gz')
- region_grad: float32 [3, 256], P(None, ('gx', 'gy', 'gz'))
Inputs may be any that keep to these rules, and one draw needn't show every extreme that they name: `region_ids`: devices are numbered with gx slowest and gz fastest; region r is owned by device r // 8. Each region's cells lie within the tiles of two neighbouring devices along gx that share their gy and gz indices, the first with an even gx index, and the region is owned by one of those two devices.
All inputs are finite; a program needn't handle non-finite values.
Results may differ from a plain program's by a relative error of at most 0.00013.
Values sent between devices are 32-bit elements; how exact they have to be, the bound alone decides.
No kernel may reach another device: no remote copies, remote signals or barrier semaphores. Data moves between devices by JAX's collectives and lax.ppermute only.
A program may use at most 64 MiB of HBM per device.

v0:
```python
import jax
import jax.numpy as jnp
from jax import lax
from jax.sharding import PartitionSpec as P

STEPS = 4
REG_DEV = 8


time_step = 0.5
grad_scale = 1.0 / 64.0


def with_halo(cells, sides, width):
    for axis, dim in sides:
        count = lax.axis_size(axis)
        ends = count - 1
        head = lax.slice_in_dim(cells, 0, width, axis=dim)
        tail = lax.slice_in_dim(cells, cells.shape[dim] - width, cells.shape[dim], axis=dim)
        cells = jnp.concatenate(
            [
                lax.ppermute(tail, axis, [(i, (i + 1) % count) for i in range(ends)]),
                cells,
                lax.ppermute(head, axis, [((i + 1) % count, i) for i in range(ends)]),
            ],
            axis=dim,
        )
    return cells


def passed_along(shard, axis, by):
    peers = lax.axis_size(axis)
    pairs = [(i, i + by) for i in range(peers) if 0 <= i + by < peers]
    return lax.ppermute(shard, axis, pairs)


def shifted(field_in, leading):
    padded = with_halo(field_in, (("gx", 1), ("gy", 2), ("gz", 3)), 1)
    if leading:
        return (padded[:, 2:, 1:-1, 1:-1], padded[:, 1:-1, 2:, 1:-1], padded[:, 1:-1, 1:-1, 2:])
    return (padded[:, :-2, 1:-1, 1:-1], padded[:, 1:-1, :-2, 1:-1], padded[:, 1:-1, 1:-1, :-2])


def curl_of(field_in, leading):
    nearby = shifted(field_in, leading)
    if leading:
        differences = [other - field_in for other in nearby]
    else:
        differences = [field_in - other for other in nearby]
    curl_first = differences[1][2] - differences[2][1]
    curl_second = differences[2][0] - differences[0][2]
    curl_third = differences[0][1] - differences[1][0]
    return jnp.stack([curl_first, curl_second, curl_third])


def local(e_start, h_start, inv_perm, adj_seed, region_ids):
    e_field, h_field = (e_start, h_start)
    curl_store = []
    for step_index in range(STEPS):
        h_field = h_field - time_step * curl_of(e_field, True)
        curl_now = curl_of(h_field, False)
        curl_store.append(curl_now)
        e_field = e_field + time_step * inv_perm * curl_now
    e_adjoint = adj_seed
    h_adjoint = jnp.zeros_like(adj_seed)
    design_grad = jnp.zeros_like(adj_seed)
    for step_index in range(STEPS - 1, -1, -1):
        design_grad = design_grad + time_step * e_adjoint * curl_store[step_index]
        if step_index > 0:
            merged = h_adjoint + time_step * curl_of(inv_perm * e_adjoint, True)
            e_adjoint = e_adjoint - time_step * curl_of(merged, False)
            h_adjoint = merged
    plane_count = lax.axis_size("gy") * lax.axis_size("gz")
    x_index = lax.axis_index("gx")
    parity = x_index % 2
    own_flat = (
        x_index * plane_count + lax.axis_index("gy") * lax.axis_size("gz") + lax.axis_index("gz")
    )
    first_owner = own_flat - parity * plane_count
    second_owner = first_owner + plane_count
    flat_ids = region_ids.reshape(-1)
    local_ids = jnp.where(
        flat_ids < second_owner * REG_DEV,
        flat_ids - first_owner * REG_DEV,
        flat_ids - second_owner * REG_DEV + REG_DEV,
    )
    slots = lax.broadcasted_iota(jnp.int32, (2 * REG_DEV, flat_ids.shape[0]), 0)
    one_hot = (slots == local_ids[None, :]).astype(jnp.float32)
    flat_grad = design_grad.reshape(3, -1)
    pair_sums = jnp.einsum("cn,rn->cr", flat_grad, one_hot, precision=lax.Precision.HIGHEST)
    is_odd = parity == 1
    outgoing = jnp.where(is_odd, pair_sums[:, :REG_DEV], pair_sums[:, REG_DEV:])
    keeping = jnp.where(is_odd, pair_sums[:, REG_DEV:], pair_sums[:, :REG_DEV])
    from_even = passed_along(outgoing, "gx", 1)
    from_odd = passed_along(outgoing, "gx", -1)
    owned = keeping + jnp.where(is_odd, from_even, from_odd)
    return (e_field, owned * grad_scale)


def solution(mesh):
    placed = (
        P(None, "gx", "gy", "gz"),
        P(None, "gx", "gy", "gz"),
        P(None, "gx", "gy", "gz"),
        P(None, "gx", "gy", "gz"),
        P("gx", "gy", "gz"),
    )
    return jax.shard_map(
        local,
        mesh=mesh,
        in_specs=placed,
        out_specs=(P(None, "gx", "gy", "gz"), P(None, ("gx", "gy", "gz"))),
        check_vma=False,
    )
```

profile of v0, /device:TPU:0, one launch (start us, length us, event | category | flops | bytes accessed | tf_op | source)
XLA Modules:
  0.0 280.8 jit_solution(5416583452780159719)
XLA Ops:
  2.7 5.5 %collective-permute-start = (f32[3,1,16,128]{3,2,1,0:T(8,128)S(1)}, f32[3,1,16,128]{3,2,1,0:T(8,128)S(1)}, u32[]{:S(2)}, u32[]{:S(2)}) collective-permute-start(f32[3,1,16,128]{3,2,1,0:T(8,128)S(1)} %get-tuple-element.145), channel_id=1, source_target_pairs={{0,4},{4,8},{8,12},{12,16},{16,20},{20,24},{24,28},{1,5},{5,9},{9,... | collective-permute-start | bytes 73736 | tf_op jit(solution)/shard_map/ppermute | solution.py:22
  9.2 5.0 %collective-permute-start.40 = (f32[3,1,16,128]{3,2,1,0:T(8,128)S(1)}, f32[3,1,16,128]{3,2,1,0:T(8,128)S(1)}, u32[]{:S(2)}, u32[]{:S(2)}) collective-permute-start(f32[3,1,16,128]{3,2,1,0:T(8,128)S(1)} %get-tuple-element.103), channel_id=1, source_target_pairs={{0,4},{4,8},{8,12},{12,16},{16,20},{20,24},{24,28},{1,5},{5,9},{9,... | collective-permute-start | bytes 73736 | tf_op jit(solution)/shard_map/ppermute | solution.py:22
  27.1 10.7 %collective-permute-done.4 = f32[3,10,18,1]{3,2,1,0:T(8,128)S(1)} collective-permute-done((f32[3,10,18,1]{3,2,1,0:T(8,128)S(1)}, f32[3,10,18,1]{3,2,1,0:T(8,128)S(1)}, u32[]{:S(2)}, u32[]{:S(2)}) %collective-permute-start.4) | collective-permute-done | bytes 2192 | tf_op jit(solution)/shard_map/ppermute | solution.py:24
  39.0 4.5 %collective-permute-start.5 = (f32[3,1,16,128]{3,2,1,0:T(8,128)S(1)}, f32[3,1,16,128]{3,2,1,0:T(8,128)S(1)}, u32[]{:S(2)}, u32[]{:S(2)}) collective-permute-start(f32[3,1,16,128]{3,2,1,0:T(8,128)S(1)} %get-tuple-element.138), channel_id=1, source_target_pairs={{0,4},{4,8},{8,12},{12,16},{16,20},{20,24},{24,28},{1,5},{5,9},{9,... | collective-permute-start | bytes 73736 | tf_op jit(solution)/shard_map/ppermute | solution.py:22
  45.2 4.5 %collective-permute-start.45 = (f32[3,1,16,128]{3,2,1,0:T(8,128)S(1)}, f32[3,1,16,128]{3,2,1,0:T(8,128)S(1)}, u32[]{:S(2)}, u32[]{:S(2)}) collective-permute-start(f32[3,1,16,128]{3,2,1,0:T(8,128)S(1)} %get-tuple-element.98), channel_id=1, source_target_pairs={{0,4},{4,8},{8,12},{12,16},{16,20},{20,24},{24,28},{1,5},{5,9},{9,... | collective-permute-start | bytes 73736 | tf_op jit(solution)/shard_map/ppermute | solution.py:22
  62.0 6.9 %collective-permute-done.9 = f32[3,10,18,1]{3,2,1,0:T(8,128)S(1)} collective-permute-done((f32[3,10,18,1]{3,2,1,0:T(8,128)S(1)}, f32[3,10,18,1]{3,2,1,0:T(8,128)S(1)}, u32[]{:S(2)}, u32[]{:S(2)}) %collective-permute-start.9) | collective-permute-done | bytes 2192 | tf_op jit(solution)/shard_map/ppermute | solution.py:22
  69.1 7.7 %collective-permute-done.49 = f32[3,10,18,1]{3,2,1,0:T(8,128)S(1)} collective-permute-done((f32[3,10,18,1]{3,2,1,0:T(8,128)S(1)}, f32[3,10,18,1]{3,2,1,0:T(8,128)S(1)}, u32[]{:S(2)}, u32[]{:S(2)}) %collective-permute-start.49) | collective-permute-done | bytes 2192 | tf_op jit(solution)/shard_map/ppermute | solution.py:22
  78.1 4.8 %collective-permute-start.10 = (f32[3,1,16,128]{3,2,1,0:T(8,128)S(1)}, f32[3,1,16,128]{3,2,1,0:T(8,128)S(1)}, u32[]{:S(2)}, u32[]{:S(2)}) collective-permute-start(f32[3,1,16,128]{3,2,1,0:T(8,128)S(1)} %get-tuple-element.133), channel_id=1, source_target_pairs={{0,4},{4,8},{8,12},{12,16},{16,20},{20,24},{24,28},{1,5},{5,9},{9,... | collective-permute-start | bytes 73736 | tf_op jit(solution)/shard_map/ppermute | solution.py:22
  84.3 5.2 %collective-permute-start.50 = (f32[3,1,16,128]{3,2,1,0:T(8,128)S(1)}, f32[3,1,16,128]{3,2,1,0:T(8,128)S(1)}, u32[]{:S(2)}, u32[]{:S(2)}) collective-permute-start(f32[3,1,16,128]{3,2,1,0:T(8,128)S(1)} %get-tuple-element.91), channel_id=1, source_target_pairs={{0,4},{4,8},{8,12},{12,16},{16,20},{20,24},{24,28},{1,5},{5,9},{9,... | collective-permute-start | bytes 73736 | tf_op jit(solution)/shard_map/ppermute | solution.py:22
  103.2 10.7 %collective-permute-done.14 = f32[3,10,18,1]{3,2,1,0:T(8,128)S(1)} collective-permute-done((f32[3,10,18,1]{3,2,1,0:T(8,128)S(1)}, f32[3,10,18,1]{3,2,1,0:T(8,128)S(1)}, u32[]{:S(2)}, u32[]{:S(2)}) %collective-permute-start.14) | collective-permute-done | bytes 2192 | tf_op jit(solution)/shard_map/ppermute | solution.py:24
  114.2 4.8 %collective-permute-start.15 = (f32[3,1,16,128]{3,2,1,0:T(8,128)S(1)}, f32[3,1,16,128]{3,2,1,0:T(8,128)S(1)}, u32[]{:S(2)}, u32[]{:S(2)}) collective-permute-start(f32[3,1,16,128]{3,2,1,0:T(8,128)S(1)} %get-tuple-element.128), channel_id=1, source_target_pairs={{0,4},{4,8},{8,12},{12,16},{16,20},{20,24},{24,28},{1,5},{5,9},{9,... | collective-permute-start | bytes 73736 | tf_op jit(solution)/shard_map/ppermute | solution.py:22
  120.7 5.2 %collective-permute-start.55 = (f32[3,1,16,128]{3,2,1,0:T(8,128)S(1)}, f32[3,1,16,128]{3,2,1,0:T(8,128)S(1)}, u32[]{:S(2)}, u32[]{:S(2)}) collective-permute-start(f32[3,1,16,128]{3,2,1,0:T(8,128)S(1)} %get-tuple-element.86), channel_id=1, source_target_pairs={{0,4},{4,8},{8,12},{12,16},{16,20},{20,24},{24,28},{1,5},{5,9},{9,... | collective-permute-start | bytes 73736 | tf_op jit(solution)/shard_map/ppermute | solution.py:22
  138.6 6.9 %collective-permute-done.19 = f32[3,10,18,1]{3,2,1,0:T(8,128)S(1)} collective-permute-done((f32[3,10,18,1]{3,2,1,0:T(8,128)S(1)}, f32[3,10,18,1]{3,2,1,0:T(8,128)S(1)}, u32[]{:S(2)}, u32[]{:S(2)}) %collective-permute-start.19) | collective-permute-done | bytes 2192 | tf_op jit(solution)/shard_map/ppermute | solution.py:22
  145.7 7.7 %collective-permute-done.59 = f32[3,10,18,1]{3,2,1,0:T(8,128)S(1)} collective-permute-done((f32[3,10,18,1]{3,2,1,0:T(8,128)S(1)}, f32[3,10,18,1]{3,2,1,0:T(8,128)S(1)}, u32[]{:S(2)}, u32[]{:S(2)}) %collective-permute-start.59) | collective-permute-done | bytes 2192 | tf_op jit(solution)/shard_map/ppermute | solution.py:22
  153.7 4.8 %collective-permute-start.20 = (f32[3,1,16,128]{3,2,1,0:T(8,128)S(1)}, f32[3,1,16,128]{3,2,1,0:T(8,128)S(1)}, u32[]{:S(2)}, u32[]{:S(2)}) collective-permute-start(f32[3,1,16,128]{3,2,1,0:T(8,128)S(1)} %get-tuple-element.123), channel_id=1, source_target_pairs={{0,4},{4,8},{8,12},{12,16},{16,20},{20,24},{24,28},{1,5},{5,9},{9,... | collective-permute-start | bytes 73736 | tf_op jit(solution)/shard_map/ppermute | solution.py:22
  160.1 4.8 %collective-permute-done.21 = f32[3,1,16,128]{3,2,1,0:T(8,128)S(1)} collective-permute-done((f32[3,1,16,128]{3,2,1,0:T(8,128)S(1)}, f32[3,1,16,128]{3,2,1,0:T(8,128)S(1)}, u32[]{:S(2)}, u32[]{:S(2)}) %collective-permute-start.21) | collective-permute-done | bytes 24608 | tf_op jit(solution)/shard_map/ppermute | solution.py:24
  169.3 4.8 %collective-permute-start.60 = (f32[3,1,16,128]{3,2,1,0:T(8,128)S(1)}, f32[3,1,16,128]{3,2,1,0:T(8,128)S(1)}, u32[]{:S(2)}, u32[]{:S(2)}) collective-permute-start(f32[3,1,16,128]{3,2,1,0:T(8,128)S(1)} %get-tuple-element.79), channel_id=1, source_target_pairs={{0,4},{4,8},{8,12},{12,16},{16,20},{20,24},{24,28},{1,5},{5,9},{9,... | collective-permute-start | bytes 73736 | tf_op jit(solution)/shard_map/ppermute | solution.py:22
  187.4 4.3 %collective-permute-start.25 = (f32[3,1,16,128]{3,2,1,0:T(8,128)S(1)}, f32[3,1,16,128]{3,2,1,0:T(8,128)S(1)}, u32[]{:S(2)}, u32[]{:S(2)}) collective-permute-start(f32[3,1,16,128]{3,2,1,0:T(8,128)S(1)} %get-tuple-element.118), channel_id=1, source_target_pairs={{0,4},{4,8},{8,12},{12,16},{16,20},{20,24},{24,28},{1,5},{5,9},{9,... | collective-permute-start | bytes 73736 | tf_op jit(solution)/shard_map/ppermute | solution.py:22
  205.1 6.6 %collective-permute-done.29 = f32[3,10,18,1]{3,2,1,0:T(8,128)S(1)} collective-permute-done((f32[3,10,18,1]{3,2,1,0:T(8,128)S(1)}, f32[3,10,18,1]{3,2,1,0:T(8,128)S(1)}, u32[]{:S(2)}, u32[]{:S(2)}) %collective-permute-start.29) | collective-permute-done | bytes 2192 | tf_op jit(solution)/shard_map/ppermute | solution.py:22
  212.0 4.5 %collective-permute-start.30 = (f32[3,1,16,128]{3,2,1,0:T(8,128)S(1)}, f32[3,1,16,128]{3,2,1,0:T(8,128)S(1)}, u32[]{:S(2)}, u32[]{:S(2)}) collective-permute-start(f32[3,1,16,128]{3,2,1,0:T(8,128)S(1)} %get-tuple-element.113), channel_id=1, source_target_pairs={{0,4},{4,8},{8,12},{12,16},{16,20},{20,24},{24,28},{1,5},{5,9},{9,... | collective-permute-start | bytes 73736 | tf_op jit(solution)/shard_map/ppermute | solution.py:22
  218.0 4.4 %collective-permute-done.31 = f32[3,1,16,128]{3,2,1,0:T(8,128)S(1)} collective-permute-done((f32[3,1,16,128]{3,2,1,0:T(8,128)S(1)}, f32[3,1,16,128]{3,2,1,0:T(8,128)S(1)}, u32[]{:S(2)}, u32[]{:S(2)}) %collective-permute-start.31) | collective-permute-done | bytes 24608 | tf_op jit(solution)/shard_map/ppermute | solution.py:24
  226.8 4.8 %collective-permute-start.65 = (f32[3,1,16,128]{3,2,1,0:T(8,128)S(1)}, f32[3,1,16,128]{3,2,1,0:T(8,128)S(1)}, u32[]{:S(2)}, u32[]{:S(2)}) collective-permute-start(f32[3,1,16,128]{3,2,1,0:T(8,128)S(1)} %get-tuple-element.74), channel_id=1, source_target_pairs={{0,4},{4,8},{8,12},{12,16},{16,20},{20,24},{24,28},{1,5},{5,9},{9,... | collective-permute-start | bytes 73736 | tf_op jit(solution)/shard_map/ppermute | solution.py:22
  240.0 4.7 %collective-permute-done.34 = f32[3,10,18,1]{3,2,1,0:T(8,128)S(1)} collective-permute-done((f32[3,10,18,1]{3,2,1,0:T(8,128)S(1)}, f32[3,10,18,1]{3,2,1,0:T(8,128)S(1)}, u32[]{:S(2)}, u32[]{:S(2)}) %collective-permute-start.34) | collective-permute-done | bytes 2192 | tf_op jit(solution)/shard_map/ppermute | solution.py:24
  263.0 6.4 %collective-permute-done.39 = f32[3,10,18,1]{3,2,1,0:T(8,128)S(1)} collective-permute-done((f32[3,10,18,1]{3,2,1,0:T(8,128)S(1)}, f32[3,10,18,1]{3,2,1,0:T(8,128)S(1)}, u32[]{:S(2)}, u32[]{:S(2)}) %collective-permute-start.39) | collective-permute-done | bytes 2192 | tf_op jit(solution)/shard_map/ppermute | solution.py:22
  (219 shorter events, 138.3 us)
Async XLA Ops:
  1.4 14.2 %collective-permute-start.1 = (f32[3,1,16,128]{3,2,1,0:T(8,128)S(1)}, f32[3,1,16,128]{3,2,1,0:T(8,128)S(1)}, u32[]{:S(2)}, u32[]{:S(2)}) collective-permute-start(f32[3,1,16,128]{3,2,1,0:T(8,128)S(1)} %get-tuple-element.144), channel_id=1, source_target_pairs={{4,0},{8,4},{12,8},{16,12},{20,16},{24,20},{28,24},{5,1},{9,5},{13... | collective-permute-start | bytes 73736 | tf_op jit(solution)/shard_map/ppermute | solution.py:24
  2.7 12.8 %collective-permute-start = (f32[3,1,16,128]{3,2,1,0:T(8,128)S(1)}, f32[3,1,16,128]{3,2,1,0:T(8,128)S(1)}, u32[]{:S(2)}, u32[]{:S(2)}) collective-permute-start(f32[3,1,16,128]{3,2,1,0:T(8,128)S(1)} %get-tuple-element.145), channel_id=1, source_target_pairs={{0,4},{4,8},{8,12},{12,16},{16,20},{20,24},{24,28},{1,5},{5,9},{9,... | collective-permute-start | bytes 73736 | tf_op jit(solution)/shard_map/ppermute | solution.py:22
  9.2 10.7 %collective-permute-start.40 = (f32[3,1,16,128]{3,2,1,0:T(8,128)S(1)}, f32[3,1,16,128]{3,2,1,0:T(8,128)S(1)}, u32[]{:S(2)}, u32[]{:S(2)}) collective-permute-start(f32[3,1,16,128]{3,2,1,0:T(8,128)S(1)} %get-tuple-element.103), channel_id=1, source_target_pairs={{0,4},{4,8},{8,12},{12,16},{16,20},{20,24},{24,28},{1,5},{5,9},{9,... | collective-permute-start | bytes 73736 | tf_op jit(solution)/shard_map/ppermute | solution.py:22
  24.4 13.4 %collective-permute-start.4 = (f32[3,10,18,1]{3,2,1,0:T(8,128)S(1)}, f32[3,10,18,1]{3,2,1,0:T(8,128)S(1)}, u32[]{:S(2)}, u32[]{:S(2)}) collective-permute-start(f32[3,10,18,1]{3,2,1,0:T(8,128)S(1)} %pad_maximum_fusion.52), channel_id=1, source_target_pairs={{1,0},{3,2},{5,4},{7,6},{9,8},{11,10},{13,12},{15,14},{17,16},{19,... | collective-permute-start | bytes 6488 | tf_op jit(solution)/shard_map/ppermute | solution.py:24
  25.8 19.1 %collective-permute-start.44 = (f32[3,10,18,1]{3,2,1,0:T(8,128)S(1)}, f32[3,10,18,1]{3,2,1,0:T(8,128)S(1)}, u32[]{:S(2)}, u32[]{:S(2)}) collective-permute-start(f32[3,10,18,1]{3,2,1,0:T(8,128)S(1)} %pad_maximum_fusion.20), channel_id=1, source_target_pairs={{1,0},{3,2},{5,4},{7,6},{9,8},{11,10},{13,12},{15,14},{17,16},{19,... | collective-permute-start | bytes 6488 | tf_op jit(solution)/shard_map/ppermute | solution.py:24
  39.0 12.0 %collective-permute-start.5 = (f32[3,1,16,128]{3,2,1,0:T(8,128)S(1)}, f32[3,1,16,128]{3,2,1,0:T(8,128)S(1)}, u32[]{:S(2)}, u32[]{:S(2)}) collective-permute-start(f32[3,1,16,128]{3,2,1,0:T(8,128)S(1)} %get-tuple-element.138), channel_id=1, source_target_pairs={{0,4},{4,8},{8,12},{12,16},{16,20},{20,24},{24,28},{1,5},{5,9},{9,... | collective-permute-start | bytes 73736 | tf_op jit(solution)/shard_map/ppermute | solution.py:22
  58.8 10.1 %collective-permute-start.9 = (f32[3,10,18,1]{3,2,1,0:T(8,128)S(1)}, f32[3,10,18,1]{3,2,1,0:T(8,128)S(1)}, u32[]{:S(2)}, u32[]{:S(2)}) collective-permute-start(f32[3,10,18,1]{3,2,1,0:T(8,128)S(1)} %pad_maximum_fusion.48), channel_id=1, source_target_pairs={{0,1},{2,3},{4,5},{6,7},{8,9},{10,11},{12,13},{14,15},{16,17},{18,... | collective-permute-start | bytes 6488 | tf_op jit(solution)/shard_map/ppermute | solution.py:22
  60.5 16.3 %collective-permute-start.49 = (f32[3,10,18,1]{3,2,1,0:T(8,128)S(1)}, f32[3,10,18,1]{3,2,1,0:T(8,128)S(1)}, u32[]{:S(2)}, u32[]{:S(2)}) collective-permute-start(f32[3,10,18,1]{3,2,1,0:T(8,128)S(1)} %pad_maximum_fusion.16), channel_id=1, source_target_pairs={{0,1},{2,3},{4,5},{6,7},{8,9},{10,11},{12,13},{14,15},{16,17},{18,... | collective-permute-start | bytes 6488 | tf_op jit(solution)/shard_map/ppermute | solution.py:22
  78.1 12.7 %collective-permute-start.10 = (f32[3,1,16,128]{3,2,1,0:T(8,128)S(1)}, f32[3,1,16,128]{3,2,1,0:T(8,128)S(1)}, u32[]{:S(2)}, u32[]{:S(2)}) collective-permute-start(f32[3,1,16,128]{3,2,1,0:T(8,128)S(1)} %get-tuple-element.133), channel_id=1, source_target_pairs={{0,4},{4,8},{8,12},{12,16},{16,20},{20,24},{24,28},{1,5},{5,9},{9,... | collective-permute-start | bytes 73736 | tf_op jit(solution)/shard_map/ppermute | solution.py:22
  84.3 10.9 %collective-permute-start.50 = (f32[3,1,16,128]{3,2,1,0:T(8,128)S(1)}, f32[3,1,16,128]{3,2,1,0:T(8,128)S(1)}, u32[]{:S(2)}, u32[]{:S(2)}) collective-permute-start(f32[3,1,16,128]{3,2,1,0:T(8,128)S(1)} %get-tuple-element.91), channel_id=1, source_target_pairs={{0,4},{4,8},{8,12},{12,16},{16,20},{20,24},{24,28},{1,5},{5,9},{9,... | collective-permute-start | bytes 73736 | tf_op jit(solution)/shard_map/ppermute | solution.py:22
  100.5 13.4 %collective-permute-start.14 = (f32[3,10,18,1]{3,2,1,0:T(8,128)S(1)}, f32[3,10,18,1]{3,2,1,0:T(8,128)S(1)}, u32[]{:S(2)}, u32[]{:S(2)}) collective-permute-start(f32[3,10,18,1]{3,2,1,0:T(8,128)S(1)} %pad_maximum_fusion.44), channel_id=1, source_target_pairs={{1,0},{3,2},{5,4},{7,6},{9,8},{11,10},{13,12},{15,14},{17,16},{19,... | collective-permute-start | bytes 6488 | tf_op jit(solution)/shard_map/ppermute | solution.py:24
  101.9 18.5 %collective-permute-start.54 = (f32[3,10,18,1]{3,2,1,0:T(8,128)S(1)}, f32[3,10,18,1]{3,2,1,0:T(8,128)S(1)}, u32[]{:S(2)}, u32[]{:S(2)}) collective-permute-start(f32[3,10,18,1]{3,2,1,0:T(8,128)S(1)} %pad_maximum_fusion.12), channel_id=1, source_target_pairs={{1,0},{3,2},{5,4},{7,6},{9,8},{11,10},{13,12},{15,14},{17,16},{19,... | collective-permute-start | bytes 6488 | tf_op jit(solution)/shard_map/ppermute | solution.py:24
  114.2 12.9 %collective-permute-start.15 = (f32[3,1,16,128]{3,2,1,0:T(8,128)S(1)}, f32[3,1,16,128]{3,2,1,0:T(8,128)S(1)}, u32[]{:S(2)}, u32[]{:S(2)}) collective-permute-start(f32[3,1,16,128]{3,2,1,0:T(8,128)S(1)} %get-tuple-element.128), channel_id=1, source_target_pairs={{0,4},{4,8},{8,12},{12,16},{16,20},{20,24},{24,28},{1,5},{5,9},{9,... | collective-permute-start | bytes 73736 | tf_op jit(solution)/shard_map/ppermute | solution.py:22
  135.3 10.1 %collective-permute-start.19 = (f32[3,10,18,1]{3,2,1,0:T(8,128)S(1)}, f32[3,10,18,1]{3,2,1,0:T(8,128)S(1)}, u32[]{:S(2)}, u32[]{:S(2)}) collective-permute-start(f32[3,10,18,1]{3,2,1,0:T(8,128)S(1)} %pad_maximum_fusion.40), channel_id=1, source_target_pairs={{0,1},{2,3},{4,5},{6,7},{8,9},{10,11},{12,13},{14,15},{16,17},{18,... | collective-permute-start | bytes 6488 | tf_op jit(solution)/shard_map/ppermute | solution.py:22
  137.1 16.3 %collective-permute-start.59 = (f32[3,10,18,1]{3,2,1,0:T(8,128)S(1)}, f32[3,10,18,1]{3,2,1,0:T(8,128)S(1)}, u32[]{:S(2)}, u32[]{:S(2)}) collective-permute-start(f32[3,10,18,1]{3,2,1,0:T(8,128)S(1)} %pad_maximum_fusion.8), channel_id=1, source_target_pairs={{0,1},{2,3},{4,5},{6,7},{8,9},{10,11},{12,13},{14,15},{16,17},{18,... | collective-permute-start | bytes 6488 | tf_op jit(solution)/shard_map/ppermute | solution.py:22
  164.9 10.5 %collective-permute-start.22 = (f32[3,10,1,128]{3,2,1,0:T(1,128)S(1)}, f32[3,10,1,128]{3,2,1,0:T(1,128)S(1)}, u32[]{:S(2)}, u32[]{:S(2)}) collective-permute-start(f32[3,10,1,128]{3,2,1,0:T(1,128)S(1)} %get-tuple-element.49), channel_id=1, source_target_pairs={{2,0},{3,1},{6,4},{7,5},{10,8},{11,9},{14,12},{15,13},{18,16},{19,... | collective-permute-start | bytes 46088 | tf_op jit(solution)/shard_map/ppermute | solution.py:24
  175.5 11.6 %collective-permute-start.24 = (f32[3,10,18,1]{3,2,1,0:T(8,128)S(1)}, f32[3,10,18,1]{3,2,1,0:T(8,128)S(1)}, u32[]{:S(2)}, u32[]{:S(2)}) collective-permute-start(f32[3,10,18,1]{3,2,1,0:T(8,128)S(1)} %pad_maximum_fusion.36), channel_id=1, source_target_pairs={{1,0},{3,2},{5,4},{7,6},{9,8},{11,10},{13,12},{15,14},{17,16},{19,... | collective-permute-start | bytes 6488 | tf_op jit(solution)/shard_map/ppermute | solution.py:24
  179.8 13.1 %collective-permute-start.62 = (f32[3,10,1,128]{3,2,1,0:T(1,128)S(1)}, f32[3,10,1,128]{3,2,1,0:T(1,128)S(1)}, u32[]{:S(2)}, u32[]{:S(2)}) collective-permute-start(f32[3,10,1,128]{3,2,1,0:T(1,128)S(1)} %get-tuple-element.33), channel_id=1, source_target_pairs={{2,0},{3,1},{6,4},{7,5},{10,8},{11,9},{14,12},{15,13},{18,16},{19,... | collective-permute-start | bytes 46088 | tf_op jit(solution)/shard_map/ppermute | solution.py:24
  181.1 11.8 %collective-permute-start.63 = (f32[3,10,1,128]{3,2,1,0:T(1,128)S(1)}, f32[3,10,1,128]{3,2,1,0:T(1,128)S(1)}, u32[]{:S(2)}, u32[]{:S(2)}) collective-permute-start(f32[3,10,1,128]{3,2,1,0:T(1,128)S(1)} %get-tuple-element.32), channel_id=1, source_target_pairs={{0,2},{1,3},{4,6},{5,7},{8,10},{9,11},{12,14},{13,15},{16,18},{17,... | collective-permute-start | bytes 46088 | tf_op jit(solution)/shard_map/ppermute | solution.py:22
  193.1 10.1 %collective-permute-start.64 = (f32[3,10,18,1]{3,2,1,0:T(8,128)S(1)}, f32[3,10,18,1]{3,2,1,0:T(8,128)S(1)}, u32[]{:S(2)}, u32[]{:S(2)}) collective-permute-start(f32[3,10,18,1]{3,2,1,0:T(8,128)S(1)} %pad_maximum_fusion.4), channel_id=1, source_target_pairs={{1,0},{3,2},{5,4},{7,6},{9,8},{11,10},{13,12},{15,14},{17,16},{19,... | collective-permute-start | bytes 6488 | tf_op jit(solution)/shard_map/ppermute | solution.py:24
  222.5 10.5 %collective-permute-start.32 = (f32[3,10,1,128]{3,2,1,0:T(1,128)S(1)}, f32[3,10,1,128]{3,2,1,0:T(1,128)S(1)}, u32[]{:S(2)}, u32[]{:S(2)}) collective-permute-start(f32[3,10,1,128]{3,2,1,0:T(1,128)S(1)} %get-tuple-element.45), channel_id=1, source_target_pairs={{2,0},{3,1},{6,4},{7,5},{10,8},{11,9},{14,12},{15,13},{18,16},{19,... | collective-permute-start | bytes 46088 | tf_op jit(solution)/shard_map/ppermute | solution.py:24
  233.1 11.6 %collective-permute-start.34 = (f32[3,10,18,1]{3,2,1,0:T(8,128)S(1)}, f32[3,10,18,1]{3,2,1,0:T(8,128)S(1)}, u32[]{:S(2)}, u32[]{:S(2)}) collective-permute-start(f32[3,10,18,1]{3,2,1,0:T(8,128)S(1)} %pad_maximum_fusion.28), channel_id=1, source_target_pairs={{1,0},{3,2},{5,4},{7,6},{9,8},{11,10},{13,12},{15,14},{17,16},{19,... | collective-permute-start | bytes 6488 | tf_op jit(solution)/shard_map/ppermute | solution.py:24
  237.4 13.2 %collective-permute-start.67 = (f32[3,10,1,128]{3,2,1,0:T(1,128)S(1)}, f32[3,10,1,128]{3,2,1,0:T(1,128)S(1)}, u32[]{:S(2)}, u32[]{:S(2)}) collective-permute-start(f32[3,10,1,128]{3,2,1,0:T(1,128)S(1)} %get-tuple-element.31), channel_id=1, source_target_pairs={{0,2},{1,3},{4,6},{5,7},{8,10},{9,11},{12,14},{13,15},{16,18},{17,... | collective-permute-start | bytes 46088 | tf_op jit(solution)/shard_map/ppermute | solution.py:22
  238.7 11.9 %collective-permute-start.68 = (f32[3,10,1,128]{3,2,1,0:T(1,128)S(1)}, f32[3,10,1,128]{3,2,1,0:T(1,128)S(1)}, u32[]{:S(2)}, u32[]{:S(2)}) collective-permute-start(f32[3,10,1,128]{3,2,1,0:T(1,128)S(1)} %get-tuple-element.30), channel_id=1, source_target_pairs={{2,0},{3,1},{6,4},{7,5},{10,8},{11,9},{14,12},{15,13},{18,16},{19,... | collective-permute-start | bytes 46088 | tf_op jit(solution)/shard_map/ppermute | solution.py:24
  (53 other events, 328.0 us)
where the time goes:
time: 283 us; the launch traced here: 281 us
  starting transfers between devices  160 us (57%)
  waiting for transfers between devices  107 us (38%)
  other arithmetic  8.33 us (3%)
    ppermute x35, starting transfers between devices, with_halo(): lax.ppermute(tail, axis, [(i, (i + 1) % count) for i in range(ends)])  109 us
    ppermute x35, waiting for transfers between devices, with_halo(): lax.ppermute(head, axis, [((i + 1) % count, i) for i in range(ends)])  60.2 us
    ppermute x35, starting transfers between devices, with_halo(): lax.ppermute(head, axis, [((i + 1) % count, i) for i in range(ends)])  45.2 us
    ppermute x35, waiting for transfers between devices, with_halo(): lax.ppermute(tail, axis, [(i, (i + 1) % count) for i in range(ends)])  43.2 us
  transfers between devices with their start and end apart: 72, of which 25 were waited for; matrix products, arithmetic and copies ran while one was open for 2% of the time, Pallas kernels for 0%

commit v1 on v0

v1 whole, which is shorter than its diff:
```python
import functools

import jax
import jax.numpy as jnp
from jax import lax
from jax.experimental import pallas as pl
from jax.experimental.pallas import tpu as pltpu
from jax.sharding import PartitionSpec as P

STEPS = 4
REG_DEV = 8
DEEP = 4
EDGE = 4
UNROLL = 2

COUNTS = ((4, 4, 4), (3, 4, 4), (3, 3, 3), (3, 3, 3))
SLOTS = []
for _f in range(4):
    for _c in range(3):
        SLOTS.append((_f, _c, COUNTS[_f][_c], sum(s[2] for s in SLOTS)))
N_SLOTS = sum(s[2] for s in SLOTS)

grad_scale = 1.0 / 64.0
F32 = jnp.float32


def lanes_of(shape):
    return lax.broadcasted_iota(jnp.int32, shape, len(shape) - 1)


def rows_of(shape):
    return lax.broadcasted_iota(jnp.int32, shape, len(shape) - 2)


def pack_kernel(meta, e, h, ip, sd, a_out, b_out, z_out, y_out):
    even, gz = meta[0], meta[1]
    refs = (e, h, ip, sd)
    cx = e.shape[1]
    for f, c, k, off in SLOTS:
        top, bottom = cx - k, 0
        a_base = jnp.where(even == 1, top, bottom)
        b_base = jnp.where(even == 1, bottom, top)
        a_out[off : off + k] = refs[f][c, pl.ds(a_base, k)]
        b_out[off : off + k] = refs[f][c, pl.ds(b_base, k)]
    group = lanes_of((16, 128)) // EDGE
    z_off = jnp.where(gz == 0, EDGE, 0)
    for t in range(3):
        total = jnp.zeros((16, 128), F32)
        for k in range(4):
            f, c = divmod(4 * t + k, 3)
            for x in range(cx):
                moved = pltpu.roll(refs[f][c, x], (16 * x + 4 * k + z_off) % 128, 1)
                total = jnp.where(group == 4 * x + k, moved, total)
        z_out[t] = total
    first = rows_of((cx, 8, 128)) < EDGE
    for f in range(4):
        for c in range(3):
            q = 3 * f + c
            y_out[q * cx : (q + 1) * cx] = jnp.where(first, refs[f][c, :, 0:8], refs[f][c, :, 8:16])


def roll_up(v, axis):
    return pltpu.roll(v, v.shape[axis] - 1, axis)


def roll_down(v, axis):
    return pltpu.roll(v, 1, axis)


def curl_f(v, nxt, shift_y, shift_z):
    vx, vy, vz = v
    ny, nz = nxt
    return (
        (shift_y(vz) - vz) - (shift_z(vy) - vy),
        (shift_z(vx) - vx) - (nz - vz),
        (ny - vy) - (shift_y(vx) - vx),
    )


def curl_b(v, prv, shift_y, shift_z):
    vx, vy, vz = v
    py, pz = prv
    return (
        (vz - shift_y(vz)) - (vy - shift_z(vy)),
        (vx - shift_z(vx)) - (vz - pz),
        (vy - py) - (vx - shift_y(vx)),
    )


def run_kernel(meta, e_in, h_in, ip_in, sd_in, ids, a_in, b_in, z_in, za_in, zb_in, y1, y2,
               e_out, s_out, E, H, I, W, M, PS, G, SE, SH, SI, SW, SM, SP, SG):
    even, gz = meta[0], meta[1]
    low_x, keep_hi, keep_lo, low_y = meta[2], meta[3], meta[4], meta[5]
    first_owner, second_owner = meta[6], meta[7]
    cx = e_in.shape[1]
    shape = (24, 128)
    lane = lanes_of(shape)
    row = rows_of(shape)

    def y_part(v):
        r = rows_of(v.shape)
        keep = jnp.where(r < EDGE, keep_hi, keep_lo) == 1
        return jnp.where(keep, v, 0.0)

    ext = (E, H, I, PS.at[STEPS - 1])
    ins = (e_in, h_in, ip_in, sd_in)
    for f, c, k, off in SLOTS:
        X = ext[f]
        if k < DEEP:
            X[c, 0] = jnp.zeros(shape, F32)
            X[c, cx + 2 * DEEP - 1] = jnp.zeros(shape, F32)
        X[c, cx + 2 * DEEP] = jnp.zeros(shape, F32)
        q = 3 * f + c
        X[c, DEEP : DEEP + cx, 0:16] = ins[f][c]
        X[c, DEEP : DEEP + cx, 16:24] = y_part(y1[q * cx : (q + 1) * cx])
        a_base = jnp.where(even == 1, DEEP + cx, DEEP - k)
        b_base = jnp.where(even == 1, DEEP - k, DEEP + cx)
        X[c, pl.ds(a_base, k), 0:16] = a_in[off : off + k]
        X[c, pl.ds(a_base, k), 16:24] = y_part(y2[off : off + k])
        X[c, pl.ds(b_base, k), 0:16] = b_in[off : off + k]
        X[c, pl.ds(b_base, k), 16:24] = y_part(y2[N_SLOTS + off : N_SLOTS + off + k])

    zs = 2 * N_SLOTS
    is_even = even == 1
    own_off = jnp.where(gz == 0, 8, 4)
    own_j = jnp.where(gz == 0, 0, 4)
    got_j = jnp.where(gz == 0, 8, 0)
    j = lane % 16
    is_own = (j >= own_j) & (j < own_j + 8)
    is_got = (j >= got_j) & (j < got_j + EDGE)

    def with_y(ref, i, at):
        return jnp.concatenate([ref[i], y_part(y2[at])], axis=0)

    def strip_of(f, c, z_tiles):
        k = (3 * f + c) % 4
        tiles = []
        for t in range(2):
            acc = jnp.zeros(shape, F32)
            for x in range(8):
                moved = pltpu.roll(ext[f][c, 8 * t + x], (16 * x + own_off) % 128, 1)
                acc = jnp.where(lane // 16 == x, moved, acc)
            got = pltpu.roll(z_tiles[t], (got_j - 4 * k + 128) % 128, 1)
            tiles.append(jnp.where(is_own, acc, jnp.where(is_got, got, 0.0)))
        return jnp.concatenate(tiles, axis=1)

    strips = (SE, SH, SI, SP.at[STEPS - 1])
    for t in range(3):
        own = pltpu.roll(with_y(z_in, t, zs + t), 64, 1)
        from_a = pltpu.roll(with_y(za_in, t, zs + 3 + t), 64, 1)
        from_b = pltpu.roll(with_y(zb_in, t, zs + 6 + t), 64, 1)
        lower = jnp.where(is_even, from_b, from_a)
        upper = jnp.where(is_even, from_a, from_b)
        z_tiles = (jnp.where(lane < 64, lower, own), jnp.where(lane < 64, own, upper))
        for k in range(4):
            f, c = divmod(4 * t + k, 3)
            strips[f][c] = strip_of(f, c, z_tiles)

    def y_up(v):
        return roll_up(v, 0)

    def y_down(v):
        return roll_down(v, 0)

    def z_up(v):
        return jnp.where(lane == 127, 0.0, roll_up(v, 1))

    def z_down(v):
        return jnp.where(lane == 0, 0.0, roll_down(v, 1))

    def sz_up(v):
        return roll_up(v, 1)

    def sz_down(v):
        return roll_down(v, 1)

    def sx_up(v):
        return pltpu.roll(v, v.shape[1] - 16, 1)

    def sx_down(v):
        return pltpu.roll(v, 16, 1)

    keep_row = jnp.where((row >= 20) & (low_y == 0), 0.0, 1.0)
    s_shape = (24, 256)
    s_keep = jnp.where((rows_of(s_shape) >= 20) & (low_y == 0), 0.0, 1.0)
    s_keep = jnp.where((lanes_of(s_shape) < 16 * DEEP) & (low_x == 0), 0.0, s_keep)

    def keep_at(x):
        return keep_row * jnp.where((x < DEEP) & (low_x == 0), 0.0, 1.0)

    def sweep(lo, count, body):
        full, rest = divmod(count, UNROLL)

        def chunk(i, _):
            body([lo + i * UNROLL + u for u in range(UNROLL)])
            return 0

        lax.fori_loop(0, full, chunk, 0)
        if rest:
            body([lo + full * UNROLL + u for u in range(rest)])

    def get(ref, x, comps=(0, 1, 2)):
        return tuple(ref[c, x] for c in comps)

    def put(ref, xs, values):
        for x, v in zip(xs, values):
            for c in range(3):
                ref[c, x] = v[c]

    def sget(ref):
        return tuple(ref[c] for c in range(3))

    def sput(ref, v):
        for c in range(3):
            ref[c] = v[c]

    def scurl_f(v):
        return curl_f(v, (sx_up(v[1]), sx_up(v[2])), y_up, sz_up)

    def scurl_b(v):
        return curl_b(v, (sx_down(v[1]), sx_down(v[2])), y_down, sz_down)

    def halve(xs):
        new = []
        for x in xs:
            i, p = get(I, x), get(PS.at[STEPS - 1], x)
            half = tuple(0.5 * v for v in i)
            new.append((half, tuple(a * b for a, b in zip(half, p))))
        put(I, xs, [n[0] for n in new])
        put(W, xs, [n[1] for n in new])

    sweep(0, cx + 2 * DEEP, halve)
    half = tuple(0.5 * v for v in sget(SI))
    sput(SI, half)
    sput(SW, tuple(a * b for a, b in zip(half, sget(SP.at[STEPS - 1]))))

    last = cx + 2 * DEEP
    for m in range(STEPS - 1):
        n = STEPS - 1 - m

        def magnetic(xs, m=m):
            new = []
            for x in xs:
                curl = curl_f(get(W, x), get(W, x + 1, (1, 2)), y_up, z_up)
                keep = keep_at(x)
                if m == 0:
                    new.append(tuple(keep * v for v in curl))
                else:
                    new.append(tuple(q + keep * v for q, v in zip(get(M, x), curl)))
            put(M, xs, new)

        def electric(xs, m=m, n=n):
            new = []
            for x in xs:
                curl = curl_b(get(M, x), get(M, x - 1, (1, 2)), y_down, z_down)
                p = tuple(q - 0.5 * v for q, v in zip(get(PS.at[n], x), curl))
                new.append((p, tuple(a * b for a, b in zip(get(I, x), p))))
            put(PS.at[n - 1], xs, [v[0] for v in new])
            if m < STEPS - 2:
                put(W, xs, [v[1] for v in new])

        sweep(1 + m, last - 3 - 2 * m, magnetic)
        curl = scurl_f(sget(SW))
        if m == 0:
            merged = tuple(s_keep * v for v in curl)
        else:
            merged = tuple(q + s_keep * v for q, v in zip(sget(SM), curl))
        sput(SM, merged)
        p = tuple(q - 0.5 * v for q, v in zip(sget(SP.at[n]), scurl_b(merged)))
        sput(SP.at[n - 1], p)
        sput(SW, tuple(a * b for a, b in zip(sget(SI), p)))
        sweep(2 + m, last - 4 - 2 * m, electric)

    for n in range(STEPS):

        def magnetic(xs):
            new = []
            for x in xs:
                curl = curl_f(get(E, x), get(E, x + 1, (1, 2)), y_up, z_up)
                keep = 0.5 * keep_at(x)
                new.append(tuple(q - keep * v for q, v in zip(get(H, x), curl)))
            put(H, xs, new)

        def electric(xs, n=n):
            new = []
            for x in xs:
                curl = curl_b(get(H, x), get(H, x - 1, (1, 2)), y_down, z_down)
                e = tuple(q + i * v for q, i, v in zip(get(E, x), get(I, x), curl))
                g = tuple(p * v for p, v in zip(get(PS.at[n], x), curl))
                if n:
                    g = tuple(o + v for o, v in zip(get(G, x), g))
                new.append((e, g))
            put(E, xs, [v[0] for v in new])
            put(G, xs, [v[1] for v in new])

        sweep(n, last - 1 - 2 * n, magnetic)
        curl = scurl_f(sget(SE))
        sh = tuple(q - 0.5 * s_keep * v for q, v in zip(sget(SH), curl))
        sput(SH, sh)
        curl = scurl_b(sh)
        sput(SE, tuple(q + i * v for q, i, v in zip(sget(SE), sget(SI), curl)))
        g = tuple(p * v for p, v in zip(sget(SP.at[n]), curl))
        if n:
            g = tuple(o + v for o, v in zip(sget(SG), g))
        sput(SG, g)
        sweep(n + 1, last - 2 - 2 * n, electric)

    lane16 = lanes_of((16, 128))
    seam_lo = jnp.where(gz == 0, 128 - EDGE, 0)
    seam = (lane16 >= seam_lo) & (lane16 < seam_lo + EDGE)

    def merged_plane(main, strip, c, x):
        tile, at = divmod(x, 8)
        s = strip[c, 0:16, 128 * tile : 128 * (tile + 1)]
        moved = pltpu.roll(s, (seam_lo - 16 * at - EDGE + 256) % 128, 1)
        return jnp.where(seam, moved, main[c, x, 0:16])

    acc = jnp.zeros((80, 128), F32)
    for x in range(DEEP, DEEP + cx):
        grads = []
        for c in range(3):
            e_out[c, x - DEEP] = merged_plane(E, SE, c, x)
            grads.append(merged_plane(G, SG, c, x))
        lhs, rhs = [], []
        for r in range(2):
            g = jnp.concatenate([v[8 * r : 8 * r + 8] for v in grads], axis=0)
            one = g.astype(jnp.bfloat16).astype(F32)
            rest = g - one
            two = rest.astype(jnp.bfloat16).astype(F32)
            three = rest - two
            lhs.append(jnp.concatenate([one, two, three, jnp.zeros((8, 128), F32)], axis=0).astype(jnp.bfloat16))
            region = ids[x - DEEP, 8 * r : 8 * r + 8]
            slot = jnp.where(
                region < second_owner * REG_DEV,
                region - first_owner * REG_DEV,
                region - second_owner * REG_DEV + REG_DEV,
            )
            hot = jnp.concatenate([jnp.where(slot == s, 1.0, 0.0) for s in range(2 * REG_DEV)], axis=0)
            rhs.append(hot.astype(jnp.bfloat16))
        acc = acc + lax.dot_general(
            jnp.concatenate(lhs, axis=1),
            jnp.concatenate(rhs, axis=1),
            (((1,), (1,)), ((), ())),
            preferred_element_type=F32,
        )
    sums = acc[0:24] + acc[24:48] + acc[48:72]
    sums = jnp.where(rows_of((24, 128)) % 8 == lanes_of((24, 128)) % 8, sums, 0.0)
    parts = [jnp.sum(sums[8 * c : 8 * c + 8], axis=0, keepdims=True) for c in range(3)]
    parts = jnp.concatenate(parts + [jnp.zeros((5, 128), F32)], axis=0)
    fold = jnp.where(rows_of((128, 128)) // 8 == lanes_of((128, 128)), 0.5 * grad_scale, 0.0)
    s_out[...] = jnp.dot(parts, fold, precision=lax.Precision.HIGHEST, preferred_element_type=F32)


def y_rows(v):
    first = lax.broadcasted_iota(jnp.int32, (1, 8, 1), 1) < EDGE
    return jnp.where(first, v[:, 0:8], v[:, 8:16])


def local(e_start, h_start, inv_perm, adj_seed, region_ids):
    n_gx, n_gy, n_gz = (lax.axis_size(a) for a in ("gx", "gy", "gz"))
    xi, yi, zi = (lax.axis_index(a) for a in ("gx", "gy", "gz"))
    cx = e_start.shape[1]
    even = (xi + 1) % 2
    plane_count = n_gy * n_gz
    own_flat = xi * plane_count + yi * n_gz + zi
    first_owner = own_flat - (1 - even) * plane_count
    keep_hi = jnp.where(yi < n_gy - 1, 1, 0)
    keep_lo = jnp.where(yi > 0, 1, 0)
    meta = jnp.stack(
        [even, zi, jnp.where(xi > 0, 1, 0), keep_hi, keep_lo, keep_lo, first_owner, first_owner + plane_count]
    ).astype(jnp.int32)
    smem = pl.BlockSpec(memory_space=pltpu.SMEM)
    vmem = pl.BlockSpec(memory_space=pltpu.VMEM)
    shape = lambda *dims: jax.ShapeDtypeStruct(dims, F32)

    a_pairs = [(i, i ^ 1) for i in range(n_gx)]
    b_pairs = [(i, ((i - 1) ^ 1) + 1) for i in range(1, n_gx - 1)]

    def swap_y(v):
        if n_gy == 2:
            return lax.ppermute(v, "gy", [(0, 1), (1, 0)])
        up = lax.ppermute(v, "gy", [(i, i + 1) for i in range(n_gy - 1)])
        down = lax.ppermute(v, "gy", [(i + 1, i) for i in range(n_gy - 1)])
        first = lax.broadcasted_iota(jnp.int32, (1, 8, 1), 1) < EDGE
        return jnp.where(first, down, up)

    a_msg, b_msg, z_msg, y_msg = pl.pallas_call(
        pack_kernel,
        out_shape=(shape(N_SLOTS, 16, 128), shape(N_SLOTS, 16, 128), shape(3, 16, 128), shape(12 * cx, 8, 128)),
        in_specs=[smem] + [vmem] * 4,
        out_specs=(vmem,) * 4,
    )(meta, e_start, h_start, inv_perm, adj_seed)

    a_got = lax.ppermute(a_msg, "gx", a_pairs)
    b_got = lax.ppermute(b_msg, "gx", b_pairs)
    z_got = lax.ppermute(z_msg, "gz", [(0, 1), (1, 0)])
    y1 = swap_y(y_msg)
    za_got = lax.ppermute(z_got, "gx", a_pairs)
    zb_got = lax.ppermute(z_got, "gx", b_pairs)
    y2 = swap_y(jnp.concatenate([y_rows(v) for v in (a_got, b_got, z_got, za_got, zb_got)], axis=0))

    planes = cx + 2 * DEEP + 1
    main = pltpu.VMEM((3, planes, 24, 128), F32)
    strip = pltpu.VMEM((3, 24, 256), F32)
    e_field, sums = pl.pallas_call(
        run_kernel,
        out_shape=(shape(*e_start.shape), shape(8, 128)),
        in_specs=[smem] + [vmem] * 12,
        out_specs=(vmem, vmem),
        scratch_shapes=[main] * 5
        + [pltpu.VMEM((STEPS, 3, planes, 24, 128), F32), main]
        + [strip] * 5
        + [pltpu.VMEM((STEPS, 3, 24, 256), F32), strip],
        compiler_params=pltpu.CompilerParams(vmem_limit_bytes=40 * 1024 * 1024),
    )(meta, e_start, h_start, inv_perm, adj_seed, region_ids, a_got, b_got, z_got, za_got, zb_got, y1, y2)

    total = sums + lax.ppermute(sums, "gx", a_pairs)
    owned = jnp.where(even == 1, total[0:3, 0:REG_DEV], total[0:3, REG_DEV : 2 * REG_DEV])
    return e_field, owned


def solution(mesh):
    placed = (
        P(None, "gx", "gy", "gz"),
        P(None, "gx", "gy", "gz"),
        P(None, "gx", "gy", "gz"),
        P(None, "gx", "gy", "gz"),
        P("gx", "gy", "gz"),
    )
    return jax.shard_map(
        local,
        mesh=mesh,
        in_specs=placed,
        out_specs=(P(None, "gx", "gy", "gz"), P(None, ("gx", "gy", "gz"))),
        check_vma=False,
    )
```

time: 283 us -> 39.6 us (0.14)
  starting transfers between devices: 160 us -> 12.5 us
  waiting for transfers between devices: 107 us -> 11.5 us
  Pallas kernels: 0 us -> 12.9 us
  other arithmetic: 8.33 us -> 1.04 us
    ppermute x72 -> x8, starting transfers between devices: 160 us -> 12.5 us  [the longest x1 4.26 us: local(): za_got = lax.ppermute(z_got, 'gx', a_pairs)]
    ppermute x72 -> x8, waiting for transfers between devices: 107 us -> 11.5 us  [the longest x1 5.74 us: local(): a_got = lax.ppermute(a_msg, 'gx', a_pairs)]
    pallas_call x0 -> x2, Pallas kernels: none -> 12.9 us  [the longest x1 10.5 us: local(): pl.pallas_call(run_kernel, out_shape=(shape(*e_start.shape), shape(8, 128...]
    sub x31 -> x0, other arithmetic: 3.07 us -> none  [the longest x7 1.44 us: curl_of(): differences = [other - field_in for other in nearby]]
  transfers between devices with their start and end apart: 72 -> 8, of which waited for: 25 -> 4; matrix products, arithmetic and copies ran while one was open for 2% -> 1% of each run, Pallas kernels for 0% -> 0%
where the time goes in v1:
time: 39.6 us; the launch traced here: 39.4 us
  Pallas kernels  12.9 us (33%)
  starting transfers between devices  12.5 us (32%)
  waiting for transfers between devices  11.5 us (29%)
  other arithmetic  1.04 us (3%)
  between operations  0.77 us (2%)
  local copies, waits for them, and re-layouts  0.7 us (2%)
    pallas_call x1, Pallas kernels, local(): pl.pallas_call(run_kernel, out_shape=(shape(*e_start.shape), shape(8, 128...  10.5 us
    ppermute x1, waiting for transfers between devices, local(): a_got = lax.ppermute(a_msg, 'gx', a_pairs)  5.74 us
    ppermute x1, starting transfers between devices, local(): za_got = lax.ppermute(z_got, 'gx', a_pairs)  4.26 us
    ppermute x1, starting transfers between devices, local(): a_got = lax.ppermute(a_msg, 'gx', a_pairs)  2.94 us
    ppermute x1, waiting for transfers between devices, local(): z_got = lax.ppermute(z_msg, 'gz', [(0, 1), (1, 0)])  2.51 us
    pallas_call x1, Pallas kernels, local(): pl.pallas_call(pack_kernel, out_shape=(shape(N_SLOTS, 16, 128), shape(N_S...  2.42 us
    ppermute x1, starting transfers between devices, local(): total = sums + lax.ppermute(sums, 'gx', a_pairs)  2.38 us
    ppermute x2, waiting for transfers between devices, swap_y(): return lax.ppermute(v, 'gy', [(0, 1), (1, 0)])  1.67 us
  transfers between devices with their start and end apart: 8, of which 4 were waited for; matrix products, arithmetic and copies ran while one was open for 1% of the time, Pallas kernels for 0%

profile of v1, /device:TPU:0, one launch (start us, length us, event | category | flops | bytes accessed | tf_op | source)
XLA Modules:
  0.0 39.4 jit_solution(10608461833038567519)
XLA Ops:
  0.7 0.7 %stack.32.meta = s32[8]{0:T(128)} concatenate(s32[1]{0:T(128)} %bitcast, s32[1]{0:T(128)} %bitcast.1, s32[1]{0:T(128)} %bitcast.2, s32[1]{0:T(128)} %bitcast.3, s32[1]{0:T(128)} %bitcast.4, s32[1]{0:T(128)} %bitcast.4, s32[1]{0:T(128)} %bitcast.5, s32[1]{0:T(128)} %bitcast.6), dimensions={0} | concatenate | bytes 64 | tf_op jit(solution)/shard_map/stack | solution.py:369
  1.3 2.4 %shard_map.68 = (f32[41,16,128]{2,1,0:T(8,128)}, f32[41,16,128]{2,1,0:T(8,128)}, f32[3,16,128]{2,1,0:T(8,128)}, f32[96,8,128]{2,1,0:T(8,128)}) custom-call(s32[8]{0:T(128)} %stack.32.meta, f32[3,8,16,128]{3,2,1,0:T(8,128)} %e_in.1, f32[3,8,16,128]{3,2,1,0:T(8,128)} %h_in.1, f32[3,8,16,128]{3,2,1,0:T(8,128)} %ip_in.1, f32[3,8,16,128]{3,2,1,0:T(8,128)} %sd_in.1), custom_call_target="tpu_custom_call" | custom-call | tf_op jit(solution)/shard_map/pallas_call | solution.py:387
  3.7 2.9 %collective-permute-start = (f32[41,16,128]{2,1,0:T(8,128)}, f32[41,16,128]{2,1,0:T(8,128)S(1)}, u32[]{:S(2)}, u32[]{:S(2)}) collective-permute-start(f32[41,16,128]{2,1,0:T(8,128)} %get-tuple-element.8), channel_id=1, source_target_pairs={{0,4},{4,0},{8,12},{12,8},{16,20},{20,16},{24,28},{28,24},{1,5},{5... | collective-permute-start | bytes 1007624 | tf_op jit(solution)/shard_map/ppermute | solution.py:394
  6.7 0.7 %collective-permute-start.1 = (f32[41,16,128]{2,1,0:T(8,128)}, f32[41,16,128]{2,1,0:T(8,128)S(1)}, u32[]{:S(2)}, u32[]{:S(2)}) collective-permute-start(f32[41,16,128]{2,1,0:T(8,128)} %get-tuple-element.9), channel_id=1, source_target_pairs={{4,8},{8,4},{12,16},{16,12},{20,24},{24,20},{5,9},{9,5},{13,17},{1... | collective-permute-start | bytes 1007624 | tf_op jit(solution)/shard_map/ppermute | solution.py:395
  7.4 1.6 %collective-permute-start.2 = (f32[3,16,128]{2,1,0:T(8,128)}, f32[3,16,128]{2,1,0:T(8,128)S(1)}, u32[]{:S(2)}, u32[]{:S(2)}) collective-permute-start(f32[3,16,128]{2,1,0:T(8,128)} %get-tuple-element.10), channel_id=1, source_target_pairs={{0,1},{1,0},{2,3},{3,2},{4,5},{5,4},{6,7},{7,6},{8,9},{9,8},{10,11... | collective-permute-start | bytes 73736 | tf_op jit(solution)/shard_map/ppermute | solution.py:396
  9.0 0.0 collective-permute-start.5
  9.0 2.5 %collective-permute-done.2.z_in = f32[3,16,128]{2,1,0:T(8,128)S(1)} collective-permute-done((f32[3,16,128]{2,1,0:T(8,128)}, f32[3,16,128]{2,1,0:T(8,128)S(1)}, u32[]{:S(2)}, u32[]{:S(2)}) %collective-permute-start.2) | collective-permute-done | bytes 24608 | tf_op jit(solution)/shard_map/ppermute | solution.py:396
  11.5 4.3 %collective-permute-start.3 = (f32[3,16,128]{2,1,0:T(8,128)S(1)}, f32[3,16,128]{2,1,0:T(8,128)S(1)}, u32[]{:S(2)}, u32[]{:S(2)}) collective-permute-start(f32[3,16,128]{2,1,0:T(8,128)S(1)} %collective-permute-done.2.z_in), channel_id=1, source_target_pairs={{0,4},{4,0},{8,12},{12,8},{16,20},{20,16},{24,28},{28,24},{1,5},{5... | collective-permute-start | bytes 73736 | tf_op jit(solution)/shard_map/ppermute | solution.py:398
  15.7 0.7 %collective-permute-start.4 = (f32[3,16,128]{2,1,0:T(8,128)S(1)}, f32[3,16,128]{2,1,0:T(8,128)S(1)}, u32[]{:S(2)}, u32[]{:S(2)}) collective-permute-start(f32[3,16,128]{2,1,0:T(8,128)S(1)} %collective-permute-done.2.z_in), channel_id=1, source_target_pairs={{4,8},{8,4},{12,16},{16,12},{20,24},{24,20},{5,9},{9,5},{13,17},{1... | collective-permute-start | bytes 73736 | tf_op jit(solution)/shard_map/ppermute | solution.py:399
  16.4 5.7 %collective-permute-done.a_in = f32[41,16,128]{2,1,0:T(8,128)S(1)} collective-permute-done((f32[41,16,128]{2,1,0:T(8,128)}, f32[41,16,128]{2,1,0:T(8,128)S(1)}, u32[]{:S(2)}, u32[]{:S(2)}) %collective-permute-start) | collective-permute-done | bytes 335904 | tf_op jit(solution)/shard_map/ppermute | solution.py:394
  22.1 0.1 fusion.1
  22.2 0.0 copy-start
  22.2 0.0 copy-start.1
  22.2 0.0 copy-start.2
  22.3 0.1 fusion
  22.4 0.1 fusion.4
  22.4 0.1 fusion.3
  22.5 0.1 fusion.2
  22.6 0.0 collective-permute-start.6
  22.6 1.7 %collective-permute-done.6.y2 = f32[91,8,128]{2,1,0:T(8,128)S(1)} collective-permute-done((f32[91,8,128]{2,1,0:T(8,128)S(1)}, f32[91,8,128]{2,1,0:T(8,128)S(1)}, u32[]{:S(2)}, u32[]{:S(2)}) %collective-permute-start.6) | collective-permute-done | bytes 372768 | tf_op jit(solution)/shard_map/ppermute | solution.py:381
  24.3 10.5 %shard_map.69 = (f32[3,8,16,128]{3,2,1,0:T(8,128)}, f32[8,128]{1,0:T(8,128)S(1)}) custom-call(s32[8]{0:T(128)S(1)} %copy-done.5, f32[3,8,16,128]{3,2,1,0:T(8,128)S(1)} %copy-done, f32[3,8,16,128]{3,2,1,0:T(8,128)S(1)} %copy-done.1, f32[3,8,16,128]{3,2,1,0:T(8,128)S(1)} %copy-done.2, f32[3,8,16,128]{3,2,1,0:T(8,128)S(1)} %copy-done.3, ...), custom_call_target="tpu_custom_call" | custom-call | tf_op jit(solution)/shard_map/pallas_call | solution.py:405
  34.8 2.4 %collective-permute-start.7 = (f32[8,128]{1,0:T(8,128)S(1)}, f32[8,128]{1,0:T(8,128)S(1)}, u32[]{:S(2)}, u32[]{:S(2)}) collective-permute-start(f32[8,128]{1,0:T(8,128)S(1)} %get-tuple-element.13), channel_id=1, source_target_pairs={{0,4},{4,0},{8,12},{12,8},{16,20},{20,16},{24,28},{28,24},{1,5},{5... | collective-permute-start | bytes 12296 | tf_op jit(solution)/shard_map/ppermute | solution.py:417
  37.2 1.6 %collective-permute-done.7 = f32[8,128]{1,0:T(8,128)S(1)} collective-permute-done((f32[8,128]{1,0:T(8,128)S(1)}, f32[8,128]{1,0:T(8,128)S(1)}, u32[]{:S(2)}, u32[]{:S(2)}) %collective-permute-start.7) | collective-permute-done | bytes 4128 | tf_op jit(solution)/shard_map/ppermute | solution.py:417
  38.8 0.7 %slice_select_fusion.5 = f32[3,8]{1,0:T(4,128)} fusion(f32[8,128]{1,0:T(8,128)S(1)} %add.24, pred[]{:T(512)S(6)} %eq.5), kind=kLoop, calls=%fused_computation.10 | loop fusion | flops 24 | bytes 289 | tf_op jit(solution)/shard_map/jit(_where)/select_n | solution.py:418
  (15 shorter events, 0.0 us)
Async XLA Ops:
  3.7 18.4 %collective-permute-start = (f32[41,16,128]{2,1,0:T(8,128)}, f32[41,16,128]{2,1,0:T(8,128)S(1)}, u32[]{:S(2)}, u32[]{:S(2)}) collective-permute-start(f32[41,16,128]{2,1,0:T(8,128)} %get-tuple-element.8), channel_id=1, source_target_pairs={{0,4},{4,0},{8,12},{12,8},{16,20},{20,16},{24,28},{28,24},{1,5},{5... | collective-permute-start | bytes 1007624 | tf_op jit(solution)/shard_map/ppermute | solution.py:394
  6.7 15.6 %collective-permute-start.1 = (f32[41,16,128]{2,1,0:T(8,128)}, f32[41,16,128]{2,1,0:T(8,128)S(1)}, u32[]{:S(2)}, u32[]{:S(2)}) collective-permute-start(f32[41,16,128]{2,1,0:T(8,128)} %get-tuple-element.9), channel_id=1, source_target_pairs={{4,8},{8,4},{12,16},{16,12},{20,24},{24,20},{5,9},{9,5},{13,17},{1... | collective-permute-start | bytes 1007624 | tf_op jit(solution)/shard_map/ppermute | solution.py:395
  7.4 4.1 %collective-permute-start.2 = (f32[3,16,128]{2,1,0:T(8,128)}, f32[3,16,128]{2,1,0:T(8,128)S(1)}, u32[]{:S(2)}, u32[]{:S(2)}) collective-permute-start(f32[3,16,128]{2,1,0:T(8,128)} %get-tuple-element.10), channel_id=1, source_target_pairs={{0,1},{1,0},{2,3},{3,2},{4,5},{5,4},{6,7},{7,6},{8,9},{9,8},{10,11... | collective-permute-start | bytes 73736 | tf_op jit(solution)/shard_map/ppermute | solution.py:396
  9.0 13.7 %collective-permute-start.5 = (f32[96,8,128]{2,1,0:T(8,128)}, f32[96,8,128]{2,1,0:T(8,128)S(1)}, u32[]{:S(2)}, u32[]{:S(2)}) collective-permute-start(f32[96,8,128]{2,1,0:T(8,128)} %get-tuple-element.11), channel_id=1, source_target_pairs={{0,2},{2,0},{1,3},{3,1},{4,6},{6,4},{5,7},{7,5},{8,10},{10,8},{9,1... | collective-permute-start | bytes 1179656 | tf_op jit(solution)/shard_map/ppermute | solution.py:381
  11.5 11.0 %collective-permute-start.3 = (f32[3,16,128]{2,1,0:T(8,128)S(1)}, f32[3,16,128]{2,1,0:T(8,128)S(1)}, u32[]{:S(2)}, u32[]{:S(2)}) collective-permute-start(f32[3,16,128]{2,1,0:T(8,128)S(1)} %collective-permute-done.2.z_in), channel_id=1, source_target_pairs={{0,4},{4,0},{8,12},{12,8},{16,20},{20,16},{24,28},{28,24},{1,5},{5... | collective-permute-start | bytes 73736 | tf_op jit(solution)/shard_map/ppermute | solution.py:398
  15.7 6.8 %collective-permute-start.4 = (f32[3,16,128]{2,1,0:T(8,128)S(1)}, f32[3,16,128]{2,1,0:T(8,128)S(1)}, u32[]{:S(2)}, u32[]{:S(2)}) collective-permute-start(f32[3,16,128]{2,1,0:T(8,128)S(1)} %collective-permute-done.2.z_in), channel_id=1, source_target_pairs={{4,8},{8,4},{12,16},{16,12},{20,24},{24,20},{5,9},{9,5},{13,17},{1... | collective-permute-start | bytes 73736 | tf_op jit(solution)/shard_map/ppermute | solution.py:399
  22.1 2.1 %copy-start.3 = (f32[3,8,16,128]{3,2,1,0:T(8,128)S(1)}, f32[3,8,16,128]{3,2,1,0:T(8,128)}, u32[]{:S(2)}) copy-start(f32[3,8,16,128]{3,2,1,0:T(8,128)} %sd_in.1) | copy-start | bytes 589828
  22.1 2.2 %copy-start.4 = (s32[8,16,128]{2,1,0:T(8,128)S(1)}, s32[8,16,128]{2,1,0:T(8,128)}, u32[]{:S(2)}) copy-start(s32[8,16,128]{2,1,0:T(8,128)} %ids.1) | copy-start | bytes 196612
  22.2 2.1 %copy-start = (f32[3,8,16,128]{3,2,1,0:T(8,128)S(1)}, f32[3,8,16,128]{3,2,1,0:T(8,128)}, u32[]{:S(2)}) copy-start(f32[3,8,16,128]{3,2,1,0:T(8,128)} %e_in.1) | copy-start | bytes 589828
  22.2 2.1 %copy-start.1 = (f32[3,8,16,128]{3,2,1,0:T(8,128)S(1)}, f32[3,8,16,128]{3,2,1,0:T(8,128)}, u32[]{:S(2)}) copy-start(f32[3,8,16,128]{3,2,1,0:T(8,128)} %h_in.1) | copy-start | bytes 589828
  22.2 2.1 %copy-start.2 = (f32[3,8,16,128]{3,2,1,0:T(8,128)S(1)}, f32[3,8,16,128]{3,2,1,0:T(8,128)}, u32[]{:S(2)}) copy-start(f32[3,8,16,128]{3,2,1,0:T(8,128)} %ip_in.1) | copy-start | bytes 589828
  22.5 1.8 %copy-start.5 = (s32[8]{0:T(128)S(1)}, s32[8]{0:T(128)}, u32[]{:S(2)}) copy-start(s32[8]{0:T(128)} %stack.32.meta) | copy-start | bytes 100
  22.6 1.7 %collective-permute-start.6 = (f32[91,8,128]{2,1,0:T(8,128)S(1)}, f32[91,8,128]{2,1,0:T(8,128)S(1)}, u32[]{:S(2)}, u32[]{:S(2)}) collective-permute-start(f32[91,8,128]{2,1,0:T(8,128)S(1)} %fusion.2), channel_id=1, source_target_pairs={{0,2},{2,0},{1,3},{3,1},{4,6},{6,4},{5,7},{7,5},{8,10},{10,8},{9,1... | collective-permute-start | bytes 1118216 | tf_op jit(solution)/shard_map/ppermute | solution.py:381
  34.8 4.0 %collective-permute-start.7 = (f32[8,128]{1,0:T(8,128)S(1)}, f32[8,128]{1,0:T(8,128)S(1)}, u32[]{:S(2)}, u32[]{:S(2)}) collective-permute-start(f32[8,128]{1,0:T(8,128)S(1)} %get-tuple-element.13), channel_id=1, source_target_pairs={{0,4},{4,0},{8,12},{12,8},{16,20},{20,16},{24,28},{28,24},{1,5},{5... | collective-permute-start | bytes 12296 | tf_op jit(solution)/shard_map/ppermute | solution.py:417

commit v2 on v1

--- a/solution.py
+++ b/solution.py
@@ -1,5 +1,3 @@
-import functools
-
 import jax
 import jax.numpy as jnp
 from jax import lax
@@ -11,7 +9,7 @@
 REG_DEV = 8
 DEEP = 4
 EDGE = 4
-UNROLL = 2
+UNROLL = 8
 
 COUNTS = ((4, 4, 4), (3, 4, 4), (3, 3, 3), (3, 3, 3))
 SLOTS = []
@@ -32,8 +30,8 @@
     return lax.broadcasted_iota(jnp.int32, shape, len(shape) - 2)
 
 
-def pack_kernel(meta, e, h, ip, sd, a_out, b_out, z_out, y_out):
-    even, gz = meta[0], meta[1]
+def pack_kernel(e, h, ip, sd, a_out, b_out, z_out, y_out):
+    even, gz = (lax.axis_index("gx") + 1) % 2, lax.axis_index("gz")
     refs = (e, h, ip, sd)
     cx = e.shape[1]
     for f, c, k, off in SLOTS:
@@ -87,11 +85,17 @@
     )
 
 
-def run_kernel(meta, e_in, h_in, ip_in, sd_in, ids, a_in, b_in, z_in, za_in, zb_in, y1, y2,
+def run_kernel(e_in, h_in, ip_in, sd_in, ids, a_in, b_in, z_in, za_in, zb_in, y1, y2,
                e_out, s_out, E, H, I, W, M, PS, G, SE, SH, SI, SW, SM, SP, SG):
-    even, gz = meta[0], meta[1]
-    low_x, keep_hi, keep_lo, low_y = meta[2], meta[3], meta[4], meta[5]
-    first_owner, second_owner = meta[6], meta[7]
+    xi, yi, gz = (lax.axis_index(a) for a in ("gx", "gy", "gz"))
+    even = (xi + 1) % 2
+    low_x = jnp.where(xi > 0, 1, 0)
+    keep_hi = jnp.where(yi < lax.axis_size("gy") - 1, 1, 0)
+    keep_lo = low_y = jnp.where(yi > 0, 1, 0)
+    plane_count = lax.axis_size("gy") * lax.axis_size("gz")
+    own_flat = xi * plane_count + yi * lax.axis_size("gz") + gz
+    first_owner = own_flat - (1 - even) * plane_count
+    second_owner = first_owner + plane_count
     cx = e_in.shape[1]
     shape = (24, 128)
     lane = lanes_of(shape)
@@ -357,19 +361,10 @@
 
 
 def local(e_start, h_start, inv_perm, adj_seed, region_ids):
-    n_gx, n_gy, n_gz = (lax.axis_size(a) for a in ("gx", "gy", "gz"))
-    xi, yi, zi = (lax.axis_index(a) for a in ("gx", "gy", "gz"))
+    n_gx, n_gy = lax.axis_size("gx"), lax.axis_size("gy")
+    xi = lax.axis_index("gx")
     cx = e_start.shape[1]
     even = (xi + 1) % 2
-    plane_count = n_gy * n_gz
-    own_flat = xi * plane_count + yi * n_gz + zi
-    first_owner = own_flat - (1 - even) * plane_count
-    keep_hi = jnp.where(yi < n_gy - 1, 1, 0)
-    keep_lo = jnp.where(yi > 0, 1, 0)
-    meta = jnp.stack(
-        [even, zi, jnp.where(xi > 0, 1, 0), keep_hi, keep_lo, keep_lo, first_owner, first_owner + plane_count]
-    ).astype(jnp.int32)
-    smem = pl.BlockSpec(memory_space=pltpu.SMEM)
     vmem = pl.BlockSpec(memory_space=pltpu.VMEM)
     shape = lambda *dims: jax.ShapeDtypeStruct(dims, F32)
 
@@ -387,9 +382,10 @@
     a_msg, b_msg, z_msg, y_msg = pl.pallas_call(
         pack_kernel,
         out_shape=(shape(N_SLOTS, 16, 128), shape(N_SLOTS, 16, 128), shape(3, 16, 128), shape(12 * cx, 8, 128)),
-        in_specs=[smem] + [vmem] * 4,
+        in_specs=[vmem] * 4,
         out_specs=(vmem,) * 4,
-    )(meta, e_start, h_start, inv_perm, adj_seed)
+        compiler_params=pltpu.CompilerParams(vmem_limit_bytes=8 * 1024 * 1024),
+    )(e_start, h_start, inv_perm, adj_seed)
 
     a_got = lax.ppermute(a_msg, "gx", a_pairs)
     b_got = lax.ppermute(b_msg, "gx", b_pairs)
@@ -405,14 +401,14 @@
     e_field, sums = pl.pallas_call(
         run_kernel,
         out_shape=(shape(*e_start.shape), shape(8, 128)),
-        in_specs=[smem] + [vmem] * 12,
+        in_specs=[vmem] * 12,
         out_specs=(vmem, vmem),
         scratch_shapes=[main] * 5
         + [pltpu.VMEM((STEPS, 3, planes, 24, 128), F32), main]
         + [strip] * 5
         + [pltpu.VMEM((STEPS, 3, 24, 256), F32), strip],
-        compiler_params=pltpu.CompilerParams(vmem_limit_bytes=40 * 1024 * 1024),
-    )(meta, e_start, h_start, inv_perm, adj_seed, region_ids, a_got, b_got, z_got, za_got, zb_got, y1, y2)
+        compiler_params=pltpu.CompilerParams(vmem_limit_bytes=20 * 1024 * 1024),
+    )(e_start, h_start, inv_perm, adj_seed, region_ids, a_got, b_got, z_got, za_got, zb_got, y1, y2)
 
     total = sums + lax.ppermute(sums, "gx", a_pairs)
     owned = jnp.where(even == 1, total[0:3, 0:REG_DEV], total[0:3, REG_DEV : 2 * REG_DEV])

time: 39.6 us -> 34 us (0.86)
  Pallas kernels: 12.9 us -> 4.38 us
  local copies, waits for them, and re-layouts: 0.7 us -> 3.73 us
    pallas_call x1, Pallas kernels: 10.5 us -> 4.07 us  [local(): pl.pallas_call(run_kernel, out_shape=(shape(*e_start.shape), shape(8, 128...]
    unnamed x12 -> x18, local copies, waits for them, and re-layouts: 0.03 us -> 3.73 us
    pallas_call x1, Pallas kernels: 2.42 us -> 0.31 us  [local(): pl.pallas_call(pack_kernel, out_shape=(shape(N_SLOTS, 16, 128), shape(N_S...]
    another operation x1 -> x0, local copies, waits for them, and re-layouts: 0.67 us -> none  [local(): jnp.stack([even, zi, jnp.where(xi > 0, 1, 0), keep_hi, keep_lo, keep_lo,...]
where the time goes in v2:
time: 34 us; the launch traced here: 33.8 us
  starting transfers between devices  12.7 us (37%)
  waiting for transfers between devices  11.2 us (33%)
  Pallas kernels  4.38 us (13%)
  local copies, waits for them, and re-layouts  3.73 us (11%)
  other arithmetic  1.04 us (3%)
  between operations  0.75 us (2%)
    ppermute x1, waiting for transfers between devices, local(): a_got = lax.ppermute(a_msg, 'gx', a_pairs)  5.64 us
    ppermute x1, starting transfers between devices, local(): za_got = lax.ppermute(z_got, 'gx', a_pairs)  4.27 us
    pallas_call x1, Pallas kernels, local(): pl.pallas_call(run_kernel, out_shape=(shape(*e_start.shape), shape(8, 128...  4.07 us
    unnamed x18, local copies, waits for them, and re-layouts  3.73 us
    ppermute x1, starting transfers between devices, local(): a_got = lax.ppermute(a_msg, 'gx', a_pairs)  3 us
    ppermute x1, starting transfers between devices, local(): total = sums + lax.ppermute(sums, 'gx', a_pairs)  2.48 us
    ppermute x1, waiting for transfers between devices, local(): z_got = lax.ppermute(z_msg, 'gz', [(0, 1), (1, 0)])  2.3 us
    ppermute x2, waiting for transfers between devices, swap_y(): return lax.ppermute(v, 'gy', [(0, 1), (1, 0)])  1.67 us
  transfers between devices with their start and end apart: 8, of which 4 were waited for; matrix products, arithmetic and copies ran while one was open for 1% of the time, Pallas kernels for 0%

profile of v2, /device:TPU:0, one launch (start us, length us, event | category | flops | bytes accessed | tf_op | source)
XLA Modules:
  0.0 33.8 jit_solution(3645748946350523714)
XLA Ops:
  0.6 0.0 copy-start
  0.6 0.9 %copy-done = f32[3,8,16,128]{3,2,1,0:T(8,128)S(1)} copy-done((f32[3,8,16,128]{3,2,1,0:T(8,128)S(1)}, f32[3,8,16,128]{3,2,1,0:T(8,128)}, u32[]{:S(2)}) %copy-start) | copy-done | bytes 196632
  1.6 0.9 %copy-done.2 = f32[3,8,16,128]{3,2,1,0:T(8,128)S(1)} copy-done((f32[3,8,16,128]{3,2,1,0:T(8,128)S(1)}, f32[3,8,16,128]{3,2,1,0:T(8,128)}, u32[]{:S(2)}) %copy-start.2) | copy-done | bytes 196632
  2.5 0.9 %copy-done.4 = f32[3,8,16,128]{3,2,1,0:T(8,128)S(1)} copy-done((f32[3,8,16,128]{3,2,1,0:T(8,128)S(1)}, f32[3,8,16,128]{3,2,1,0:T(8,128)}, u32[]{:S(2)}) %copy-start.4) | copy-done | bytes 196632
  3.4 0.9 %copy-done.6 = f32[3,8,16,128]{3,2,1,0:T(8,128)S(1)} copy-done((f32[3,8,16,128]{3,2,1,0:T(8,128)S(1)}, f32[3,8,16,128]{3,2,1,0:T(8,128)}, u32[]{:S(2)}) %copy-start.6) | copy-done | bytes 196632
  4.3 0.3 shard_map.68
  4.7 3.0 %collective-permute-start = (f32[41,16,128]{2,1,0:T(8,128)S(1)}, f32[41,16,128]{2,1,0:T(8,128)S(1)}, u32[]{:S(2)}, u32[]{:S(2)}) collective-permute-start(f32[41,16,128]{2,1,0:T(8,128)S(1)} %get-tuple-element.8), channel_id=1, source_target_pairs={{0,4},{4,0},{8,12},{12,8},{16,20},{20,16},{24,28},{28,24},{1,5},{5... | collective-permute-start | bytes 1007624 | tf_op jit(solution)/shard_map/ppermute | solution.py:390
  7.7 0.7 %collective-permute-start.1 = (f32[41,16,128]{2,1,0:T(8,128)S(1)}, f32[41,16,128]{2,1,0:T(8,128)S(1)}, u32[]{:S(2)}, u32[]{:S(2)}) collective-permute-start(f32[41,16,128]{2,1,0:T(8,128)S(1)} %get-tuple-element.9), channel_id=1, source_target_pairs={{4,8},{8,4},{12,16},{16,12},{20,24},{24,20},{5,9},{9,5},{13,17},{1... | collective-permute-start | bytes 1007624 | tf_op jit(solution)/shard_map/ppermute | solution.py:391
  8.3 1.6 %collective-permute-start.2 = (f32[3,16,128]{2,1,0:T(8,128)S(1)}, f32[3,16,128]{2,1,0:T(8,128)S(1)}, u32[]{:S(2)}, u32[]{:S(2)}) collective-permute-start(f32[3,16,128]{2,1,0:T(8,128)S(1)} %get-tuple-element.10), channel_id=1, source_target_pairs={{0,1},{1,0},{2,3},{3,2},{4,5},{5,4},{6,7},{7,6},{8,9},{9,8},{10,11... | collective-permute-start | bytes 73736 | tf_op jit(solution)/shard_map/ppermute | solution.py:392
  9.9 2.3 %collective-permute-done.2.z_in = f32[3,16,128]{2,1,0:T(8,128)S(1)} collective-permute-done((f32[3,16,128]{2,1,0:T(8,128)S(1)}, f32[3,16,128]{2,1,0:T(8,128)S(1)}, u32[]{:S(2)}, u32[]{:S(2)}) %collective-permute-start.2) | collective-permute-done | bytes 24608 | tf_op jit(solution)/shard_map/ppermute | solution.py:392
  12.2 4.3 %collective-permute-start.3 = (f32[3,16,128]{2,1,0:T(8,128)S(1)}, f32[3,16,128]{2,1,0:T(8,128)S(1)}, u32[]{:S(2)}, u32[]{:S(2)}) collective-permute-start(f32[3,16,128]{2,1,0:T(8,128)S(1)} %collective-permute-done.2.z_in), channel_id=1, source_target_pairs={{0,4},{4,0},{8,12},{12,8},{16,20},{20,16},{24,28},{28,24},{1,5},{5... | collective-permute-start | bytes 73736 | tf_op jit(solution)/shard_map/ppermute | solution.py:394
  16.5 0.7 %collective-permute-start.4 = (f32[3,16,128]{2,1,0:T(8,128)S(1)}, f32[3,16,128]{2,1,0:T(8,128)S(1)}, u32[]{:S(2)}, u32[]{:S(2)}) collective-permute-start(f32[3,16,128]{2,1,0:T(8,128)S(1)} %collective-permute-done.2.z_in), channel_id=1, source_target_pairs={{4,8},{8,4},{12,16},{16,12},{20,24},{24,20},{5,9},{9,5},{13,17},{1... | collective-permute-start | bytes 73736 | tf_op jit(solution)/shard_map/ppermute | solution.py:395
  17.2 5.6 %collective-permute-done.a_in = f32[41,16,128]{2,1,0:T(8,128)S(1)} collective-permute-done((f32[41,16,128]{2,1,0:T(8,128)S(1)}, f32[41,16,128]{2,1,0:T(8,128)S(1)}, u32[]{:S(2)}, u32[]{:S(2)}) %collective-permute-start) | collective-permute-done | bytes 335904 | tf_op jit(solution)/shard_map/ppermute | solution.py:390
  22.8 0.1 fusion.1
  22.9 0.1 fusion
  23.0 0.1 fusion.4
  23.1 0.1 fusion.3
  23.2 0.1 fusion.2
  23.2 0.0 collective-permute-start.6
  23.3 1.7 %collective-permute-done.6.y2 = f32[91,8,128]{2,1,0:T(8,128)S(1)} collective-permute-done((f32[91,8,128]{2,1,0:T(8,128)S(1)}, f32[91,8,128]{2,1,0:T(8,128)S(1)}, u32[]{:S(2)}, u32[]{:S(2)}) %collective-permute-start.6) | collective-permute-done | bytes 372768 | tf_op jit(solution)/shard_map/ppermute | solution.py:376
  25.0 4.1 %shard_map.69 = (f32[3,8,16,128]{3,2,1,0:T(8,128)}, f32[8,128]{1,0:T(8,128)S(1)}) custom-call(f32[3,8,16,128]{3,2,1,0:T(8,128)S(1)} %copy-done.1, f32[3,8,16,128]{3,2,1,0:T(8,128)S(1)} %copy-done.3, f32[3,8,16,128]{3,2,1,0:T(8,128)S(1)} %copy-done.5, f32[3,8,16,128]{3,2,1,0:T(8,128)S(1)} %copy-done.7, s32[8,16,128]{2,1,0:T(8,128)S(1)} %copy-done.8, ...), custom_call_target="tpu_custom_call" | custom-call | tf_op jit(solution)/shard_map/pallas_call | solution.py:401
  29.0 2.5 %collective-permute-start.7 = (f32[8,128]{1,0:T(8,128)S(1)}, f32[8,128]{1,0:T(8,128)S(1)}, u32[]{:S(2)}, u32[]{:S(2)}) collective-permute-start(f32[8,128]{1,0:T(8,128)S(1)} %get-tuple-element.13), channel_id=1, source_target_pairs={{0,4},{4,0},{8,12},{12,8},{16,20},{20,16},{24,28},{28,24},{1,5},{5... | collective-permute-start | bytes 12296 | tf_op jit(solution)/shard_map/ppermute | solution.py:413
  31.5 1.6 %collective-permute-done.7 = f32[8,128]{1,0:T(8,128)S(1)} collective-permute-done((f32[8,128]{1,0:T(8,128)S(1)}, f32[8,128]{1,0:T(8,128)S(1)}, u32[]{:S(2)}, u32[]{:S(2)}) %collective-permute-start.7) | collective-permute-done | bytes 4128 | tf_op jit(solution)/shard_map/ppermute | solution.py:413
  33.1 0.7 %slice_select_fusion.5 = f32[3,8]{1,0:T(4,128)} fusion(f32[8,128]{1,0:T(8,128)S(1)} %add.12, pred[]{:T(512)S(6)} %eq.5), kind=kLoop, calls=%fused_computation.10 | loop fusion | flops 24 | bytes 289 | tf_op jit(solution)/shard_map/jit(_where)/select_n | solution.py:414
  (20 shorter events, 0.1 us)
Async XLA Ops:
  0.6 0.9 %copy-start = (f32[3,8,16,128]{3,2,1,0:T(8,128)S(1)}, f32[3,8,16,128]{3,2,1,0:T(8,128)}, u32[]{:S(2)}) copy-start(f32[3,8,16,128]{3,2,1,0:T(8,128)} %e_in.1) | copy-start | bytes 589828
  1.6 0.9 %copy-start.2 = (f32[3,8,16,128]{3,2,1,0:T(8,128)S(1)}, f32[3,8,16,128]{3,2,1,0:T(8,128)}, u32[]{:S(2)}) copy-start(f32[3,8,16,128]{3,2,1,0:T(8,128)} %h_in.1) | copy-start | bytes 589828
  2.5 0.9 %copy-start.4 = (f32[3,8,16,128]{3,2,1,0:T(8,128)S(1)}, f32[3,8,16,128]{3,2,1,0:T(8,128)}, u32[]{:S(2)}) copy-start(f32[3,8,16,128]{3,2,1,0:T(8,128)} %ip_in.1) | copy-start | bytes 589828
  3.4 0.9 %copy-start.6 = (f32[3,8,16,128]{3,2,1,0:T(8,128)S(1)}, f32[3,8,16,128]{3,2,1,0:T(8,128)}, u32[]{:S(2)}) copy-start(f32[3,8,16,128]{3,2,1,0:T(8,128)} %sd_in.1) | copy-start | bytes 589828
  4.7 18.1 %collective-permute-start = (f32[41,16,128]{2,1,0:T(8,128)S(1)}, f32[41,16,128]{2,1,0:T(8,128)S(1)}, u32[]{:S(2)}, u32[]{:S(2)}) collective-permute-start(f32[41,16,128]{2,1,0:T(8,128)S(1)} %get-tuple-element.8), channel_id=1, source_target_pairs={{0,4},{4,0},{8,12},{12,8},{16,20},{20,16},{24,28},{28,24},{1,5},{5... | collective-permute-start | bytes 1007624 | tf_op jit(solution)/shard_map/ppermute | solution.py:390
  7.7 15.3 %collective-permute-start.1 = (f32[41,16,128]{2,1,0:T(8,128)S(1)}, f32[41,16,128]{2,1,0:T(8,128)S(1)}, u32[]{:S(2)}, u32[]{:S(2)}) collective-permute-start(f32[41,16,128]{2,1,0:T(8,128)S(1)} %get-tuple-element.9), channel_id=1, source_target_pairs={{4,8},{8,4},{12,16},{16,12},{20,24},{24,20},{5,9},{9,5},{13,17},{1... | collective-permute-start | bytes 1007624 | tf_op jit(solution)/shard_map/ppermute | solution.py:391
  8.3 3.9 %collective-permute-start.2 = (f32[3,16,128]{2,1,0:T(8,128)S(1)}, f32[3,16,128]{2,1,0:T(8,128)S(1)}, u32[]{:S(2)}, u32[]{:S(2)}) collective-permute-start(f32[3,16,128]{2,1,0:T(8,128)S(1)} %get-tuple-element.10), channel_id=1, source_target_pairs={{0,1},{1,0},{2,3},{3,2},{4,5},{5,4},{6,7},{7,6},{8,9},{9,8},{10,11... | collective-permute-start | bytes 73736 | tf_op jit(solution)/shard_map/ppermute | solution.py:392
  9.9 13.3 %collective-permute-start.5 = (f32[96,8,128]{2,1,0:T(8,128)S(1)}, f32[96,8,128]{2,1,0:T(8,128)S(1)}, u32[]{:S(2)}, u32[]{:S(2)}) collective-permute-start(f32[96,8,128]{2,1,0:T(8,128)S(1)} %get-tuple-element.11), channel_id=1, source_target_pairs={{0,2},{2,0},{1,3},{3,1},{4,6},{6,4},{5,7},{7,5},{8,10},{10,8},{9,1... | collective-permute-start | bytes 1179656 | tf_op jit(solution)/shard_map/ppermute | solution.py:376
  12.2 10.9 %collective-permute-start.3 = (f32[3,16,128]{2,1,0:T(8,128)S(1)}, f32[3,16,128]{2,1,0:T(8,128)S(1)}, u32[]{:S(2)}, u32[]{:S(2)}) collective-permute-start(f32[3,16,128]{2,1,0:T(8,128)S(1)} %collective-permute-done.2.z_in), channel_id=1, source_target_pairs={{0,4},{4,0},{8,12},{12,8},{16,20},{20,16},{24,28},{28,24},{1,5},{5... | collective-permute-start | bytes 73736 | tf_op jit(solution)/shard_map/ppermute | solution.py:394
  16.5 6.7 %collective-permute-start.4 = (f32[3,16,128]{2,1,0:T(8,128)S(1)}, f32[3,16,128]{2,1,0:T(8,128)S(1)}, u32[]{:S(2)}, u32[]{:S(2)}) collective-permute-start(f32[3,16,128]{2,1,0:T(8,128)S(1)} %collective-permute-done.2.z_in), channel_id=1, source_target_pairs={{4,8},{8,4},{12,16},{16,12},{20,24},{24,20},{5,9},{9,5},{13,17},{1... | collective-permute-start | bytes 73736 | tf_op jit(solution)/shard_map/ppermute | solution.py:395
  22.8 2.1 %copy-start.7 = (f32[3,8,16,128]{3,2,1,0:T(8,128)S(1)}, f32[3,8,16,128]{3,2,1,0:T(8,128)}, u32[]{:S(2)}) copy-start(f32[3,8,16,128]{3,2,1,0:T(8,128)} %sd_in.1) | copy-start | bytes 589828
  22.8 2.1 %copy-start.8 = (s32[8,16,128]{2,1,0:T(8,128)S(1)}, s32[8,16,128]{2,1,0:T(8,128)}, u32[]{:S(2)}) copy-start(s32[8,16,128]{2,1,0:T(8,128)} %ids.1) | copy-start | bytes 196612
  22.9 2.1 %copy-start.1 = (f32[3,8,16,128]{3,2,1,0:T(8,128)S(1)}, f32[3,8,16,128]{3,2,1,0:T(8,128)}, u32[]{:S(2)}) copy-start(f32[3,8,16,128]{3,2,1,0:T(8,128)} %e_in.1) | copy-start | bytes 589828
  22.9 2.1 %copy-start.3 = (f32[3,8,16,128]{3,2,1,0:T(8,128)S(1)}, f32[3,8,16,128]{3,2,1,0:T(8,128)}, u32[]{:S(2)}) copy-start(f32[3,8,16,128]{3,2,1,0:T(8,128)} %h_in.1) | copy-start | bytes 589828
  22.9 2.1 %copy-start.5 = (f32[3,8,16,128]{3,2,1,0:T(8,128)S(1)}, f32[3,8,16,128]{3,2,1,0:T(8,128)}, u32[]{:S(2)}) copy-start(f32[3,8,16,128]{3,2,1,0:T(8,128)} %ip_in.1) | copy-start | bytes 589828
  23.2 1.7 %collective-permute-start.6 = (f32[91,8,128]{2,1,0:T(8,128)S(1)}, f32[91,8,128]{2,1,0:T(8,128)S(1)}, u32[]{:S(2)}, u32[]{:S(2)}) collective-permute-start(f32[91,8,128]{2,1,0:T(8,128)S(1)} %fusion.2), channel_id=1, source_target_pairs={{0,2},{2,0},{1,3},{3,1},{4,6},{6,4},{5,7},{7,5},{8,10},{10,8},{9,1... | collective-permute-start | bytes 1118216 | tf_op jit(solution)/shard_map/ppermute | solution.py:376
  29.0 4.1 %collective-permute-start.7 = (f32[8,128]{1,0:T(8,128)S(1)}, f32[8,128]{1,0:T(8,128)S(1)}, u32[]{:S(2)}, u32[]{:S(2)}) collective-permute-start(f32[8,128]{1,0:T(8,128)S(1)} %get-tuple-element.13), channel_id=1, source_target_pairs={{0,4},{4,0},{8,12},{12,8},{16,20},{20,16},{24,28},{28,24},{1,5},{5... | collective-permute-start | bytes 12296 | tf_op jit(solution)/shard_map/ppermute | solution.py:413

commit v3 on v0

v3 whole, which is shorter than its diff:
```python
import jax
import jax.numpy as jnp
from jax import lax
from jax.experimental import pallas as pl
from jax.experimental.pallas import tpu as pltpu
from jax.sharding import PartitionSpec as P

STEPS = 4
REG_DEV = 8
DEEP = 3
EDGE = 4
PERM, SEED, ELEC, MAGN = range(4)
N_SLOTS = 2 * 3 * DEEP
N_TRACES = 2 * STEPS

time_step = 0.5
grad_scale = 1.0 / 64.0
F32 = jnp.float32


def lanes_of(shape):
    return lax.broadcasted_iota(jnp.int32, shape, len(shape) - 1)


def rows_of(shape):
    return lax.broadcasted_iota(jnp.int32, shape, len(shape) - 2)


def roll_up(v, axis):
    return pltpu.roll(v, v.shape[axis] - 1, axis)


def roll_down(v, axis):
    return pltpu.roll(v, 1, axis)


def curl_f(v, nxt, shift_y, shift_z):
    vx, vy, vz = v
    ny, nz = nxt
    return (
        (shift_y(vz) - vz) - (shift_z(vy) - vy),
        (shift_z(vx) - vx) - (nz - vz),
        (ny - vy) - (shift_y(vx) - vx),
    )


def curl_b(v, prv, shift_y, shift_z):
    vx, vy, vz = v
    py, pz = prv
    return (
        (vz - shift_y(vz)) - (vy - shift_z(vy)),
        (vx - shift_z(vx)) - (vz - pz),
        (vy - py) - (vx - shift_y(vx)),
    )


class Place:
    def __init__(self):
        xi, yi, self.gz = (lax.axis_index(a) for a in ("gx", "gy", "gz"))
        n_gy, n_gz = lax.axis_size("gy"), lax.axis_size("gz")
        even = (xi + 1) % 2
        self.even = even == 1
        self.no_low_x = xi == 0
        self.no_low_y = yi == 0
        self.no_high_y = yi == n_gy - 1
        own_flat = xi * n_gy * n_gz + yi * n_gz + self.gz
        self.first_owner = own_flat - (1 - even) * n_gy * n_gz
        self.second_owner = self.first_owner + n_gy * n_gz
        self.lane = lanes_of((24, 128))
        self.row = rows_of((24, 128))
        self.keep_row = jnp.where((self.row >= 20) & self.no_low_y, 0.0, 1.0)
        self.own_off = jnp.where(self.gz == 0, 8, 4)
        self.own_j = jnp.where(self.gz == 0, 0, 4)
        self.got_j = jnp.where(self.gz == 0, 8, 0)

    def y_part(self, v):
        high = jnp.where(self.no_high_y, 0.0, 1.0)
        low = jnp.where(self.no_low_y, 0.0, 1.0)
        return v * jnp.where(rows_of(v.shape[-2:]) < EDGE, high, low)

    def strip_tile(self, planes, got, q):
        lane = self.lane
        acc = jnp.zeros((24, 128), F32)
        for x, plane in enumerate(planes):
            acc = jnp.where(lane // 16 == x, pltpu.roll(plane, (16 * x + self.own_off) % 128, 1), acc)
        j = lane % 16
        is_own = (j >= self.own_j) & (j < self.own_j + 8)
        is_got = (j >= self.got_j) & (j < self.got_j + EDGE)
        got = pltpu.roll(got, (self.got_j - 4 * (q % 4) + 128) % 128, 1)
        return jnp.where(is_own, acc, jnp.where(is_got, got, 0.0))

    def z_up(self, v):
        return jnp.where(self.lane == 127, 0.0, roll_up(v, 1))

    def z_down(self, v):
        return jnp.where(self.lane == 0, 0.0, roll_down(v, 1))


def y_up(v):
    return roll_up(v, 0)


def y_down(v):
    return roll_down(v, 0)


def sz_up(v):
    return roll_up(v, 1)


def sz_down(v):
    return roll_down(v, 1)


def get(ref, x, comps=(0, 1, 2)):
    return tuple(ref[c, x] for c in comps)


def put(ref, xs, values):
    for x, v in zip(xs, values):
        for c in range(3):
            ref[c, x] = v[c]


def sget(ref):
    return tuple(ref[c] for c in range(3))


def sput(ref, v):
    for c in range(3):
        ref[c] = v[c]


def pack_kernel(ip_hbm, sd_hbm, e_hbm, h_hbm, a_out, b_out, z_out, y_out, ip, sd, e, h, sems):
    even, gz = (lax.axis_index("gx") + 1) % 2, lax.axis_index("gz")
    refs = (ip, sd, e, h)
    copies = []
    for i, src in enumerate((ip_hbm, sd_hbm, e_hbm, h_hbm)):
        copies.append(pltpu.make_async_copy(src, refs[i], sems.at[i]))
    for copy in copies:
        copy.start()
    for copy in copies:
        copy.wait()
    cx = e.shape[1]
    a_base = jnp.where(even == 1, cx - DEEP, 0)
    b_base = jnp.where(even == 1, 0, cx - DEEP)
    for f in (PERM, SEED):
        for c in range(3):
            off = DEEP * (3 * f + c)
            a_out[off : off + DEEP] = refs[f][c, pl.ds(a_base, DEEP)]
            b_out[off : off + DEEP] = refs[f][c, pl.ds(b_base, DEEP)]
    group = lanes_of((16, 128)) // EDGE
    z_off = jnp.where(gz == 0, EDGE, 0)
    for t in range(3):
        total = jnp.zeros((16, 128), F32)
        for k in range(4):
            f, c = divmod(4 * t + k, 3)
            for x in range(cx):
                moved = pltpu.roll(refs[f][c, x], (16 * x + 4 * k + z_off) % 128, 1)
                total = jnp.where(group == 4 * x + k, moved, total)
        z_out[t] = total
    first = rows_of((cx, 8, 128)) < EDGE
    for f in range(4):
        for c in range(3):
            q = 3 * f + c
            y_out[q * cx : (q + 1) * cx] = jnp.where(first, refs[f][c, :, 0:8], refs[f][c, :, 8:16])


def own_kernel(ip_in, e_in, h_in, y1, z_in, yz,
               a_out, b_out, c_out, e_out, sc_out, se_out, I, E, H):
    at = Place()
    cx = e_in.shape[1]
    lane = at.lane
    zero = jnp.zeros((24, 128), F32)
    strips = []
    for f, X, src in ((PERM, I, ip_in), (ELEC, E, e_in), (MAGN, H, h_in)):
        strip = []
        for c in range(3):
            q = 3 * f + c
            X[c, 0] = zero
            X[c, cx + 1] = zero
            X[c, 1 : cx + 1, 0:16] = src[c]
            X[c, 1 : cx + 1, 16:24] = at.y_part(y1[q * cx : (q + 1) * cx])
            if f == PERM:
                X[c] = time_step * X[c]
            got = jnp.concatenate([z_in[q // 4], at.y_part(yz[q // 4])], axis=0)
            tile = at.strip_tile([X[c, x] for x in range(1, cx + 1)], time_step * got if f == PERM else got, q)
            strip.append(tile)
        strips.append(tuple(strip))
    si, se, sh = strips

    def sx_up(v):
        return jnp.where(lane >= 112, 0.0, pltpu.roll(v, 112, 1))

    def sx_down(v):
        return jnp.where(lane < 16, 0.0, pltpu.roll(v, 16, 1))

    xs = list(range(1, cx + 1))
    up_strip, down_strip = zero, zero
    for n in range(STEPS):
        downs = get(E, 1, (1, 2))
        new = []
        for x in xs:
            curl = curl_f(get(E, x), get(E, x + 1, (1, 2)), y_up, at.z_up)
            keep = time_step * at.keep_row
            new.append(tuple(q - keep * v for q, v in zip(get(H, x), curl)))
        put(H, xs, new)
        curl = curl_f(se, (sx_up(se[1]), sx_up(se[2])), y_up, sz_up)
        down_from = se
        sh = tuple(q - time_step * at.keep_row * v for q, v in zip(sh, curl))
        ups = get(H, cx, (1, 2))
        new, curls = [], []
        for x in xs:
            curl = curl_b(get(H, x), get(H, x - 1, (1, 2)), y_down, at.z_down)
            new.append(tuple(q + i * v for q, i, v in zip(get(E, x), get(I, x), curl)))
            curls.append(curl)
        put(E, xs, new)
        for x, curl in zip(xs, curls):
            for c in range(3):
                c_out[n, c, x - 1] = curl[c][0:16]
        curl = curl_b(sh, (sx_down(sh[1]), sx_down(sh[2])), y_down, sz_down)
        se = tuple(q + i * v for q, i, v in zip(se, si, curl))
        for c in range(3):
            sc_out[n, c] = curl[c]
        for k in range(2):
            i = 2 * n + k
            a_out[i] = jnp.where(at.even, ups[k], downs[k])
            b_out[i] = jnp.where(at.even, downs[k], ups[k])
            here = lane // 16 == i
            up_strip = jnp.where(here, pltpu.roll(sh[1 + k], (16 * i + 16) % 128, 1), up_strip)
            down_strip = jnp.where(here, pltpu.roll(down_from[1 + k], 16 * i, 1), down_strip)
    a_out[N_TRACES] = jnp.where(at.even, up_strip, down_strip)
    b_out[N_TRACES] = jnp.where(at.even, down_strip, up_strip)
    for c in range(3):
        e_out[c] = E[c, 1 : cx + 1, 0:16]
    sput(se_out, se)


def adjoint_kernel(ip_in, sd_in, a_in, b_in, z_in, za_in, zb_in, y1, yz, y2, c_own, sc_own,
                   i_out, si_out, p_out, sp_out, g_out, sg_out, I, W, M, PS, SI, SW, SM, SP):
    at = Place()
    cx = ip_in.shape[1]
    lane = at.lane
    last = cx + 2 * DEEP
    top = STEPS - 1
    a_base = jnp.where(at.even, DEEP + cx, 0)
    b_base = jnp.where(at.even, 0, DEEP + cx)
    for f, X, src in ((PERM, I, ip_in), (SEED, PS.at[top], sd_in)):
        for c in range(3):
            q = 3 * f + c
            off = DEEP * q
            X[c, last] = jnp.zeros((24, 128), F32)
            X[c, DEEP : DEEP + cx, 0:16] = src[c]
            X[c, DEEP : DEEP + cx, 16:24] = at.y_part(y1[q * cx : (q + 1) * cx])
            X[c, pl.ds(a_base, DEEP), 0:16] = a_in[off : off + DEEP]
            X[c, pl.ds(a_base, DEEP), 16:24] = at.y_part(y2[off : off + DEEP])
            X[c, pl.ds(b_base, DEEP), 0:16] = b_in[off : off + DEEP]
            X[c, pl.ds(b_base, DEEP), 16:24] = at.y_part(y2[N_SLOTS + off : N_SLOTS + off + DEEP])
    zs = 2 * N_SLOTS
    for f, X, S in ((PERM, I, SI), (SEED, PS.at[top], SP.at[top])):
        for c in range(3):
            q = 3 * f + c
            t = q // 4
            own = jnp.concatenate([z_in[t], at.y_part(yz[t])], axis=0)
            from_a = jnp.concatenate([za_in[t], at.y_part(y2[zs + t])], axis=0)
            from_b = jnp.concatenate([zb_in[t], at.y_part(y2[zs + 2 + t])], axis=0)
            above = jnp.where(at.even, from_a, from_b)
            below = jnp.where(at.even, from_b, from_a)
            halo = jnp.where(lane < 64, above, below)
            around = [X[c, DEEP + cx + k] for k in range(DEEP)] + [jnp.zeros((24, 128), F32)] * 2
            around += [X[c, k] for k in range(DEEP)]
            tiles = [at.strip_tile([X[c, DEEP + x] for x in range(cx)], own, q), at.strip_tile(around, halo, q)]
            S[c] = jnp.concatenate(tiles, axis=1)

    s_shape = (24, 256)
    s_keep = jnp.where((rows_of(s_shape) >= 20) & at.no_low_y, 0.0, 1.0)
    s_keep = jnp.where((lanes_of(s_shape) >= 192) & at.no_low_x, 0.0, s_keep)

    def sx_up(v):
        return pltpu.roll(v, 240, 1)

    def sx_down(v):
        return pltpu.roll(v, 16, 1)

    def keep_at(x):
        return at.keep_row * jnp.where(at.no_low_x, 0.0, 1.0) if x < DEEP else at.keep_row

    def sweep(lo, hi, body):
        for first in range(lo, hi, 8):
            body(list(range(first, min(first + 8, hi))))

    def halve(xs):
        new = []
        for x in xs:
            half = tuple(time_step * v for v in get(I, x))
            new.append((half, tuple(a * b for a, b in zip(half, get(PS.at[top], x)))))
        put(I, xs, [n[0] for n in new])
        put(W, xs, [n[1] for n in new])

    sweep(0, last, halve)
    for c in range(3):
        W[c, last] = jnp.zeros((24, 128), F32)
        i_out[c] = I[c, 1 : 1 + i_out.shape[1]]
    half = tuple(time_step * v for v in sget(SI))
    sput(SI, half)
    sput(si_out, half)
    sput(SW, tuple(a * b for a, b in zip(half, sget(SP.at[top]))))

    for m in range(STEPS - 1):
        n = top - m

        def magnetic(xs, m=m):
            new = []
            for x in xs:
                curl = curl_f(get(W, x), get(W, x + 1, (1, 2)), y_up, at.z_up)
                keep = keep_at(x)
                if m == 0:
                    new.append(tuple(keep * v for v in curl))
                else:
                    new.append(tuple(q + keep * v for q, v in zip(get(M, x), curl)))
            put(M, xs, new)

        def electric(xs, m=m, n=n):
            new = []
            for x in xs:
                curl = curl_b(get(M, x), get(M, x - 1, (1, 2)), y_down, at.z_down)
                p = tuple(q - time_step * v for q, v in zip(get(PS.at[n], x), curl))
                new.append((p, tuple(a * b for a, b in zip(get(I, x), p))))
            put(PS.at[n - 1], xs, [v[0] for v in new])
            if m < STEPS - 2:
                put(W, xs, [v[1] for v in new])

        sweep(m, last - 1 - m, magnetic)
        v = sget(SW)
        curl = curl_f(v, (sx_up(v[1]), sx_up(v[2])), y_up, sz_up)
        if m == 0:
            merged = tuple(s_keep * v for v in curl)
        else:
            merged = tuple(q + s_keep * v for q, v in zip(sget(SM), curl))
        sput(SM, merged)
        curl = curl_b(merged, (sx_down(merged[1]), sx_down(merged[2])), y_down, sz_down)
        p = tuple(q - time_step * v for q, v in zip(sget(SP.at[n]), curl))
        sput(SP.at[n - 1], p)
        sput(SW, tuple(a * b for a, b in zip(sget(SI), p)))
        sweep(m + 1, last - 1 - m, electric)

    for c in range(3):
        for x in range(cx):
            g = jnp.zeros((16, 128), F32)
            for n in range(STEPS):
                p = PS[n, c, DEEP + x, 0:16]
                g = g + p * c_own[n, c, x]
                if n < top:
                    p_out[n, c, x] = p
            g_out[c, x] = g
        g = jnp.zeros((24, 128), F32)
        for n in range(STEPS):
            p = SP[n, c, :, 0:128]
            g = g + p * sc_own[n, c]
            sp_out[n, c] = p
        sg_out[c] = g


LOW_H = ([-1], [-2, -1, 0], [-2, -1, 0, 1], [-1, 0, 1, 2])
LOW_E = ([-1, 0], [-2, -1, 0, 1], [-1, 0, 1, 2], [0, 1, 2, 3])
HIGH_H = ([-1], [-2, -1, 0], [-3, -2, -1, 0], [-4, -3, -2, -1])
HIGH_E = ([-1, 0], [-2, -1, 0, 1], [-3, -2, -1, 0], [-4, -3, -2, -1])


def driven_kernel(sd_in, a_sent, b_sent, a_in, b_in, e_own, se_own, i_in, si_in, p_in, sp_in, g_own, sg_own, ids,
                  e_out, s_out, E, H, G):
    at = Place()
    cx = e_own.shape[1]
    lane = at.lane
    base = 3
    zero = jnp.zeros((24, 128), F32)
    for c in range(3):
        for x in range(E.shape[1]):
            E[c, x] = zero
            H[c, x] = zero
        G[c] = g_own[c]

    def traces(a, b, i):
        return jnp.where(at.even, a[i], b[i])

    def upper(i):
        return traces(a_in, b_in, i)

    def lower(i):
        return traces(b_in, a_in, i)

    def own_up(i):
        return traces(a_sent, b_sent, i)

    def own_down(i):
        return traces(b_sent, a_sent, i)

    s_upper, s_lower, s_own_up, s_own_down = (t(N_TRACES) for t in (upper, lower, own_up, own_down))
    s_shape = (24, 256)
    s_keep = jnp.where((rows_of(s_shape) >= 20) & at.no_low_y, 0.0, time_step)
    s_keep = jnp.where((lanes_of(s_shape) >= 192) & at.no_low_x, 0.0, s_keep)

    def source(first, second, i, group):
        tiles = [pltpu.roll(v, (16 * (group - i)) % 128, 1) for v in (first, second)]
        return jnp.concatenate([jnp.where(lane // 16 == group, v, 0.0) for v in tiles], axis=1)

    si = sget(si_in)
    se = sh = (jnp.zeros(s_shape, F32),) * 3
    sg = sget(sg_own)
    for n in range(STEPS):
        xs = LOW_H[n] + [cx + x for x in HIGH_H[n]]
        new = []
        for x in xs:
            nxt = get(E, base + x + 1, (1, 2))
            if x == -1:
                nxt = tuple(v + own_down(2 * n + k) for k, v in enumerate(nxt))
            if x == cx - 1:
                nxt = tuple(v + upper(2 * n + k) for k, v in enumerate(nxt))
            curl = curl_f(get(E, base + x), nxt, y_up, at.z_up)
            keep = time_step * at.keep_row
            if x < 0:
                keep = keep * jnp.where(at.no_low_x, 0.0, 1.0)
            new.append(tuple(q - keep * v for q, v in zip(get(H, base + x), curl)))
        put(H, [base + x for x in xs], new)
        nxt = tuple(pltpu.roll(se[1 + k], 240, 1) + source(s_upper, s_own_down, 2 * n + k, 7) for k in range(2))
        curl = curl_f(se, nxt, y_up, sz_up)
        sh = tuple(q - s_keep * v for q, v in zip(sh, curl))

        xs = LOW_E[n] + [cx + x for x in HIGH_E[n]]
        new, grads = [], []
        for x in xs:
            prv = get(H, base + x - 1, (1, 2))
            if x == 0:
                prv = tuple(v + lower(2 * n + k) for k, v in enumerate(prv))
            if x == cx:
                prv = tuple(v + own_up(2 * n + k) for k, v in enumerate(prv))
            curl = curl_b(get(H, base + x), prv, y_down, at.z_down)
            new.append(tuple(q + i * v for q, i, v in zip(get(E, base + x), get(i_in, 2 + x), curl)))
            grads.append(curl)
        put(E, [base + x for x in xs], new)
        for x, curl in zip(xs, grads):
            if 0 <= x < cx:
                for c in range(3):
                    p = sd_in[c, x] if n == STEPS - 1 else p_in[n, c, x]
                    G[c, x] += p * curl[c][0:16]
        prv = tuple(pltpu.roll(sh[1 + k], 16, 1) + source(s_lower, s_own_up, 2 * n + k, 0) for k in range(2))
        curl = curl_b(sh, prv, y_down, sz_down)
        se = tuple(q + i * v for q, i, v in zip(se, si, curl))
        sg = tuple(g + sp_in[n, c] * curl[c][:, 0:128] for c, g in enumerate(sg))

    lane16 = lanes_of((16, 128))
    seam_lo = jnp.where(at.gz == 0, 128 - EDGE, 0)
    seam = (lane16 >= seam_lo) & (lane16 < seam_lo + EDGE)
    s_elec = [(se[c][0:16, 0:128] + se_own[c, 0:16]) for c in range(3)]
    s_grad = [sg[c][0:16] for c in range(3)]

    def with_seam(plane, strip, x):
        moved = pltpu.roll(strip, (seam_lo - 16 * x - EDGE + 256) % 128, 1)
        return jnp.where(seam, moved, plane)

    acc = jnp.zeros((80, 128), F32)
    for x in range(cx):
        grads = []
        for c in range(3):
            e_out[c, x] = with_seam(E[c, base + x, 0:16] + e_own[c, x], s_elec[c], x)
            grads.append(with_seam(G[c, x], s_grad[c], x))
        lhs, rhs = [], []
        for r in range(2):
            g = jnp.concatenate([v[8 * r : 8 * r + 8] for v in grads], axis=0)
            one = g.astype(jnp.bfloat16).astype(F32)
            rest = g - one
            two = rest.astype(jnp.bfloat16).astype(F32)
            three = rest - two
            lhs.append(jnp.concatenate([one, two, three, jnp.zeros((8, 128), F32)], axis=0).astype(jnp.bfloat16))
            region = ids[x, 8 * r : 8 * r + 8]
            slot = jnp.where(
                region < at.second_owner * REG_DEV,
                region - at.first_owner * REG_DEV,
                region - at.second_owner * REG_DEV + REG_DEV,
            )
            hot = jnp.concatenate([jnp.where(slot == s, 1.0, 0.0) for s in range(2 * REG_DEV)], axis=0)
            rhs.append(hot.astype(jnp.bfloat16))
        acc = acc + lax.dot_general(
            jnp.concatenate(lhs, axis=1),
            jnp.concatenate(rhs, axis=1),
            (((1,), (1,)), ((), ())),
            preferred_element_type=F32,
        )
    sums = acc[0:24] + acc[24:48] + acc[48:72]
    sums = jnp.where(rows_of((24, 128)) % 8 == lanes_of((24, 128)) % 8, sums, 0.0)
    parts = [jnp.sum(sums[8 * c : 8 * c + 8], axis=0, keepdims=True) for c in range(3)]
    parts = jnp.concatenate(parts + [jnp.zeros((5, 128), F32)], axis=0)
    fold = jnp.where(rows_of((128, 128)) // 8 == lanes_of((128, 128)), time_step * grad_scale, 0.0)
    s_out[...] = jnp.dot(parts, fold, precision=lax.Precision.HIGHEST, preferred_element_type=F32)


def y_rows(v):
    first = lax.broadcasted_iota(jnp.int32, (1, 8, 1), 1) < EDGE
    return jnp.where(first, v[:, 0:8], v[:, 8:16])


def local(e_start, h_start, inv_perm, adj_seed, region_ids):
    n_gx, n_gy = lax.axis_size("gx"), lax.axis_size("gy")
    xi = lax.axis_index("gx")
    cx = e_start.shape[1]
    even = (xi + 1) % 2
    vmem = pl.BlockSpec(memory_space=pltpu.VMEM)
    shape = lambda *dims: jax.ShapeDtypeStruct(dims, F32)
    tile = lambda *dims: pltpu.VMEM(dims, F32)

    a_pairs = [(i, i ^ 1) for i in range(n_gx)]
    b_pairs = [(i, ((i - 1) ^ 1) + 1) for i in range(1, n_gx - 1)]

    def swap_y(v):
        if n_gy == 2:
            return lax.ppermute(v, "gy", [(0, 1), (1, 0)])
        up = lax.ppermute(v, "gy", [(i, i + 1) for i in range(n_gy - 1)])
        down = lax.ppermute(v, "gy", [(i + 1, i) for i in range(n_gy - 1)])
        first = lax.broadcasted_iota(jnp.int32, (1, 8, 1), 1) < EDGE
        return jnp.where(first, down, up)

    def call(kernel, outs, scratch, args, mib, specs=None):
        return pl.pallas_call(
            kernel,
            out_shape=outs,
            in_specs=specs or [vmem] * len(args),
            out_specs=(vmem,) * len(outs),
            scratch_shapes=scratch,
            compiler_params=pltpu.CompilerParams(vmem_limit_bytes=mib * 1024 * 1024),
        )(*args)

    own = tile(*e_start.shape)
    a_msg, b_msg, z_msg, y_msg = call(
        pack_kernel,
        (shape(N_SLOTS, 16, 128), shape(N_SLOTS, 16, 128), shape(3, 16, 128), shape(12 * cx, 8, 128)),
        [own] * 4 + [pltpu.SemaphoreType.DMA((4,))],
        tuple(pltpu.with_memory_space_constraint(v, pltpu.HBM) for v in (inv_perm, adj_seed, e_start, h_start)),
        8,
        [pl.BlockSpec(memory_space=pltpu.HBM)] * 4,
    )
    z_got = lax.ppermute(z_msg, "gz", [(0, 1), (1, 0)])
    y1 = swap_y(y_msg)
    a_got = lax.ppermute(a_msg, "gx", a_pairs)
    b_got = lax.ppermute(b_msg, "gx", b_pairs)
    yz = swap_y(y_rows(z_got))
    za_got = lax.ppermute(z_got[0:2], "gx", a_pairs)
    zb_got = lax.ppermute(z_got[0:2], "gx", b_pairs)

    n_msg = N_TRACES + 1
    field = tile(3, cx + 2, 24, 128)
    a_sent, b_sent, c_own, e_own, sc_own, se_own = call(
        own_kernel,
        (
            shape(n_msg, 24, 128),
            shape(n_msg, 24, 128),
            shape(STEPS, 3, cx, 16, 128),
            shape(3, cx, 16, 128),
            shape(STEPS, 3, 24, 128),
            shape(3, 24, 128),
        ),
        [field] * 3,
        (inv_perm, e_start, h_start, y1, z_got, yz),
        8,
    )
    a_in = lax.ppermute(a_sent, "gx", a_pairs)
    b_in = lax.ppermute(b_sent, "gx", b_pairs)
    a_got, b_got, za_got, zb_got, _ = lax.optimization_barrier((a_got, b_got, za_got, zb_got, a_sent))
    y2 = swap_y(jnp.concatenate([y_rows(v) for v in (a_got, b_got, za_got, zb_got)], axis=0))

    planes = cx + 2 * DEEP + 1
    field = tile(3, planes, 24, 128)
    strip = tile(3, 24, 256)
    i_ext, si_ext, p_own, sp_own, g_own, sg_own = call(
        adjoint_kernel,
        (
            shape(3, cx + 4, 24, 128),
            shape(3, 24, 256),
            shape(STEPS - 1, 3, cx, 16, 128),
            shape(STEPS, 3, 24, 128),
            shape(3, cx, 16, 128),
            shape(3, 24, 128),
        ),
        [field] * 3 + [tile(STEPS, 3, planes, 24, 128)] + [strip] * 3 + [tile(STEPS, 3, 24, 256)],
        (inv_perm, adj_seed, a_got, b_got, z_got, za_got, zb_got, y1, yz, y2, c_own, sc_own),
        12,
    )
    field = tile(3, cx + 5, 24, 128)
    e_field, sums = call(
        driven_kernel,
        (shape(*e_start.shape), shape(8, 128)),
        [field] * 2 + [own],
        (adj_seed, a_sent, b_sent, a_in, b_in, e_own, se_own, i_ext, si_ext, p_own, sp_own, g_own, sg_own, region_ids),
        8,
    )
    total = sums + lax.ppermute(sums, "gx", a_pairs)
    owned = jnp.where(even == 1, total[0:3, 0:REG_DEV], total[0:3, REG_DEV : 2 * REG_DEV])
    return e_field, owned


def solution(mesh):
    placed = (
        P(None, "gx", "gy", "gz"),
        P(None, "gx", "gy", "gz"),
        P(None, "gx", "gy", "gz"),
        P(None, "gx", "gy", "gz"),
        P("gx", "gy", "gz"),
    )
    return jax.shard_map(
        local,
        mesh=mesh,
        in_specs=placed,
        out_specs=(P(None, "gx", "gy", "gz"), P(None, ("gx", "gy", "gz"))),
        check_vma=False,
    )
```

time: 283 us -> 32.8 us (0.12)
  starting transfers between devices: 160 us -> 21.5 us
  waiting for transfers between devices: 107 us -> 3.31 us
  other arithmetic: 8.33 us -> 0.9 us
  Pallas kernels: 0 us -> 5.89 us
    ppermute x72 -> x11, starting transfers between devices: 160 us -> 21.5 us  [the longest x1 5.72 us: local(): a_in = lax.ppermute(a_sent, 'gx', a_pairs)]
    ppermute x72 -> x11, waiting for transfers between devices: 107 us -> 3.31 us  [the longest x1 1.63 us: local(): a_in = lax.ppermute(a_sent, 'gx', a_pairs)]
    pallas_call x0 -> x4, Pallas kernels: none -> 5.89 us  [call(): pl.pallas_call(kernel, out_shape=outs, in_specs=specs or [vmem] * len(arg...]
    sub x31 -> x0, other arithmetic: 3.07 us -> none  [the longest x7 1.44 us: curl_of(): differences = [other - field_in for other in nearby]]
  transfers between devices with their start and end apart: 72 -> 11, of which waited for: 25 -> 3; matrix products, arithmetic and copies ran while one was open for 2% -> 0% of each run, Pallas kernels for 0% -> 7%
where the time goes in v3:
time: 32.8 us; the launch traced here: 32.4 us
  starting transfers between devices  21.5 us (66%)
  Pallas kernels  5.89 us (18%)
  waiting for transfers between devices  3.31 us (10%)
  other arithmetic  0.9 us (3%)
  between operations  0.81 us (2%)
    pallas_call x4, Pallas kernels, call(): pl.pallas_call(kernel, out_shape=outs, in_specs=specs or [vmem] * len(arg...  5.89 us
    ppermute x1, starting transfers between devices, local(): a_in = lax.ppermute(a_sent, 'gx', a_pairs)  5.72 us
    ppermute x1, starting transfers between devices, local(): total = sums + lax.ppermute(sums, 'gx', a_pairs)  4.66 us
    ppermute x1, starting transfers between devices, local(): za_got = lax.ppermute(z_got[0:2], 'gx', a_pairs)  4.34 us
    ppermute x1, starting transfers between devices, local(): z_got = lax.ppermute(z_msg, 'gz', [(0, 1), (1, 0)])  2.59 us
    ppermute x1, waiting for transfers between devices, local(): a_in = lax.ppermute(a_sent, 'gx', a_pairs)  1.63 us
    ppermute x1, waiting for transfers between devices, local(): total = sums + lax.ppermute(sums, 'gx', a_pairs)  1.58 us
    ppermute x1, starting transfers between devices, local(): a_got = lax.ppermute(a_msg, 'gx', a_pairs)  1.49 us
  transfers between devices with their start and end apart: 11, of which 3 were waited for; matrix products, arithmetic and copies ran while one was open for 0% of the time, Pallas kernels for 7%

profile of v3, /device:TPU:0, one launch (start us, length us, event | category | flops | bytes accessed | tf_op | source)
XLA Modules:
  0.0 32.4 jit_solution(12683630303847442014)
XLA Ops:
  0.7 1.6 %shard_map.68 = (f32[18,16,128]{2,1,0:T(8,128)S(1)}, f32[18,16,128]{2,1,0:T(8,128)S(1)}, f32[3,16,128]{2,1,0:T(8,128)S(1)}, f32[96,8,128]{2,1,0:T(8,128)S(1)}) custom-call(f32[3,8,16,128]{3,2,1,0:T(8,128)} %ip_in.3, f32[3,8,16,128]{3,2,1,0:T(8,128)} %sd_in.3, f32[3,8,16,128]{3,2,1,0:T(8,128)} %e_in.1, f32[3,8,16,128]{3,2,1,0:T(8,128)} %h_in.1), custom_call_target="tpu_custom_call" | custom-call | tf_op jit(solution)/shard_map/pallas_call | solution.py:523
  2.3 0.5 %collective-permute-start = (f32[96,8,128]{2,1,0:T(8,128)S(1)}, f32[96,8,128]{2,1,0:T(8,128)S(1)}, u32[]{:S(2)}, u32[]{:S(2)}) collective-permute-start(f32[96,8,128]{2,1,0:T(8,128)S(1)} %get-tuple-element.24), channel_id=1, source_target_pairs={{0,2},{2,0},{1,3},{3,1},{4,6},{6,4},{5,7},{7,5},{8,10},{10,8},{9,1... | collective-permute-start | bytes 1179656 | tf_op jit(solution)/shard_map/ppermute | solution.py:516
  2.8 2.6 %collective-permute-start.1 = (f32[3,16,128]{2,1,0:T(8,128)S(1)}, f32[3,16,128]{2,1,0:T(8,128)S(1)}, u32[]{:S(2)}, u32[]{:S(2)}) collective-permute-start(f32[3,16,128]{2,1,0:T(8,128)S(1)} %get-tuple-element.25), channel_id=1, source_target_pairs={{0,1},{1,0},{2,3},{3,2},{4,5},{5,4},{6,7},{7,6},{8,9},{9,8},{10,11... | collective-permute-start | bytes 73736 | tf_op jit(solution)/shard_map/ppermute | solution.py:541
  5.4 1.5 %collective-permute-start.5 = (f32[18,16,128]{2,1,0:T(8,128)S(1)}, f32[18,16,128]{2,1,0:T(8,128)S(1)}, u32[]{:S(2)}, u32[]{:S(2)}) collective-permute-start(f32[18,16,128]{2,1,0:T(8,128)S(1)} %get-tuple-element.30), channel_id=1, source_target_pairs={{0,4},{4,0},{8,12},{12,8},{16,20},{20,16},{24,28},{28,24},{1,5},{5... | collective-permute-start | bytes 442376 | tf_op jit(solution)/shard_map/ppermute | solution.py:543
  6.9 0.7 %collective-permute-start.6 = (f32[18,16,128]{2,1,0:T(8,128)S(1)}, f32[18,16,128]{2,1,0:T(8,128)S(1)}, u32[]{:S(2)}, u32[]{:S(2)}) collective-permute-start(f32[18,16,128]{2,1,0:T(8,128)S(1)} %get-tuple-element.31), channel_id=1, source_target_pairs={{4,8},{8,4},{12,16},{16,12},{20,24},{24,20},{5,9},{9,5},{13,17},{1... | collective-permute-start | bytes 442376 | tf_op jit(solution)/shard_map/ppermute | solution.py:544
  7.6 0.1 slice_select_fusion.2
  7.6 0.0 collective-permute-start.2
  7.7 4.3 %collective-permute-start.7 = (f32[2,16,128]{2,1,0:T(8,128)S(1)}, f32[2,16,128]{2,1,0:T(8,128)S(1)}, u32[]{:S(2)}, u32[]{:S(2)}) collective-permute-start(f32[2,16,128]{2,1,0:T(8,128)S(1)} %slice.55), channel_id=1, source_target_pairs={{0,4},{4,0},{8,12},{12,8},{16,20},{20,16},{24,28},{28,24},{1,5},{5... | collective-permute-start | bytes 49160 | tf_op jit(solution)/shard_map/ppermute | solution.py:546
  12.0 0.7 %collective-permute-start.8 = (f32[2,16,128]{2,1,0:T(8,128)S(1)}, f32[2,16,128]{2,1,0:T(8,128)S(1)}, u32[]{:S(2)}, u32[]{:S(2)}) collective-permute-start(f32[2,16,128]{2,1,0:T(8,128)S(1)} %slice.55), channel_id=1, source_target_pairs={{4,8},{8,4},{12,16},{16,12},{20,24},{24,20},{5,9},{9,5},{13,17},{1... | collective-permute-start | bytes 49160 | tf_op jit(solution)/shard_map/ppermute | solution.py:547
  12.7 1.1 %shard_map.69 = (f32[9,24,128]{2,1,0:T(8,128)S(1)}, f32[9,24,128]{2,1,0:T(8,128)S(1)}, f32[4,3,8,16,128]{4,3,2,1,0:T(8,128)S(1)}, f32[3,8,16,128]{3,2,1,0:T(8,12...) custom-call(f32[3,8,16,128]{3,2,1,0:T(8,128)S(1)} %copy-done.1, f32[3,8,16,128]{3,2,1,0:T(8,128)S(1)} %copy-done.2, ...), custom_call_target="tpu_custom_call" | custom-call | tf_op jit(solution)/shard_map/pallas_call | solution.py:523
  13.8 0.1 collective-permute-done.7.za_in
  13.9 0.1 slice_select_fusion.1
  14.0 0.0 copy-start
  14.0 0.1 slice_select_fusion.4
  14.1 0.2 collective-permute-start.9
  14.2 5.7 %collective-permute-start.3 = (f32[9,24,128]{2,1,0:T(8,128)S(1)}, f32[9,24,128]{2,1,0:T(8,128)S(1)}, u32[]{:S(2)}, u32[]{:S(2)}) collective-permute-start(f32[9,24,128]{2,1,0:T(8,128)S(1)} %get-tuple-element.26.a_sent), channel_id=1, source_target_pairs={{0,4},{4,0},{8,12},{12,8},{16,20},{20,16},{24,28},{28,24},{1,5},{5... | collective-permute-start | bytes 331784 | tf_op jit(solution)/shard_map/ppermute | solution.py:565
  20.0 0.7 %collective-permute-start.4 = (f32[9,24,128]{2,1,0:T(8,128)S(1)}, f32[9,24,128]{2,1,0:T(8,128)S(1)}, u32[]{:S(2)}, u32[]{:S(2)}) collective-permute-start(f32[9,24,128]{2,1,0:T(8,128)S(1)} %get-tuple-element.27.b_sent), channel_id=1, source_target_pairs={{4,8},{8,4},{12,16},{16,12},{20,24},{24,20},{5,9},{9,5},{13,17},{1... | collective-permute-start | bytes 331784 | tf_op jit(solution)/shard_map/ppermute | solution.py:566
  20.6 0.0 copy-start.4
  20.7 1.3 %shard_map.70 = (f32[3,12,24,128]{3,2,1,0:T(8,128)S(1)}, f32[3,24,256]{2,1,0:T(8,128)S(1)}, f32[3,3,8,16,128]{4,3,2,1,0:T(8,128)S(1)}, f32[4,3,24,128]{3,2,1,0:T...) custom-call(f32[3,8,16,128]{3,2,1,0:T(8,128)S(1)} %copy-done.1, f32[3,8,16,128]{3,2,1,0:T(8,128)S(1)} %copy-done, ...), custom_call_target="tpu_custom_call" | custom-call | tf_op jit(solution)/shard_map/pallas_call | solution.py:523
  22.0 1.6 %collective-permute-done.3.a_in = f32[9,24,128]{2,1,0:T(8,128)S(1)} collective-permute-done((f32[9,24,128]{2,1,0:T(8,128)S(1)}, f32[9,24,128]{2,1,0:T(8,128)S(1)}, u32[]{:S(2)}, u32[]{:S(2)}) %collective-permute-start.3) | collective-permute-done | bytes 110624 | tf_op jit(solution)/shard_map/ppermute | solution.py:565
  23.6 1.9 %shard_map.71 = (f32[3,8,16,128]{3,2,1,0:T(8,128)}, f32[8,128]{1,0:T(8,128)S(1)}) custom-call(f32[3,8,16,128]{3,2,1,0:T(8,128)S(1)} %copy-done, f32[9,24,128]{2,1,0:T(8,128)S(1)} %get-tuple-element.26.a_sent, f32[9,24,128]{2,1,0:T(8,128)S(1)} %get-tuple-element.27.b_sent, f32[9,24,128]{2,1,0:T(8,128)S(1)} %collective-permute-done.3.a_in, ...), custom_call_target="tpu_custom_call" | custom-call | tf_op jit(solution)/shard_map/pallas_call | solution.py:523
  25.5 4.7 %collective-permute-start.10 = (f32[8,128]{1,0:T(8,128)S(1)}, f32[8,128]{1,0:T(8,128)S(1)}, u32[]{:S(2)}, u32[]{:S(2)}) collective-permute-start(f32[8,128]{1,0:T(8,128)S(1)} %get-tuple-element.45), channel_id=1, source_target_pairs={{0,4},{4,0},{8,12},{12,8},{16,20},{20,16},{24,28},{28,24},{1,5},{5... | collective-permute-start | bytes 12296 | tf_op jit(solution)/shard_map/ppermute | solution.py:595
  30.2 1.6 %collective-permute-done.10 = f32[8,128]{1,0:T(8,128)S(1)} collective-permute-done((f32[8,128]{1,0:T(8,128)S(1)}, f32[8,128]{1,0:T(8,128)S(1)}, u32[]{:S(2)}, u32[]{:S(2)}) %collective-permute-start.10) | collective-permute-done | bytes 4128 | tf_op jit(solution)/shard_map/ppermute | solution.py:595
  31.8 0.7 %slice_select_fusion.5 = f32[3,8]{1,0:T(4,128)} fusion(f32[8,128]{1,0:T(8,128)S(1)} %add.12, pred[]{:T(512)S(6)} %eq.5), kind=kLoop, calls=%fused_computation.6 | loop fusion | flops 24 | bytes 289 | tf_op jit(solution)/shard_map/jit(_where)/select_n | solution.py:596
  (20 shorter events, 0.1 us)
Async XLA Ops:
  0.6 12.1 %copy-start.1 = (f32[3,8,16,128]{3,2,1,0:T(8,128)S(1)}, f32[3,8,16,128]{3,2,1,0:T(8,128)}, u32[]{:S(2)}) copy-start(f32[3,8,16,128]{3,2,1,0:T(8,128)} %ip_in.3) | copy-start | bytes 589828
  0.6 12.1 %copy-start.2 = (f32[3,8,16,128]{3,2,1,0:T(8,128)S(1)}, f32[3,8,16,128]{3,2,1,0:T(8,128)}, u32[]{:S(2)}) copy-start(f32[3,8,16,128]{3,2,1,0:T(8,128)} %e_in.1) | copy-start | bytes 589828
  0.7 12.1 %copy-start.3 = (f32[3,8,16,128]{3,2,1,0:T(8,128)S(1)}, f32[3,8,16,128]{3,2,1,0:T(8,128)}, u32[]{:S(2)}) copy-start(f32[3,8,16,128]{3,2,1,0:T(8,128)} %h_in.1) | copy-start | bytes 589828
  2.3 10.4 %collective-permute-start = (f32[96,8,128]{2,1,0:T(8,128)S(1)}, f32[96,8,128]{2,1,0:T(8,128)S(1)}, u32[]{:S(2)}, u32[]{:S(2)}) collective-permute-start(f32[96,8,128]{2,1,0:T(8,128)S(1)} %get-tuple-element.24), channel_id=1, source_target_pairs={{0,2},{2,0},{1,3},{3,1},{4,6},{6,4},{5,7},{7,5},{8,10},{10,8},{9,1... | collective-permute-start | bytes 1179656 | tf_op jit(solution)/shard_map/ppermute | solution.py:516
  2.8 4.8 %collective-permute-start.1 = (f32[3,16,128]{2,1,0:T(8,128)S(1)}, f32[3,16,128]{2,1,0:T(8,128)S(1)}, u32[]{:S(2)}, u32[]{:S(2)}) collective-permute-start(f32[3,16,128]{2,1,0:T(8,128)S(1)} %get-tuple-element.25), channel_id=1, source_target_pairs={{0,1},{1,0},{2,3},{3,2},{4,5},{5,4},{6,7},{7,6},{8,9},{9,8},{10,11... | collective-permute-start | bytes 73736 | tf_op jit(solution)/shard_map/ppermute | solution.py:541
  5.4 8.5 %collective-permute-start.5 = (f32[18,16,128]{2,1,0:T(8,128)S(1)}, f32[18,16,128]{2,1,0:T(8,128)S(1)}, u32[]{:S(2)}, u32[]{:S(2)}) collective-permute-start(f32[18,16,128]{2,1,0:T(8,128)S(1)} %get-tuple-element.30), channel_id=1, source_target_pairs={{0,4},{4,0},{8,12},{12,8},{16,20},{20,16},{24,28},{28,24},{1,5},{5... | collective-permute-start | bytes 442376 | tf_op jit(solution)/shard_map/ppermute | solution.py:543
  6.9 7.0 %collective-permute-start.6 = (f32[18,16,128]{2,1,0:T(8,128)S(1)}, f32[18,16,128]{2,1,0:T(8,128)S(1)}, u32[]{:S(2)}, u32[]{:S(2)}) collective-permute-start(f32[18,16,128]{2,1,0:T(8,128)S(1)} %get-tuple-element.31), channel_id=1, source_target_pairs={{4,8},{8,4},{12,16},{16,12},{20,24},{24,20},{5,9},{9,5},{13,17},{1... | collective-permute-start | bytes 442376 | tf_op jit(solution)/shard_map/ppermute | solution.py:544
  7.6 4.4 %collective-permute-start.2 = (f32[3,8,128]{2,1,0:T(8,128)S(1)}, f32[3,8,128]{2,1,0:T(8,128)S(1)}, u32[]{:S(2)}, u32[]{:S(2)}) collective-permute-start(f32[3,8,128]{2,1,0:T(8,128)S(1)} %slice_select_fusion.2), channel_id=1, source_target_pairs={{0,2},{2,0},{1,3},{3,1},{4,6},{6,4},{5,7},{7,5},{8,10},{10,8},{9,1... | collective-permute-start | bytes 36872 | tf_op jit(solution)/shard_map/ppermute | solution.py:516
  7.7 6.2 %collective-permute-start.7 = (f32[2,16,128]{2,1,0:T(8,128)S(1)}, f32[2,16,128]{2,1,0:T(8,128)S(1)}, u32[]{:S(2)}, u32[]{:S(2)}) collective-permute-start(f32[2,16,128]{2,1,0:T(8,128)S(1)} %slice.55), channel_id=1, source_target_pairs={{0,4},{4,0},{8,12},{12,8},{16,20},{20,16},{24,28},{28,24},{1,5},{5... | collective-permute-start | bytes 49160 | tf_op jit(solution)/shard_map/ppermute | solution.py:546
  12.0 1.8 %collective-permute-start.8 = (f32[2,16,128]{2,1,0:T(8,128)S(1)}, f32[2,16,128]{2,1,0:T(8,128)S(1)}, u32[]{:S(2)}, u32[]{:S(2)}) collective-permute-start(f32[2,16,128]{2,1,0:T(8,128)S(1)} %slice.55), channel_id=1, source_target_pairs={{4,8},{8,4},{12,16},{16,12},{20,24},{24,20},{5,9},{9,5},{13,17},{1... | collective-permute-start | bytes 49160 | tf_op jit(solution)/shard_map/ppermute | solution.py:547
  14.0 6.7 %copy-start = (f32[3,8,16,128]{3,2,1,0:T(8,128)S(1)}, f32[3,8,16,128]{3,2,1,0:T(8,128)}, u32[]{:S(2)}) copy-start(f32[3,8,16,128]{3,2,1,0:T(8,128)} %sd_in.3) | copy-start | bytes 589828
  14.1 6.6 %collective-permute-start.9 = (f32[40,8,128]{2,1,0:T(8,128)S(1)}, f32[40,8,128]{2,1,0:T(8,128)S(1)}, u32[]{:S(2)}, u32[]{:S(2)}) collective-permute-start(f32[40,8,128]{2,1,0:T(8,128)S(1)} %pad_maximum_fusion), channel_id=1, source_target_pairs={{0,2},{2,0},{1,3},{3,1},{4,6},{6,4},{5,7},{7,5},{8,10},{10,8},{9,1... | collective-permute-start | bytes 491528 | tf_op jit(solution)/shard_map/ppermute | solution.py:516
  14.2 9.4 %collective-permute-start.3 = (f32[9,24,128]{2,1,0:T(8,128)S(1)}, f32[9,24,128]{2,1,0:T(8,128)S(1)}, u32[]{:S(2)}, u32[]{:S(2)}) collective-permute-start(f32[9,24,128]{2,1,0:T(8,128)S(1)} %get-tuple-element.26.a_sent), channel_id=1, source_target_pairs={{0,4},{4,0},{8,12},{12,8},{16,20},{20,16},{24,28},{28,24},{1,5},{5... | collective-permute-start | bytes 331784 | tf_op jit(solution)/shard_map/ppermute | solution.py:565
  20.0 3.7 %collective-permute-start.4 = (f32[9,24,128]{2,1,0:T(8,128)S(1)}, f32[9,24,128]{2,1,0:T(8,128)S(1)}, u32[]{:S(2)}, u32[]{:S(2)}) collective-permute-start(f32[9,24,128]{2,1,0:T(8,128)S(1)} %get-tuple-element.27.b_sent), channel_id=1, source_target_pairs={{4,8},{8,4},{12,16},{16,12},{20,24},{24,20},{5,9},{9,5},{13,17},{1... | collective-permute-start | bytes 331784 | tf_op jit(solution)/shard_map/ppermute | solution.py:566
  20.6 3.0 %copy-start.4 = (s32[8,16,128]{2,1,0:T(8,128)S(1)}, s32[8,16,128]{2,1,0:T(8,128)}, u32[]{:S(2)}) copy-start(s32[8,16,128]{2,1,0:T(8,128)} %ids.1) | copy-start | bytes 196612
  25.5 6.2 %collective-permute-start.10 = (f32[8,128]{1,0:T(8,128)S(1)}, f32[8,128]{1,0:T(8,128)S(1)}, u32[]{:S(2)}, u32[]{:S(2)}) collective-permute-start(f32[8,128]{1,0:T(8,128)S(1)} %get-tuple-element.45), channel_id=1, source_target_pairs={{0,4},{4,0},{8,12},{12,8},{16,20},{20,16},{24,28},{28,24},{1,5},{5... | collective-permute-start | bytes 12296 | tf_op jit(solution)/shard_map/ppermute | solution.py:595

commit v4 on v3

--- a/solution.py
+++ b/solution.py
@@ -78,16 +78,18 @@
         low = jnp.where(self.no_low_y, 0.0, 1.0)
         return v * jnp.where(rows_of(v.shape[-2:]) < EDGE, high, low)
 
-    def strip_tile(self, planes, got, q):
+    def strip_own(self, planes):
         lane = self.lane
         acc = jnp.zeros((24, 128), F32)
         for x, plane in enumerate(planes):
             acc = jnp.where(lane // 16 == x, pltpu.roll(plane, (16 * x + self.own_off) % 128, 1), acc)
         j = lane % 16
-        is_own = (j >= self.own_j) & (j < self.own_j + 8)
-        is_got = (j >= self.got_j) & (j < self.got_j + EDGE)
+        return jnp.where((j >= self.own_j) & (j < self.own_j + 8), acc, 0.0)
+
+    def strip_got(self, tile, got, q):
+        j = self.lane % 16
         got = pltpu.roll(got, (self.got_j - 4 * (q % 4) + 128) % 128, 1)
-        return jnp.where(is_own, acc, jnp.where(is_got, got, 0.0))
+        return jnp.where((j >= self.got_j) & (j < self.got_j + EDGE), got, tile)
 
     def z_up(self, v):
         return jnp.where(self.lane == 127, 0.0, roll_up(v, 1))
@@ -184,7 +186,8 @@
             if f == PERM:
                 X[c] = time_step * X[c]
             got = jnp.concatenate([z_in[q // 4], at.y_part(yz[q // 4])], axis=0)
-            tile = at.strip_tile([X[c, x] for x in range(1, cx + 1)], time_step * got if f == PERM else got, q)
+            tile = at.strip_own([X[c, x] for x in range(1, cx + 1)])
+            tile = at.strip_got(tile, time_step * got if f == PERM else got, q)
             strip.append(tile)
         strips.append(tuple(strip))
     si, se, sh = strips
@@ -229,6 +232,11 @@
             here = lane // 16 == i
             up_strip = jnp.where(here, pltpu.roll(sh[1 + k], (16 * i + 16) % 128, 1), up_strip)
             down_strip = jnp.where(here, pltpu.roll(down_from[1 + k], 16 * i, 1), down_strip)
+    edges = [jnp.concatenate([z_in[t], at.y_part(yz[t])], axis=0) for t in range(2)]
+    up_edges = jnp.where(lane < 64, pltpu.roll(edges[0], 64, 1), edges[1])
+    down_edges = jnp.where(lane < 64, edges[0], pltpu.roll(edges[1], 64, 1))
+    a_out[N_TRACES + 1] = jnp.where(at.even, up_edges, down_edges)
+    b_out[N_TRACES + 1] = jnp.where(at.even, down_edges, up_edges)
     a_out[N_TRACES] = jnp.where(at.even, up_strip, down_strip)
     b_out[N_TRACES] = jnp.where(at.even, down_strip, up_strip)
     for c in range(3):
@@ -236,8 +244,8 @@
     sput(se_out, se)
 
 
-def adjoint_kernel(ip_in, sd_in, a_in, b_in, z_in, za_in, zb_in, y1, yz, y2, c_own, sc_own,
-                   i_out, si_out, p_out, sp_out, g_out, sg_out, I, W, M, PS, SI, SW, SM, SP):
+def adjoint_kernel(ip_in, sd_in, a_in, b_in, z_in, y1, yz, y2, c_own,
+                   i_out, s_out, p_out, g_out, I, W, M, PS):
     at = Place()
     cx = ip_in.shape[1]
     lane = at.lane
@@ -256,31 +264,15 @@
             X[c, pl.ds(a_base, DEEP), 16:24] = at.y_part(y2[off : off + DEEP])
             X[c, pl.ds(b_base, DEEP), 0:16] = b_in[off : off + DEEP]
             X[c, pl.ds(b_base, DEEP), 16:24] = at.y_part(y2[N_SLOTS + off : N_SLOTS + off + DEEP])
-    zs = 2 * N_SLOTS
-    for f, X, S in ((PERM, I, SI), (SEED, PS.at[top], SP.at[top])):
+    for f, X in ((PERM, I), (SEED, PS.at[top])):
         for c in range(3):
             q = 3 * f + c
             t = q // 4
             own = jnp.concatenate([z_in[t], at.y_part(yz[t])], axis=0)
-            from_a = jnp.concatenate([za_in[t], at.y_part(y2[zs + t])], axis=0)
-            from_b = jnp.concatenate([zb_in[t], at.y_part(y2[zs + 2 + t])], axis=0)
-            above = jnp.where(at.even, from_a, from_b)
-            below = jnp.where(at.even, from_b, from_a)
-            halo = jnp.where(lane < 64, above, below)
             around = [X[c, DEEP + cx + k] for k in range(DEEP)] + [jnp.zeros((24, 128), F32)] * 2
             around += [X[c, k] for k in range(DEEP)]
-            tiles = [at.strip_tile([X[c, DEEP + x] for x in range(cx)], own, q), at.strip_tile(around, halo, q)]
-            S[c] = jnp.concatenate(tiles, axis=1)
-
-    s_shape = (24, 256)
-    s_keep = jnp.where((rows_of(s_shape) >= 20) & at.no_low_y, 0.0, 1.0)
-    s_keep = jnp.where((lanes_of(s_shape) >= 192) & at.no_low_x, 0.0, s_keep)
-
-    def sx_up(v):
-        return pltpu.roll(v, 240, 1)
-
-    def sx_down(v):
-        return pltpu.roll(v, 16, 1)
+            s_out[q, :, 0:128] = at.strip_got(at.strip_own([X[c, DEEP + x] for x in range(cx)]), own, q)
+            s_out[q, :, 128:256] = at.strip_own(around)
 
     def keep_at(x):
         return at.keep_row * jnp.where(at.no_low_x, 0.0, 1.0) if x < DEEP else at.keep_row
@@ -301,10 +293,6 @@
     for c in range(3):
         W[c, last] = jnp.zeros((24, 128), F32)
         i_out[c] = I[c, 1 : 1 + i_out.shape[1]]
-    half = tuple(time_step * v for v in sget(SI))
-    sput(SI, half)
-    sput(si_out, half)
-    sput(SW, tuple(a * b for a, b in zip(half, sget(SP.at[top]))))
 
     for m in range(STEPS - 1):
         n = top - m
@@ -331,17 +319,6 @@
                 put(W, xs, [v[1] for v in new])
 
         sweep(m, last - 1 - m, magnetic)
-        v = sget(SW)
-        curl = curl_f(v, (sx_up(v[1]), sx_up(v[2])), y_up, sz_up)
-        if m == 0:
-            merged = tuple(s_keep * v for v in curl)
-        else:
-            merged = tuple(q + s_keep * v for q, v in zip(sget(SM), curl))
-        sput(SM, merged)
-        curl = curl_b(merged, (sx_down(merged[1]), sx_down(merged[2])), y_down, sz_down)
-        p = tuple(q - time_step * v for q, v in zip(sget(SP.at[n]), curl))
-        sput(SP.at[n - 1], p)
-        sput(SW, tuple(a * b for a, b in zip(sget(SI), p)))
         sweep(m + 1, last - 1 - m, electric)
 
     for c in range(3):
@@ -353,12 +330,6 @@
                 if n < top:
                     p_out[n, c, x] = p
             g_out[c, x] = g
-        g = jnp.zeros((24, 128), F32)
-        for n in range(STEPS):
-            p = SP[n, c, :, 0:128]
-            g = g + p * sc_own[n, c]
-            sp_out[n, c] = p
-        sg_out[c] = g
 
 
 LOW_H = ([-1], [-2, -1, 0], [-2, -1, 0, 1], [-1, 0, 1, 2])
@@ -367,7 +338,7 @@
 HIGH_E = ([-1, 0], [-2, -1, 0, 1], [-3, -2, -1, 0], [-4, -3, -2, -1])
 
 
-def driven_kernel(sd_in, a_sent, b_sent, a_in, b_in, e_own, se_own, i_in, si_in, p_in, sp_in, g_own, sg_own, ids,
+def driven_kernel(sd_in, a_sent, b_sent, a_in, b_in, e_own, sc_own, se_own, i_in, s_in, p_in, g_own, ids,
                   e_out, s_out, E, H, G):
     at = Place()
     cx = e_own.shape[1]
@@ -404,9 +375,29 @@
         tiles = [pltpu.roll(v, (16 * (group - i)) % 128, 1) for v in (first, second)]
         return jnp.concatenate([jnp.where(lane // 16 == group, v, 0.0) for v in tiles], axis=1)
 
-    si = sget(si_in)
+    above, below = upper(N_TRACES + 1), lower(N_TRACES + 1)
+    edges = (
+        jnp.where(lane < 64, above, pltpu.roll(below, 64, 1)),
+        jnp.where(lane < 64, pltpu.roll(above, 64, 1), below),
+    )
+    strips = []
+    for q in range(6):
+        tile = at.strip_got(s_in[q, :, 128:256], edges[q // 4], q)
+        strips.append(jnp.concatenate([s_in[q, :, 0:128], tile], axis=1))
+    si = tuple(time_step * v for v in strips[0:3])
+    sp = tuple(strips[3:6])
+    adjoint = [None] * (STEPS - 1) + [sp]
+    sm = (0.0, 0.0, 0.0)
+    for n in range(STEPS - 1, 0, -1):
+        sw = tuple(a * b for a, b in zip(si, sp))
+        curl = curl_f(sw, [pltpu.roll(v, 240, 1) for v in sw[1:]], y_up, sz_up)
+        sm = tuple(q + 2.0 * s_keep * v for q, v in zip(sm, curl))
+        curl = curl_b(sm, [pltpu.roll(v, 16, 1) for v in sm[1:]], y_down, sz_down)
+        sp = tuple(q - time_step * v for q, v in zip(sp, curl))
+        adjoint[n - 1] = sp
+
     se = sh = (jnp.zeros(s_shape, F32),) * 3
-    sg = sget(sg_own)
+    sg = (0.0, 0.0, 0.0)
     for n in range(STEPS):
         xs = LOW_H[n] + [cx + x for x in HIGH_H[n]]
         new = []
@@ -446,7 +437,9 @@
         prv = tuple(pltpu.roll(sh[1 + k], 16, 1) + source(s_lower, s_own_up, 2 * n + k, 0) for k in range(2))
         curl = curl_b(sh, prv, y_down, sz_down)
         se = tuple(q + i * v for q, i, v in zip(se, si, curl))
-        sg = tuple(g + sp_in[n, c] * curl[c][:, 0:128] for c, g in enumerate(sg))
+        sg = tuple(
+            g + adjoint[n][c][:, 0:128] * (curl[c][:, 0:128] + sc_own[n, c]) for c, g in enumerate(sg)
+        )
 
     lane16 = lanes_of((16, 128))
     seam_lo = jnp.where(at.gz == 0, 128 - EDGE, 0)
@@ -543,10 +536,8 @@
     a_got = lax.ppermute(a_msg, "gx", a_pairs)
     b_got = lax.ppermute(b_msg, "gx", b_pairs)
     yz = swap_y(y_rows(z_got))
-    za_got = lax.ppermute(z_got[0:2], "gx", a_pairs)
-    zb_got = lax.ppermute(z_got[0:2], "gx", b_pairs)
-
-    n_msg = N_TRACES + 1
+
+    n_msg = N_TRACES + 2
     field = tile(3, cx + 2, 24, 128)
     a_sent, b_sent, c_own, e_own, sc_own, se_own = call(
         own_kernel,
@@ -564,24 +555,21 @@
     )
     a_in = lax.ppermute(a_sent, "gx", a_pairs)
     b_in = lax.ppermute(b_sent, "gx", b_pairs)
-    a_got, b_got, za_got, zb_got, _ = lax.optimization_barrier((a_got, b_got, za_got, zb_got, a_sent))
-    y2 = swap_y(jnp.concatenate([y_rows(v) for v in (a_got, b_got, za_got, zb_got)], axis=0))
+    a_got, b_got, _ = lax.optimization_barrier((a_got, b_got, a_sent))
+    y2 = swap_y(jnp.concatenate([y_rows(v) for v in (a_got, b_got)], axis=0))
 
     planes = cx + 2 * DEEP + 1
     field = tile(3, planes, 24, 128)
-    strip = tile(3, 24, 256)
-    i_ext, si_ext, p_own, sp_own, g_own, sg_own = call(
+    i_ext, s_ext, p_own, g_own = call(
         adjoint_kernel,
         (
             shape(3, cx + 4, 24, 128),
-            shape(3, 24, 256),
+            shape(6, 24, 256),
             shape(STEPS - 1, 3, cx, 16, 128),
-            shape(STEPS, 3, 24, 128),
             shape(3, cx, 16, 128),
-            shape(3, 24, 128),
         ),
-        [field] * 3 + [tile(STEPS, 3, planes, 24, 128)] + [strip] * 3 + [tile(STEPS, 3, 24, 256)],
-        (inv_perm, adj_seed, a_got, b_got, z_got, za_got, zb_got, y1, yz, y2, c_own, sc_own),
+        [field] * 3 + [tile(STEPS, 3, planes, 24, 128)],
+        (inv_perm, adj_seed, a_got, b_got, z_got, y1, yz, y2, c_own),
         12,
     )
     field = tile(3, cx + 5, 24, 128)
@@ -589,7 +577,7 @@
         driven_kernel,
         (shape(*e_start.shape), shape(8, 128)),
         [field] * 2 + [own],
-        (adj_seed, a_sent, b_sent, a_in, b_in, e_own, se_own, i_ext, si_ext, p_own, sp_own, g_own, sg_own, region_ids),
+        (adj_seed, a_sent, b_sent, a_in, b_in, e_own, sc_own, se_own, i_ext, s_ext, p_own, g_own, region_ids),
         8,
     )
     total = sums + lax.ppermute(sums, "gx", a_pairs)

time: 32.8 us -> 29.3 us (0.89)
  starting transfers between devices: 21.5 us -> 15.4 us
  waiting for transfers between devices: 3.31 us -> 6.35 us
    ppermute x2 -> x0, starting transfers between devices: 4.99 us -> none  [the longest x1 4.34 us: local(): za_got = lax.ppermute(z_got[0:2], 'gx', a_pairs)]
    ppermute x1, waiting for transfers between devices: 0.01 us -> 1.38 us  [local(): a_got = lax.ppermute(a_msg, 'gx', a_pairs)]
    ppermute x3, waiting for transfers between devices: 0.01 us -> 1.17 us  [swap_y(): return lax.ppermute(v, 'gy', [(0, 1), (1, 0)])]
    ppermute x1, starting transfers between devices: 5.72 us -> 4.72 us  [local(): a_in = lax.ppermute(a_sent, 'gx', a_pairs)]
    ppermute x1, waiting for transfers between devices: 1.63 us -> 2.21 us  [local(): a_in = lax.ppermute(a_sent, 'gx', a_pairs)]
  transfers between devices with their start and end apart: 11 -> 9, of which waited for: 3 -> 4; matrix products, arithmetic and copies ran while one was open for 0% -> 0% of each run, Pallas kernels for 7% -> 7%
where the time goes in v4:
time: 29.3 us; the launch traced here: 28.9 us
  starting transfers between devices  15.4 us (53%)
  waiting for transfers between devices  6.35 us (22%)
  Pallas kernels  5.58 us (19%)
  other arithmetic  0.83 us (3%)
  between operations  0.78 us (3%)
    pallas_call x4, Pallas kernels, call(): pl.pallas_call(kernel, out_shape=outs, in_specs=specs or [vmem] * len(arg...  5.58 us
    ppermute x1, starting transfers between devices, local(): a_in = lax.ppermute(a_sent, 'gx', a_pairs)  4.72 us
    ppermute x1, starting transfers between devices, local(): total = sums + lax.ppermute(sums, 'gx', a_pairs)  4.66 us
    ppermute x1, starting transfers between devices, local(): z_got = lax.ppermute(z_msg, 'gz', [(0, 1), (1, 0)])  2.59 us
    ppermute x1, waiting for transfers between devices, local(): a_in = lax.ppermute(a_sent, 'gx', a_pairs)  2.21 us
    ppermute x1, waiting for transfers between devices, local(): total = sums + lax.ppermute(sums, 'gx', a_pairs)  1.58 us
    ppermute x1, starting transfers between devices, local(): a_got = lax.ppermute(a_msg, 'gx', a_pairs)  1.49 us
    ppermute x1, waiting for transfers between devices, local(): a_got = lax.ppermute(a_msg, 'gx', a_pairs)  1.38 us
  transfers between devices with their start and end apart: 9, of which 4 were waited for; matrix products, arithmetic and copies ran while one was open for 0% of the time, Pallas kernels for 7%

profile of v4, /device:TPU:0, one launch (start us, length us, event | category | flops | bytes accessed | tf_op | source)
XLA Modules:
  0.0 28.9 jit_solution(15301160971637777128)
XLA Ops:
  0.7 1.6 %shard_map.68 = (f32[18,16,128]{2,1,0:T(8,128)S(1)}, f32[18,16,128]{2,1,0:T(8,128)S(1)}, f32[3,16,128]{2,1,0:T(8,128)S(1)}, f32[96,8,128]{2,1,0:T(8,128)S(1)}) custom-call(f32[3,8,16,128]{3,2,1,0:T(8,128)} %ip_in.3, f32[3,8,16,128]{3,2,1,0:T(8,128)} %sd_in.3, f32[3,8,16,128]{3,2,1,0:T(8,128)} %e_in.1, f32[3,8,16,128]{3,2,1,0:T(8,128)} %h_in.1), custom_call_target="tpu_custom_call" | custom-call | tf_op jit(solution)/shard_map/pallas_call | solution.py:516
  2.3 0.5 %collective-permute-start = (f32[96,8,128]{2,1,0:T(8,128)S(1)}, f32[96,8,128]{2,1,0:T(8,128)S(1)}, u32[]{:S(2)}, u32[]{:S(2)}) collective-permute-start(f32[96,8,128]{2,1,0:T(8,128)S(1)} %get-tuple-element.20), channel_id=1, source_target_pairs={{0,2},{2,0},{1,3},{3,1},{4,6},{6,4},{5,7},{7,5},{8,10},{10,8},{9,1... | collective-permute-start | bytes 1179656 | tf_op jit(solution)/shard_map/ppermute | solution.py:509
  2.8 2.6 %collective-permute-start.1 = (f32[3,16,128]{2,1,0:T(8,128)S(1)}, f32[3,16,128]{2,1,0:T(8,128)S(1)}, u32[]{:S(2)}, u32[]{:S(2)}) collective-permute-start(f32[3,16,128]{2,1,0:T(8,128)S(1)} %get-tuple-element.21), channel_id=1, source_target_pairs={{0,1},{1,0},{2,3},{3,2},{4,5},{5,4},{6,7},{7,6},{8,9},{9,8},{10,11... | collective-permute-start | bytes 73736 | tf_op jit(solution)/shard_map/ppermute | solution.py:534
  5.4 1.5 %collective-permute-start.5 = (f32[18,16,128]{2,1,0:T(8,128)S(1)}, f32[18,16,128]{2,1,0:T(8,128)S(1)}, u32[]{:S(2)}, u32[]{:S(2)}) collective-permute-start(f32[18,16,128]{2,1,0:T(8,128)S(1)} %get-tuple-element.27), channel_id=1, source_target_pairs={{0,4},{4,0},{8,12},{12,8},{16,20},{20,16},{24,28},{28,24},{1,5},{5... | collective-permute-start | bytes 442376 | tf_op jit(solution)/shard_map/ppermute | solution.py:536
  6.9 0.7 %collective-permute-start.6 = (f32[18,16,128]{2,1,0:T(8,128)S(1)}, f32[18,16,128]{2,1,0:T(8,128)S(1)}, u32[]{:S(2)}, u32[]{:S(2)}) collective-permute-start(f32[18,16,128]{2,1,0:T(8,128)S(1)} %get-tuple-element.28), channel_id=1, source_target_pairs={{4,8},{8,4},{12,16},{16,12},{20,24},{24,20},{5,9},{9,5},{13,17},{1... | collective-permute-start | bytes 442376 | tf_op jit(solution)/shard_map/ppermute | solution.py:537
  7.6 0.0 collective-permute-done.1.z_in
  7.6 0.1 slice_select_fusion.2
  7.6 0.0 collective-permute-start.2
  7.7 1.2 %collective-permute-done.2.yz = f32[3,8,128]{2,1,0:T(8,128)S(1)} collective-permute-done((f32[3,8,128]{2,1,0:T(8,128)S(1)}, f32[3,8,128]{2,1,0:T(8,128)S(1)}, u32[]{:S(2)}, u32[]{:S(2)}) %collective-permute-start.2) | collective-permute-done | bytes 12320 | tf_op jit(solution)/shard_map/ppermute | solution.py:509
  8.8 0.0 collective-permute-done.y1
  8.8 1.1 %shard_map.69 = (f32[10,24,128]{2,1,0:T(8,128)S(1)}, f32[10,24,128]{2,1,0:T(8,128)S(1)}, f32[4,3,8,16,128]{4,3,2,1,0:T(8,128)S(1)}, f32[3,8,16,128]{3,2,1,0:T(8,...) custom-call(f32[3,8,16,128]{3,2,1,0:T(8,128)S(1)} %copy-done.1, f32[3,8,16,128]{3,2,1,0:T(8,128)S(1)} %copy-done.2, ...), custom_call_target="tpu_custom_call" | custom-call | tf_op jit(solution)/shard_map/pallas_call | solution.py:516
  9.9 1.4 %collective-permute-done.5.a_in = f32[18,16,128]{2,1,0:T(8,128)S(1)} collective-permute-done((f32[18,16,128]{2,1,0:T(8,128)S(1)}, f32[18,16,128]{2,1,0:T(8,128)S(1)}, u32[]{:S(2)}, u32[]{:S(2)}) %collective-permute-start.5) | collective-permute-done | bytes 147488 | tf_op jit(solution)/shard_map/ppermute | solution.py:536
  11.3 0.1 slice_select_fusion.1
  11.4 0.0 copy-start
  11.4 0.1 collective-permute-start.7
  11.5 4.7 %collective-permute-start.3 = (f32[10,24,128]{2,1,0:T(8,128)S(1)}, f32[10,24,128]{2,1,0:T(8,128)S(1)}, u32[]{:S(2)}, u32[]{:S(2)}) collective-permute-start(f32[10,24,128]{2,1,0:T(8,128)S(1)} %get-tuple-element.22.a_sent), channel_id=1, source_target_pairs={{0,4},{4,0},{8,12},{12,8},{16,20},{20,16},{24,28},{28,24},{1,5},{5... | collective-permute-start | bytes 368648 | tf_op jit(solution)/shard_map/ppermute | solution.py:556
  16.2 0.7 %collective-permute-start.4 = (f32[10,24,128]{2,1,0:T(8,128)S(1)}, f32[10,24,128]{2,1,0:T(8,128)S(1)}, u32[]{:S(2)}, u32[]{:S(2)}) collective-permute-start(f32[10,24,128]{2,1,0:T(8,128)S(1)} %get-tuple-element.23.b_sent), channel_id=1, source_target_pairs={{4,8},{8,4},{12,16},{16,12},{20,24},{24,20},{5,9},{9,5},{13,17},{1... | collective-permute-start | bytes 368648 | tf_op jit(solution)/shard_map/ppermute | solution.py:557
  16.9 0.0 copy-start.4
  16.9 1.0 %shard_map.70 = (f32[3,12,24,128]{3,2,1,0:T(8,128)S(1)}, f32[6,24,256]{2,1,0:T(8,128)S(1)}, f32[3,3,8,16,128]{4,3,2,1,0:T(8,128)S(1)}, f32[3,8,16,128]{3,2,1,0:T(8,128)S(1)}) custom-call(f32[3,8,16,128]{3,2,1,0:T(8,128)S(1)} %copy-done.1, f32[3,8,16,128]{3,2,1,0:T(8,128)S(1)} %copy-done, f32[18,16,128]{2,1,0:T(8,128)S(1)} %collective-permute-done.5.a_in, ...), custom_call_target="tpu_custom_call" | custom-call | tf_op jit(solution)/shard_map/pallas_call | solution.py:516
  17.9 2.2 %collective-permute-done.3.a_in = f32[10,24,128]{2,1,0:T(8,128)S(1)} collective-permute-done((f32[10,24,128]{2,1,0:T(8,128)S(1)}, f32[10,24,128]{2,1,0:T(8,128)S(1)}, u32[]{:S(2)}, u32[]{:S(2)}) %collective-permute-start.3) | collective-permute-done | bytes 122912 | tf_op jit(solution)/shard_map/ppermute | solution.py:556
  20.1 1.9 %shard_map.71 = (f32[3,8,16,128]{3,2,1,0:T(8,128)}, f32[8,128]{1,0:T(8,128)S(1)}) custom-call(f32[3,8,16,128]{3,2,1,0:T(8,128)S(1)} %copy-done, f32[10,24,128]{2,1,0:T(8,128)S(1)} %get-tuple-element.22.a_sent, f32[10,24,128]{2,1,0:T(8,128)S(1)} %get-tuple-element.23.b_sent, f32[10,24,128]{2,1,0:T(8,128)S(1)} %collective-permute-done.3.a_in, ...), custom_call_target="tpu_custom_call" | custom-call | tf_op jit(solution)/shard_map/pallas_call | solution.py:516
  22.0 4.7 %collective-permute-start.8 = (f32[8,128]{1,0:T(8,128)S(1)}, f32[8,128]{1,0:T(8,128)S(1)}, u32[]{:S(2)}, u32[]{:S(2)}) collective-permute-start(f32[8,128]{1,0:T(8,128)S(1)} %get-tuple-element.37), channel_id=1, source_target_pairs={{0,4},{4,0},{8,12},{12,8},{16,20},{20,16},{24,28},{28,24},{1,5},{5... | collective-permute-start | bytes 12296 | tf_op jit(solution)/shard_map/ppermute | solution.py:583
  26.7 1.6 %collective-permute-done.8 = f32[8,128]{1,0:T(8,128)S(1)} collective-permute-done((f32[8,128]{1,0:T(8,128)S(1)}, f32[8,128]{1,0:T(8,128)S(1)}, u32[]{:S(2)}, u32[]{:S(2)}) %collective-permute-start.8) | collective-permute-done | bytes 4128 | tf_op jit(solution)/shard_map/ppermute | solution.py:583
  28.3 0.7 %slice_select_fusion.3 = f32[3,8]{1,0:T(4,128)} fusion(f32[8,128]{1,0:T(8,128)S(1)} %add.12, pred[]{:T(512)S(6)} %eq.5), kind=kLoop, calls=%fused_computation.4 | loop fusion | flops 24 | bytes 289 | tf_op jit(solution)/shard_map/jit(_where)/select_n | solution.py:584
  (14 shorter events, 0.0 us)
Async XLA Ops:
  0.6 8.2 %copy-start.2 = (f32[3,8,16,128]{3,2,1,0:T(8,128)S(1)}, f32[3,8,16,128]{3,2,1,0:T(8,128)}, u32[]{:S(2)}) copy-start(f32[3,8,16,128]{3,2,1,0:T(8,128)} %e_in.1) | copy-start | bytes 589828
  0.6 8.2 %copy-start.3 = (f32[3,8,16,128]{3,2,1,0:T(8,128)S(1)}, f32[3,8,16,128]{3,2,1,0:T(8,128)}, u32[]{:S(2)}) copy-start(f32[3,8,16,128]{3,2,1,0:T(8,128)} %h_in.1) | copy-start | bytes 589828
  0.7 8.2 %copy-start.1 = (f32[3,8,16,128]{3,2,1,0:T(8,128)S(1)}, f32[3,8,16,128]{3,2,1,0:T(8,128)}, u32[]{:S(2)}) copy-start(f32[3,8,16,128]{3,2,1,0:T(8,128)} %ip_in.3) | copy-start | bytes 589828
  2.3 6.6 %collective-permute-start = (f32[96,8,128]{2,1,0:T(8,128)S(1)}, f32[96,8,128]{2,1,0:T(8,128)S(1)}, u32[]{:S(2)}, u32[]{:S(2)}) collective-permute-start(f32[96,8,128]{2,1,0:T(8,128)S(1)} %get-tuple-element.20), channel_id=1, source_target_pairs={{0,2},{2,0},{1,3},{3,1},{4,6},{6,4},{5,7},{7,5},{8,10},{10,8},{9,1... | collective-permute-start | bytes 1179656 | tf_op jit(solution)/shard_map/ppermute | solution.py:509
  2.8 4.8 %collective-permute-start.1 = (f32[3,16,128]{2,1,0:T(8,128)S(1)}, f32[3,16,128]{2,1,0:T(8,128)S(1)}, u32[]{:S(2)}, u32[]{:S(2)}) collective-permute-start(f32[3,16,128]{2,1,0:T(8,128)S(1)} %get-tuple-element.21), channel_id=1, source_target_pairs={{0,1},{1,0},{2,3},{3,2},{4,5},{5,4},{6,7},{7,6},{8,9},{9,8},{10,11... | collective-permute-start | bytes 73736 | tf_op jit(solution)/shard_map/ppermute | solution.py:534
  5.4 5.9 %collective-permute-start.5 = (f32[18,16,128]{2,1,0:T(8,128)S(1)}, f32[18,16,128]{2,1,0:T(8,128)S(1)}, u32[]{:S(2)}, u32[]{:S(2)}) collective-permute-start(f32[18,16,128]{2,1,0:T(8,128)S(1)} %get-tuple-element.27), channel_id=1, source_target_pairs={{0,4},{4,0},{8,12},{12,8},{16,20},{20,16},{24,28},{28,24},{1,5},{5... | collective-permute-start | bytes 442376 | tf_op jit(solution)/shard_map/ppermute | solution.py:536
  6.9 4.4 %collective-permute-start.6 = (f32[18,16,128]{2,1,0:T(8,128)S(1)}, f32[18,16,128]{2,1,0:T(8,128)S(1)}, u32[]{:S(2)}, u32[]{:S(2)}) collective-permute-start(f32[18,16,128]{2,1,0:T(8,128)S(1)} %get-tuple-element.28), channel_id=1, source_target_pairs={{4,8},{8,4},{12,16},{16,12},{20,24},{24,20},{5,9},{9,5},{13,17},{1... | collective-permute-start | bytes 442376 | tf_op jit(solution)/shard_map/ppermute | solution.py:537
  7.6 1.2 %collective-permute-start.2 = (f32[3,8,128]{2,1,0:T(8,128)S(1)}, f32[3,8,128]{2,1,0:T(8,128)S(1)}, u32[]{:S(2)}, u32[]{:S(2)}) collective-permute-start(f32[3,8,128]{2,1,0:T(8,128)S(1)} %slice_select_fusion.2), channel_id=1, source_target_pairs={{0,2},{2,0},{1,3},{3,1},{4,6},{6,4},{5,7},{7,5},{8,10},{10,8},{9,1... | collective-permute-start | bytes 36872 | tf_op jit(solution)/shard_map/ppermute | solution.py:509
  11.4 5.5 %copy-start = (f32[3,8,16,128]{3,2,1,0:T(8,128)S(1)}, f32[3,8,16,128]{3,2,1,0:T(8,128)}, u32[]{:S(2)}) copy-start(f32[3,8,16,128]{3,2,1,0:T(8,128)} %sd_in.3) | copy-start | bytes 589828
  11.4 5.5 %collective-permute-start.7 = (f32[36,8,128]{2,1,0:T(8,128)S(1)}, f32[36,8,128]{2,1,0:T(8,128)S(1)}, u32[]{:S(2)}, u32[]{:S(2)}) collective-permute-start(f32[36,8,128]{2,1,0:T(8,128)S(1)} %pad_maximum_fusion), channel_id=1, source_target_pairs={{0,2},{2,0},{1,3},{3,1},{4,6},{6,4},{5,7},{7,5},{8,10},{10,8},{9,1... | collective-permute-start | bytes 442376 | tf_op jit(solution)/shard_map/ppermute | solution.py:509
  11.5 8.6 %collective-permute-start.3 = (f32[10,24,128]{2,1,0:T(8,128)S(1)}, f32[10,24,128]{2,1,0:T(8,128)S(1)}, u32[]{:S(2)}, u32[]{:S(2)}) collective-permute-start(f32[10,24,128]{2,1,0:T(8,128)S(1)} %get-tuple-element.22.a_sent), channel_id=1, source_target_pairs={{0,4},{4,0},{8,12},{12,8},{16,20},{20,16},{24,28},{28,24},{1,5},{5... | collective-permute-start | bytes 368648 | tf_op jit(solution)/shard_map/ppermute | solution.py:556
  16.2 3.9 %collective-permute-start.4 = (f32[10,24,128]{2,1,0:T(8,128)S(1)}, f32[10,24,128]{2,1,0:T(8,128)S(1)}, u32[]{:S(2)}, u32[]{:S(2)}) collective-permute-start(f32[10,24,128]{2,1,0:T(8,128)S(1)} %get-tuple-element.23.b_sent), channel_id=1, source_target_pairs={{4,8},{8,4},{12,16},{16,12},{20,24},{24,20},{5,9},{9,5},{13,17},{1... | collective-permute-start | bytes 368648 | tf_op jit(solution)/shard_map/ppermute | solution.py:557
  16.9 3.2 %copy-start.4 = (s32[8,16,128]{2,1,0:T(8,128)S(1)}, s32[8,16,128]{2,1,0:T(8,128)}, u32[]{:S(2)}) copy-start(s32[8,16,128]{2,1,0:T(8,128)} %ids.1) | copy-start | bytes 196612
  22.0 6.2 %collective-permute-start.8 = (f32[8,128]{1,0:T(8,128)S(1)}, f32[8,128]{1,0:T(8,128)S(1)}, u32[]{:S(2)}, u32[]{:S(2)}) collective-permute-start(f32[8,128]{1,0:T(8,128)S(1)} %get-tuple-element.37), channel_id=1, source_target_pairs={{0,4},{4,0},{8,12},{12,8},{16,20},{20,16},{24,28},{28,24},{1,5},{5... | collective-permute-start | bytes 12296 | tf_op jit(solution)/shard_map/ppermute | solution.py:583

commit v5 on v4

--- a/solution.py
+++ b/solution.py
@@ -90,6 +90,12 @@
         j = self.lane % 16
         got = pltpu.roll(got, (self.got_j - 4 * (q % 4) + 128) % 128, 1)
         return jnp.where((j >= self.got_j) & (j < self.got_j + EDGE), got, tile)
+
+    def with_seam(self, plane, strip, x):
+        lane = lanes_of((16, 128))
+        lo = jnp.where(self.gz == 0, 128 - EDGE, 0)
+        moved = pltpu.roll(strip, (lo - 16 * x - EDGE + 256) % 128, 1)
+        return jnp.where((lane >= lo) & (lane < lo + EDGE), moved, plane)
 
     def z_up(self, v):
         return jnp.where(self.lane == 127, 0.0, roll_up(v, 1))
@@ -338,8 +344,8 @@
 HIGH_E = ([-1, 0], [-2, -1, 0, 1], [-3, -2, -1, 0], [-4, -3, -2, -1])
 
 
-def driven_kernel(sd_in, a_sent, b_sent, a_in, b_in, e_own, sc_own, se_own, i_in, s_in, p_in, g_own, ids,
-                  e_out, s_out, E, H, G):
+def driven_kernel(sd_in, a_sent, b_sent, high_in, low_in, e_own, sc_own, se_own, i_in, s_in, p_in, g_own, ids,
+                  e_out, se_out, s_out, E, H, G):
     at = Place()
     cx = e_own.shape[1]
     lane = at.lane
@@ -355,10 +361,10 @@
         return jnp.where(at.even, a[i], b[i])
 
     def upper(i):
-        return traces(a_in, b_in, i)
+        return high_in[i]
 
     def lower(i):
-        return traces(b_in, a_in, i)
+        return low_in[i]
 
     def own_up(i):
         return traces(a_sent, b_sent, i)
@@ -441,22 +447,16 @@
             g + adjoint[n][c][:, 0:128] * (curl[c][:, 0:128] + sc_own[n, c]) for c, g in enumerate(sg)
         )
 
-    lane16 = lanes_of((16, 128))
-    seam_lo = jnp.where(at.gz == 0, 128 - EDGE, 0)
-    seam = (lane16 >= seam_lo) & (lane16 < seam_lo + EDGE)
-    s_elec = [(se[c][0:16, 0:128] + se_own[c, 0:16]) for c in range(3)]
+    for c in range(3):
+        se_out[c] = se[c][0:16, 0:128] + se_own[c, 0:16]
+        e_out[c] = E[c, base : base + cx, 0:16] + e_own[c]
     s_grad = [sg[c][0:16] for c in range(3)]
-
-    def with_seam(plane, strip, x):
-        moved = pltpu.roll(strip, (seam_lo - 16 * x - EDGE + 256) % 128, 1)
-        return jnp.where(seam, moved, plane)
 
     acc = jnp.zeros((80, 128), F32)
     for x in range(cx):
         grads = []
         for c in range(3):
-            e_out[c, x] = with_seam(E[c, base + x, 0:16] + e_own[c, x], s_elec[c], x)
-            grads.append(with_seam(G[c, x], s_grad[c], x))
+            grads.append(at.with_seam(G[c, x], s_grad[c], x))
         lhs, rhs = [], []
         for r in range(2):
             g = jnp.concatenate([v[8 * r : 8 * r + 8] for v in grads], axis=0)
@@ -487,6 +487,20 @@
     s_out[...] = jnp.dot(parts, fold, precision=lax.Precision.HIGHEST, preferred_element_type=F32)
 
 
+def last_kernel(ip_in, sd_in, a_got, b_got, z_in, y1, yz, y2, c_own, a_sent, b_sent, a_in, b_in, e_own, sc_own, se_own, ids,
+                e_out, se_out, s_out, I, W, M, PS, E, H, G, i_ext, s_ext, p_own, g_own):
+    adjoint_kernel(ip_in, sd_in, a_got, b_got, z_in, y1, yz, y2, c_own, i_ext, s_ext, p_own, g_own, I, W, M, PS)
+    driven_kernel(sd_in, a_sent, b_sent, a_in, b_in, e_own, sc_own, se_own, i_ext, s_ext, p_own, g_own, ids,
+                  e_out, se_out, s_out, E, H, G)
+
+
+def finish_kernel(e_in, se_in, e_out):
+    at = Place()
+    for c in range(3):
+        for x in range(e_in.shape[1]):
+            e_out[c, x] = at.with_seam(e_in[c, x], se_in[c], x)
+
+
 def y_rows(v):
     first = lax.broadcasted_iota(jnp.int32, (1, 8, 1), 1) < EDGE
     return jnp.where(first, v[:, 0:8], v[:, 8:16])
@@ -512,13 +526,14 @@
         first = lax.broadcasted_iota(jnp.int32, (1, 8, 1), 1) < EDGE
         return jnp.where(first, down, up)
 
-    def call(kernel, outs, scratch, args, mib, specs=None):
+    def call(kernel, outs, scratch, args, mib, specs=None, cost=None):
         return pl.pallas_call(
             kernel,
             out_shape=outs,
             in_specs=specs or [vmem] * len(args),
             out_specs=(vmem,) * len(outs),
             scratch_shapes=scratch,
+            cost_estimate=cost,
             compiler_params=pltpu.CompilerParams(vmem_limit_bytes=mib * 1024 * 1024),
         )(*args)
 
@@ -556,30 +571,24 @@
     a_in = lax.ppermute(a_sent, "gx", a_pairs)
     b_in = lax.ppermute(b_sent, "gx", b_pairs)
     a_got, b_got, _ = lax.optimization_barrier((a_got, b_got, a_sent))
+    high_in = jnp.where(even == 1, a_in, b_in)
+    low_in = jnp.where(even == 1, b_in, a_in)
     y2 = swap_y(jnp.concatenate([y_rows(v) for v in (a_got, b_got)], axis=0))
 
     planes = cx + 2 * DEEP + 1
     field = tile(3, planes, 24, 128)
-    i_ext, s_ext, p_own, g_own = call(
-        adjoint_kernel,
-        (
-            shape(3, cx + 4, 24, 128),
-            shape(6, 24, 256),
-            shape(STEPS - 1, 3, cx, 16, 128),
-            shape(3, cx, 16, 128),
-        ),
-        [field] * 3 + [tile(STEPS, 3, planes, 24, 128)],
-        (inv_perm, adj_seed, a_got, b_got, z_got, y1, yz, y2, c_own),
-        12,
-    )
-    field = tile(3, cx + 5, 24, 128)
-    e_field, sums = call(
-        driven_kernel,
-        (shape(*e_start.shape), shape(8, 128)),
-        [field] * 2 + [own],
-        (adj_seed, a_sent, b_sent, a_in, b_in, e_own, sc_own, se_own, i_ext, s_ext, p_own, g_own, region_ids),
-        8,
-    )
+    driven = tile(3, cx + 5, 24, 128)
+    e_main, e_strip, sums = call(
+        last_kernel,
+        (shape(*e_start.shape), shape(3, 16, 128), shape(8, 128)),
+        [field] * 3
+        + [tile(STEPS, 3, planes, 24, 128)]
+        + [driven] * 2
+        + [own, tile(3, cx + 4, 24, 128), tile(6, 24, 256), tile(STEPS - 1, 3, cx, 16, 128), own],
+        (inv_perm, adj_seed, a_got, b_got, z_got, y1, yz, y2, c_own, a_sent, b_sent, high_in, low_in, e_own, sc_own, se_own, region_ids),
+        16,
+    )
+    (e_field,) = call(finish_kernel, (shape(*e_start.shape),), [], (e_main, e_strip), 4)
     total = sums + lax.ppermute(sums, "gx", a_pairs)
     owned = jnp.where(even == 1, total[0:3, 0:REG_DEV], total[0:3, REG_DEV : 2 * REG_DEV])
     return e_field, owned

time: 29.3 us -> 28.5 us (0.973)
  waiting for transfers between devices: 6.35 us -> 4.7 us
  starting transfers between devices: 15.4 us -> 16.1 us
    ppermute x1, waiting for transfers between devices: 1.38 us -> 0.01 us  [local(): a_got = lax.ppermute(a_msg, 'gx', a_pairs)]
    ppermute x1, starting transfers between devices: 4.66 us -> 5.74 us  [local(): total = sums + lax.ppermute(sums, 'gx', a_pairs)]
    ppermute x1, waiting for transfers between devices: 1.58 us -> 0.78 us  [local(): total = sums + lax.ppermute(sums, 'gx', a_pairs)]
    ppermute x1, waiting for transfers between devices: 2.21 us -> 2.75 us  [local(): a_in = lax.ppermute(a_sent, 'gx', a_pairs)]
    ppermute x1, starting transfers between devices: 4.72 us -> 4.34 us  [local(): a_in = lax.ppermute(a_sent, 'gx', a_pairs)]
  transfers between devices with their start and end apart: 9 -> 9, of which waited for: 4 -> 3; matrix products, arithmetic and copies ran while one was open for 0% -> 1% of each run, Pallas kernels for 7% -> 7%
where the time goes in v5:
time: 28.5 us; the launch traced here: 28.3 us
  starting transfers between devices  16.1 us (56%)
  Pallas kernels  5.86 us (21%)
  waiting for transfers between devices  4.7 us (16%)
  other arithmetic  0.85 us (3%)
  between operations  0.81 us (3%)
    pallas_call x4, Pallas kernels, call(): pl.pallas_call(kernel, out_shape=outs, in_specs=specs or [vmem] * len(arg...  5.86 us
    ppermute x1, starting transfers between devices, local(): total = sums + lax.ppermute(sums, 'gx', a_pairs)  5.74 us
    ppermute x1, starting transfers between devices, local(): a_in = lax.ppermute(a_sent, 'gx', a_pairs)  4.34 us
    ppermute x1, waiting for transfers between devices, local(): a_in = lax.ppermute(a_sent, 'gx', a_pairs)  2.75 us
    ppermute x1, starting transfers between devices, local(): z_got = lax.ppermute(z_msg, 'gz', [(0, 1), (1, 0)])  2.59 us
    ppermute x1, starting transfers between devices, local(): a_got = lax.ppermute(a_msg, 'gx', a_pairs)  1.49 us
    ppermute x3, waiting for transfers between devices, swap_y(): return lax.ppermute(v, 'gy', [(0, 1), (1, 0)])  1.16 us
    ppermute x1, waiting for transfers between devices, local(): total = sums + lax.ppermute(sums, 'gx', a_pairs)  0.78 us
  transfers between devices with their start and end apart: 9, of which 3 were waited for; matrix products, arithmetic and copies ran while one was open for 1% of the time, Pallas kernels for 7%

profile of v5, /device:TPU:0, one launch (start us, length us, event | category | flops | bytes accessed | tf_op | source)
XLA Modules:
  0.0 28.3 jit_solution(15856654773293752740)
XLA Ops:
  0.7 1.6 %shard_map.68 = (f32[18,16,128]{2,1,0:T(8,128)S(1)}, f32[18,16,128]{2,1,0:T(8,128)S(1)}, f32[3,16,128]{2,1,0:T(8,128)S(1)}, f32[96,8,128]{2,1,0:T(8,128)S(1)}) custom-call(f32[3,8,16,128]{3,2,1,0:T(8,128)} %ip_in.3, f32[3,8,16,128]{3,2,1,0:T(8,128)} %sd_in.1, f32[3,8,16,128]{3,2,1,0:T(8,128)} %e_in.1, f32[3,8,16,128]{3,2,1,0:T(8,128)} %h_in.1), custom_call_target="tpu_custom_call" | custom-call | tf_op jit(solution)/shard_map/pallas_call | solution.py:530
  2.3 0.5 %collective-permute-start.2 = (f32[96,8,128]{2,1,0:T(8,128)S(1)}, f32[96,8,128]{2,1,0:T(8,128)S(1)}, u32[]{:S(2)}, u32[]{:S(2)}) collective-permute-start(f32[96,8,128]{2,1,0:T(8,128)S(1)} %get-tuple-element.19), channel_id=1, source_target_pairs={{0,2},{2,0},{1,3},{3,1},{4,6},{6,4},{5,7},{7,5},{8,10},{10,8},{9,1... | collective-permute-start | bytes 1179656 | tf_op jit(solution)/shard_map/ppermute | solution.py:523
  2.8 2.6 %collective-permute-start.3 = (f32[3,16,128]{2,1,0:T(8,128)S(1)}, f32[3,16,128]{2,1,0:T(8,128)S(1)}, u32[]{:S(2)}, u32[]{:S(2)}) collective-permute-start(f32[3,16,128]{2,1,0:T(8,128)S(1)} %get-tuple-element.20), channel_id=1, source_target_pairs={{0,1},{1,0},{2,3},{3,2},{4,5},{5,4},{6,7},{7,6},{8,9},{9,8},{10,11... | collective-permute-start | bytes 73736 | tf_op jit(solution)/shard_map/ppermute | solution.py:549
  5.4 1.5 %collective-permute-start = (f32[18,16,128]{2,1,0:T(8,128)S(1)}, f32[18,16,128]{2,1,0:T(8,128)S(1)}, u32[]{:S(2)}, u32[]{:S(2)}) collective-permute-start(f32[18,16,128]{2,1,0:T(8,128)S(1)} %get-tuple-element.17), channel_id=1, source_target_pairs={{0,4},{4,0},{8,12},{12,8},{16,20},{20,16},{24,28},{28,24},{1,5},{5... | collective-permute-start | bytes 442376 | tf_op jit(solution)/shard_map/ppermute | solution.py:551
  6.9 0.7 %collective-permute-start.1 = (f32[18,16,128]{2,1,0:T(8,128)S(1)}, f32[18,16,128]{2,1,0:T(8,128)S(1)}, u32[]{:S(2)}, u32[]{:S(2)}) collective-permute-start(f32[18,16,128]{2,1,0:T(8,128)S(1)} %get-tuple-element.18), channel_id=1, source_target_pairs={{4,8},{8,4},{12,16},{16,12},{20,24},{24,20},{5,9},{9,5},{13,17},{1... | collective-permute-start | bytes 442376 | tf_op jit(solution)/shard_map/ppermute | solution.py:552
  7.6 0.1 slice_select_fusion.2
  7.6 0.0 collective-permute-start.4
  7.7 1.2 %collective-permute-done.4.yz = f32[3,8,128]{2,1,0:T(8,128)S(1)} collective-permute-done((f32[3,8,128]{2,1,0:T(8,128)S(1)}, f32[3,8,128]{2,1,0:T(8,128)S(1)}, u32[]{:S(2)}, u32[]{:S(2)}) %collective-permute-start.4) | collective-permute-done | bytes 12320 | tf_op jit(solution)/shard_map/ppermute | solution.py:523
  8.8 1.1 %shard_map.69 = (f32[10,24,128]{2,1,0:T(8,128)S(1)}, f32[10,24,128]{2,1,0:T(8,128)S(1)}, f32[4,3,8,16,128]{4,3,2,1,0:T(8,128)S(1)}, f32[3,8,16,128]{3,2,1,0:T(8,...) custom-call(f32[3,8,16,128]{3,2,1,0:T(8,128)S(1)} %copy-done, f32[3,8,16,128]{3,2,1,0:T(8,128)S(1)} %copy-done.2, ...), custom_call_target="tpu_custom_call" | custom-call | tf_op jit(solution)/shard_map/pallas_call | solution.py:530
  9.9 4.3 %collective-permute-start.6 = (f32[10,24,128]{2,1,0:T(8,128)S(1)}, f32[10,24,128]{2,1,0:T(8,128)S(1)}, u32[]{:S(2)}, u32[]{:S(2)}) collective-permute-start(f32[10,24,128]{2,1,0:T(8,128)S(1)} %get-tuple-element.21.a_sent), channel_id=1, source_target_pairs={{0,4},{4,0},{8,12},{12,8},{16,20},{20,16},{24,28},{28,24},{1,5},{5... | collective-permute-start | bytes 368648 | tf_op jit(solution)/shard_map/ppermute | solution.py:571
  14.3 0.0 collective-permute-done.a_got
  14.3 0.0 collective-permute-done.1.b_got
  14.3 0.7 %collective-permute-start.7 = (f32[10,24,128]{2,1,0:T(8,128)S(1)}, f32[10,24,128]{2,1,0:T(8,128)S(1)}, u32[]{:S(2)}, u32[]{:S(2)}) collective-permute-start(f32[10,24,128]{2,1,0:T(8,128)S(1)} %get-tuple-element.25.b_sent), channel_id=1, source_target_pairs={{4,8},{8,4},{12,16},{16,12},{20,24},{24,20},{5,9},{9,5},{13,17},{1... | collective-permute-start | bytes 368648 | tf_op jit(solution)/shard_map/ppermute | solution.py:572
  14.9 0.1 slice_select_fusion.1
  15.0 0.0 copy-start.1
  15.0 0.0 copy-start.4
  15.1 0.1 collective-permute-start.5
  15.1 0.0 collective-permute-done.7
  15.1 2.8 %collective-permute-done.6 = f32[10,24,128]{2,1,0:T(8,128)S(1)} collective-permute-done((f32[10,24,128]{2,1,0:T(8,128)S(1)}, f32[10,24,128]{2,1,0:T(8,128)S(1)}, u32[]{:S(2)}, u32[]{:S(2)}) %collective-permute-start.6) | collective-permute-done | bytes 122912 | tf_op jit(solution)/shard_map/ppermute | solution.py:571
  18.0 2.4 %shard_map.70 = (f32[3,8,16,128]{3,2,1,0:T(8,128)S(1)}, f32[3,16,128]{2,1,0:T(8,128)S(1)}, f32[8,128]{1,0:T(8,128)S(1)}) custom-call(f32[3,8,16,128]{3,2,1,0:T(8,128)S(1)} %copy-done, f32[3,8,16,128]{3,2,1,0:T(8,128)S(1)} %copy-done.1, f32[18,16,128]{2,1,0:T(8,128)S(1)} %collective-permute-done.a_got, f32[18,16,128]{2,1,0:T(8,128)S(1)} %collective-permute-done.1.b_got, ...), custom_call_target="tpu_custom_call" | custom-call | tf_op jit(solution)/shard_map/pallas_call | solution.py:530
  20.4 5.7 %collective-permute-start.8 = (f32[8,128]{1,0:T(8,128)S(1)}, f32[8,128]{1,0:T(8,128)S(1)}, u32[]{:S(2)}, u32[]{:S(2)}) collective-permute-start(f32[8,128]{1,0:T(8,128)S(1)} %get-tuple-element.31), channel_id=1, source_target_pairs={{0,4},{4,0},{8,12},{12,8},{16,20},{20,16},{24,28},{28,24},{1,5},{5... | collective-permute-start | bytes 12296 | tf_op jit(solution)/shard_map/ppermute | solution.py:592
  26.1 0.8 %shard_map.71 = f32[3,8,16,128]{3,2,1,0:T(8,128)} custom-call(f32[3,8,16,128]{3,2,1,0:T(8,128)S(1)} %get-tuple-element.29.e_in, f32[3,16,128]{2,1,0:T(8,128)S(1)} %get-tuple-element.30.se_in), custom_call_target="tpu_custom_call" | custom-call | tf_op jit(solution)/shard_map/pallas_call | solution.py:530
  26.9 0.8 %collective-permute-done.8 = f32[8,128]{1,0:T(8,128)S(1)} collective-permute-done((f32[8,128]{1,0:T(8,128)S(1)}, f32[8,128]{1,0:T(8,128)S(1)}, u32[]{:S(2)}, u32[]{:S(2)}) %collective-permute-start.8) | collective-permute-done | bytes 4128 | tf_op jit(solution)/shard_map/ppermute | solution.py:592
  27.7 0.7 %slice_select_fusion.3 = f32[3,8]{1,0:T(4,128)} fusion(f32[8,128]{1,0:T(8,128)S(1)} %add.12, pred[]{:T(512)S(6)} %eq.4), kind=kLoop, calls=%fused_computation.6 | loop fusion | flops 24 | bytes 289 | tf_op jit(solution)/shard_map/jit(_where)/select_n | solution.py:593
  (15 shorter events, 0.1 us)
Async XLA Ops:
  0.6 8.2 %copy-start = (f32[3,8,16,128]{3,2,1,0:T(8,128)S(1)}, f32[3,8,16,128]{3,2,1,0:T(8,128)}, u32[]{:S(2)}) copy-start(f32[3,8,16,128]{3,2,1,0:T(8,128)} %ip_in.3) | copy-start | bytes 589828
  0.6 8.2 %copy-start.2 = (f32[3,8,16,128]{3,2,1,0:T(8,128)S(1)}, f32[3,8,16,128]{3,2,1,0:T(8,128)}, u32[]{:S(2)}) copy-start(f32[3,8,16,128]{3,2,1,0:T(8,128)} %e_in.1) | copy-start | bytes 589828
  0.7 8.2 %copy-start.3 = (f32[3,8,16,128]{3,2,1,0:T(8,128)S(1)}, f32[3,8,16,128]{3,2,1,0:T(8,128)}, u32[]{:S(2)}) copy-start(f32[3,8,16,128]{3,2,1,0:T(8,128)} %h_in.1) | copy-start | bytes 589828
  2.3 6.6 %collective-permute-start.2 = (f32[96,8,128]{2,1,0:T(8,128)S(1)}, f32[96,8,128]{2,1,0:T(8,128)S(1)}, u32[]{:S(2)}, u32[]{:S(2)}) collective-permute-start(f32[96,8,128]{2,1,0:T(8,128)S(1)} %get-tuple-element.19), channel_id=1, source_target_pairs={{0,2},{2,0},{1,3},{3,1},{4,6},{6,4},{5,7},{7,5},{8,10},{10,8},{9,1... | collective-permute-start | bytes 1179656 | tf_op jit(solution)/shard_map/ppermute | solution.py:523
  2.8 4.8 %collective-permute-start.3 = (f32[3,16,128]{2,1,0:T(8,128)S(1)}, f32[3,16,128]{2,1,0:T(8,128)S(1)}, u32[]{:S(2)}, u32[]{:S(2)}) collective-permute-start(f32[3,16,128]{2,1,0:T(8,128)S(1)} %get-tuple-element.20), channel_id=1, source_target_pairs={{0,1},{1,0},{2,3},{3,2},{4,5},{5,4},{6,7},{7,6},{8,9},{9,8},{10,11... | collective-permute-start | bytes 73736 | tf_op jit(solution)/shard_map/ppermute | solution.py:549
  5.4 8.9 %collective-permute-start = (f32[18,16,128]{2,1,0:T(8,128)S(1)}, f32[18,16,128]{2,1,0:T(8,128)S(1)}, u32[]{:S(2)}, u32[]{:S(2)}) collective-permute-start(f32[18,16,128]{2,1,0:T(8,128)S(1)} %get-tuple-element.17), channel_id=1, source_target_pairs={{0,4},{4,0},{8,12},{12,8},{16,20},{20,16},{24,28},{28,24},{1,5},{5... | collective-permute-start | bytes 442376 | tf_op jit(solution)/shard_map/ppermute | solution.py:551
  6.9 7.4 %collective-permute-start.1 = (f32[18,16,128]{2,1,0:T(8,128)S(1)}, f32[18,16,128]{2,1,0:T(8,128)S(1)}, u32[]{:S(2)}, u32[]{:S(2)}) collective-permute-start(f32[18,16,128]{2,1,0:T(8,128)S(1)} %get-tuple-element.18), channel_id=1, source_target_pairs={{4,8},{8,4},{12,16},{16,12},{20,24},{24,20},{5,9},{9,5},{13,17},{1... | collective-permute-start | bytes 442376 | tf_op jit(solution)/shard_map/ppermute | solution.py:552
  7.6 1.2 %collective-permute-start.4 = (f32[3,8,128]{2,1,0:T(8,128)S(1)}, f32[3,8,128]{2,1,0:T(8,128)S(1)}, u32[]{:S(2)}, u32[]{:S(2)}) collective-permute-start(f32[3,8,128]{2,1,0:T(8,128)S(1)} %slice_select_fusion.2), channel_id=1, source_target_pairs={{0,2},{2,0},{1,3},{3,1},{4,6},{6,4},{5,7},{7,5},{8,10},{10,8},{9,1... | collective-permute-start | bytes 36872 | tf_op jit(solution)/shard_map/ppermute | solution.py:523
  9.9 8.0 %collective-permute-start.6 = (f32[10,24,128]{2,1,0:T(8,128)S(1)}, f32[10,24,128]{2,1,0:T(8,128)S(1)}, u32[]{:S(2)}, u32[]{:S(2)}) collective-permute-start(f32[10,24,128]{2,1,0:T(8,128)S(1)} %get-tuple-element.21.a_sent), channel_id=1, source_target_pairs={{0,4},{4,0},{8,12},{12,8},{16,20},{20,16},{24,28},{28,24},{1,5},{5... | collective-permute-start | bytes 368648 | tf_op jit(solution)/shard_map/ppermute | solution.py:571
  14.3 0.9 %collective-permute-start.7 = (f32[10,24,128]{2,1,0:T(8,128)S(1)}, f32[10,24,128]{2,1,0:T(8,128)S(1)}, u32[]{:S(2)}, u32[]{:S(2)}) collective-permute-start(f32[10,24,128]{2,1,0:T(8,128)S(1)} %get-tuple-element.25.b_sent), channel_id=1, source_target_pairs={{4,8},{8,4},{12,16},{16,12},{20,24},{24,20},{5,9},{9,5},{13,17},{1... | collective-permute-start | bytes 368648 | tf_op jit(solution)/shard_map/ppermute | solution.py:572
  15.0 2.9 %copy-start.1 = (f32[3,8,16,128]{3,2,1,0:T(8,128)S(1)}, f32[3,8,16,128]{3,2,1,0:T(8,128)}, u32[]{:S(2)}) copy-start(f32[3,8,16,128]{3,2,1,0:T(8,128)} %sd_in.1) | copy-start | bytes 589828
  15.0 2.9 %copy-start.4 = (s32[8,16,128]{2,1,0:T(8,128)S(1)}, s32[8,16,128]{2,1,0:T(8,128)}, u32[]{:S(2)}) copy-start(s32[8,16,128]{2,1,0:T(8,128)} %ids.1) | copy-start | bytes 196612
  15.1 2.9 %collective-permute-start.5 = (f32[36,8,128]{2,1,0:T(8,128)S(1)}, f32[36,8,128]{2,1,0:T(8,128)S(1)}, u32[]{:S(2)}, u32[]{:S(2)}) collective-permute-start(f32[36,8,128]{2,1,0:T(8,128)S(1)} %pad_maximum_fusion), channel_id=1, source_target_pairs={{0,2},{2,0},{1,3},{3,1},{4,6},{6,4},{5,7},{7,5},{8,10},{10,8},{9,1... | collective-permute-start | bytes 442376 | tf_op jit(solution)/shard_map/ppermute | solution.py:523
  20.4 7.3 %collective-permute-start.8 = (f32[8,128]{1,0:T(8,128)S(1)}, f32[8,128]{1,0:T(8,128)S(1)}, u32[]{:S(2)}, u32[]{:S(2)}) collective-permute-start(f32[8,128]{1,0:T(8,128)S(1)} %get-tuple-element.31), channel_id=1, source_target_pairs={{0,4},{4,0},{8,12},{12,8},{16,20},{20,16},{24,28},{28,24},{1,5},{5... | collective-permute-start | bytes 12296 | tf_op jit(solution)/shard_map/ppermute | solution.py:592

commit v6 on v5

--- a/solution.py
+++ b/solution.py
@@ -12,6 +12,7 @@
 PERM, SEED, ELEC, MAGN = range(4)
 N_SLOTS = 2 * 3 * DEEP
 N_TRACES = 2 * STEPS
+GROUP = 2
 
 time_step = 0.5
 grad_scale = 1.0 / 64.0
@@ -120,6 +121,10 @@
     return roll_down(v, 1)
 
 
+def parts_of(xs):
+    return [xs[i : i + GROUP] for i in range(0, len(xs), GROUP)]
+
+
 def get(ref, x, comps=(0, 1, 2)):
     return tuple(ref[c, x] for c in comps)
 
@@ -208,25 +213,27 @@
     up_strip, down_strip = zero, zero
     for n in range(STEPS):
         downs = get(E, 1, (1, 2))
-        new = []
-        for x in xs:
-            curl = curl_f(get(E, x), get(E, x + 1, (1, 2)), y_up, at.z_up)
-            keep = time_step * at.keep_row
-            new.append(tuple(q - keep * v for q, v in zip(get(H, x), curl)))
-        put(H, xs, new)
+        keep = time_step * at.keep_row
+        for part in parts_of(xs):
+            new = []
+            for x in part:
+                curl = curl_f(get(E, x), get(E, x + 1, (1, 2)), y_up, at.z_up)
+                new.append(tuple(q - keep * v for q, v in zip(get(H, x), curl)))
+            put(H, part, new)
         curl = curl_f(se, (sx_up(se[1]), sx_up(se[2])), y_up, sz_up)
         down_from = se
         sh = tuple(q - time_step * at.keep_row * v for q, v in zip(sh, curl))
         ups = get(H, cx, (1, 2))
-        new, curls = [], []
-        for x in xs:
-            curl = curl_b(get(H, x), get(H, x - 1, (1, 2)), y_down, at.z_down)
-            new.append(tuple(q + i * v for q, i, v in zip(get(E, x), get(I, x), curl)))
-            curls.append(curl)
-        put(E, xs, new)
-        for x, curl in zip(xs, curls):
-            for c in range(3):
-                c_out[n, c, x - 1] = curl[c][0:16]
+        for part in parts_of(xs):
+            new, curls = [], []
+            for x in part:
+                curl = curl_b(get(H, x), get(H, x - 1, (1, 2)), y_down, at.z_down)
+                new.append(tuple(q + i * v for q, i, v in zip(get(E, x), get(I, x), curl)))
+                curls.append(curl)
+            put(E, part, new)
+            for x, curl in zip(part, curls):
+                for c in range(3):
+                    c_out[n, c, x - 1] = curl[c][0:16]
         curl = curl_b(sh, (sx_down(sh[1]), sx_down(sh[2])), y_down, sz_down)
         se = tuple(q + i * v for q, i, v in zip(se, si, curl))
         for c in range(3):
@@ -250,8 +257,8 @@
     sput(se_out, se)
 
 
-def adjoint_kernel(ip_in, sd_in, a_in, b_in, z_in, y1, yz, y2, c_own,
-                   i_out, s_out, p_out, g_out, I, W, M, PS):
+def adjoint_kernel(ip_in, sd_in, a_in, b_in, z_in, y1, yz, y2,
+                   s_out, I, W, M, PS):
     at = Place()
     cx = ip_in.shape[1]
     lane = at.lane
@@ -284,8 +291,8 @@
         return at.keep_row * jnp.where(at.no_low_x, 0.0, 1.0) if x < DEEP else at.keep_row
 
     def sweep(lo, hi, body):
-        for first in range(lo, hi, 8):
-            body(list(range(first, min(first + 8, hi))))
+        for first in range(lo, hi, GROUP):
+            body(list(range(first, min(first + GROUP, hi))))
 
     def halve(xs):
         new = []
@@ -298,7 +305,6 @@
     sweep(0, last, halve)
     for c in range(3):
         W[c, last] = jnp.zeros((24, 128), F32)
-        i_out[c] = I[c, 1 : 1 + i_out.shape[1]]
 
     for m in range(STEPS - 1):
         n = top - m
@@ -324,18 +330,10 @@
             if m < STEPS - 2:
                 put(W, xs, [v[1] for v in new])
 
+        yield
         sweep(m, last - 1 - m, magnetic)
+        yield
         sweep(m + 1, last - 1 - m, electric)
-
-    for c in range(3):
-        for x in range(cx):
-            g = jnp.zeros((16, 128), F32)
-            for n in range(STEPS):
-                p = PS[n, c, DEEP + x, 0:16]
-                g = g + p * c_own[n, c, x]
-                if n < top:
-                    p_out[n, c, x] = p
-            g_out[c, x] = g
 
 
 LOW_H = ([-1], [-2, -1, 0], [-2, -1, 0, 1], [-1, 0, 1, 2])
@@ -344,8 +342,7 @@
 HIGH_E = ([-1, 0], [-2, -1, 0, 1], [-3, -2, -1, 0], [-4, -3, -2, -1])
 
 
-def driven_kernel(sd_in, a_sent, b_sent, high_in, low_in, e_own, sc_own, se_own, i_in, s_in, p_in, g_own, ids,
-                  e_out, se_out, s_out, E, H, G):
+def driven_kernel(a_sent, b_sent, high_in, low_in, e_own, sc_own, se_own, s_in, I, e_out, se_out, sg_out, E, H, CD):
     at = Place()
     cx = e_own.shape[1]
     lane = at.lane
@@ -355,7 +352,6 @@
         for x in range(E.shape[1]):
             E[c, x] = zero
             H[c, x] = zero
-        G[c] = g_own[c]
 
     def traces(a, b, i):
         return jnp.where(at.even, a[i], b[i])
@@ -394,69 +390,80 @@
     sp = tuple(strips[3:6])
     adjoint = [None] * (STEPS - 1) + [sp]
     sm = (0.0, 0.0, 0.0)
-    for n in range(STEPS - 1, 0, -1):
-        sw = tuple(a * b for a, b in zip(si, sp))
-        curl = curl_f(sw, [pltpu.roll(v, 240, 1) for v in sw[1:]], y_up, sz_up)
-        sm = tuple(q + 2.0 * s_keep * v for q, v in zip(sm, curl))
-        curl = curl_b(sm, [pltpu.roll(v, 16, 1) for v in sm[1:]], y_down, sz_down)
-        sp = tuple(q - time_step * v for q, v in zip(sp, curl))
-        adjoint[n - 1] = sp
-
+    s_curls = []
     se = sh = (jnp.zeros(s_shape, F32),) * 3
-    sg = (0.0, 0.0, 0.0)
     for n in range(STEPS):
+        yield
         xs = LOW_H[n] + [cx + x for x in HIGH_H[n]]
-        new = []
-        for x in xs:
-            nxt = get(E, base + x + 1, (1, 2))
-            if x == -1:
-                nxt = tuple(v + own_down(2 * n + k) for k, v in enumerate(nxt))
-            if x == cx - 1:
-                nxt = tuple(v + upper(2 * n + k) for k, v in enumerate(nxt))
-            curl = curl_f(get(E, base + x), nxt, y_up, at.z_up)
-            keep = time_step * at.keep_row
-            if x < 0:
-                keep = keep * jnp.where(at.no_low_x, 0.0, 1.0)
-            new.append(tuple(q - keep * v for q, v in zip(get(H, base + x), curl)))
-        put(H, [base + x for x in xs], new)
+        for part in parts_of(xs):
+            new = []
+            for x in part:
+                nxt = get(E, base + x + 1, (1, 2))
+                if x == -1:
+                    nxt = tuple(v + own_down(2 * n + k) for k, v in enumerate(nxt))
+                if x == cx - 1:
+                    nxt = tuple(v + upper(2 * n + k) for k, v in enumerate(nxt))
+                curl = curl_f(get(E, base + x), nxt, y_up, at.z_up)
+                keep = time_step * at.keep_row
+                if x < 0:
+                    keep = keep * jnp.where(at.no_low_x, 0.0, 1.0)
+                new.append(tuple(q - keep * v for q, v in zip(get(H, base + x), curl)))
+            put(H, [base + x for x in part], new)
         nxt = tuple(pltpu.roll(se[1 + k], 240, 1) + source(s_upper, s_own_down, 2 * n + k, 7) for k in range(2))
         curl = curl_f(se, nxt, y_up, sz_up)
         sh = tuple(q - s_keep * v for q, v in zip(sh, curl))
-
+        if n < STEPS - 1:
+            sw = tuple(a * b for a, b in zip(si, sp))
+            curl = curl_f(sw, [pltpu.roll(v, 240, 1) for v in sw[1:]], y_up, sz_up)
+            sm = tuple(q + 2.0 * s_keep * v for q, v in zip(sm, curl))
+
+        yield
         xs = LOW_E[n] + [cx + x for x in HIGH_E[n]]
-        new, grads = [], []
-        for x in xs:
-            prv = get(H, base + x - 1, (1, 2))
-            if x == 0:
-                prv = tuple(v + lower(2 * n + k) for k, v in enumerate(prv))
-            if x == cx:
-                prv = tuple(v + own_up(2 * n + k) for k, v in enumerate(prv))
-            curl = curl_b(get(H, base + x), prv, y_down, at.z_down)
-            new.append(tuple(q + i * v for q, i, v in zip(get(E, base + x), get(i_in, 2 + x), curl)))
-            grads.append(curl)
-        put(E, [base + x for x in xs], new)
-        for x, curl in zip(xs, grads):
-            if 0 <= x < cx:
-                for c in range(3):
-                    p = sd_in[c, x] if n == STEPS - 1 else p_in[n, c, x]
-                    G[c, x] += p * curl[c][0:16]
+        for part in parts_of(xs):
+            new, grads = [], []
+            for x in part:
+                prv = get(H, base + x - 1, (1, 2))
+                if x == 0:
+                    prv = tuple(v + lower(2 * n + k) for k, v in enumerate(prv))
+                if x == cx:
+                    prv = tuple(v + own_up(2 * n + k) for k, v in enumerate(prv))
+                curl = curl_b(get(H, base + x), prv, y_down, at.z_down)
+                new.append(tuple(q + i * v for q, i, v in zip(get(E, base + x), get(I, DEEP + x), curl)))
+                grads.append(curl)
+            put(E, [base + x for x in part], new)
+            for x, curl in zip(part, grads):
+                if 0 <= x < cx:
+                    for c in range(3):
+                        CD[n, c, x] = curl[c][0:16]
         prv = tuple(pltpu.roll(sh[1 + k], 16, 1) + source(s_lower, s_own_up, 2 * n + k, 0) for k in range(2))
         curl = curl_b(sh, prv, y_down, sz_down)
         se = tuple(q + i * v for q, i, v in zip(se, si, curl))
-        sg = tuple(
-            g + adjoint[n][c][:, 0:128] * (curl[c][:, 0:128] + sc_own[n, c]) for c, g in enumerate(sg)
-        )
-
+        s_curls.append(tuple(v[:, 0:128] for v in curl))
+        if n < STEPS - 1:
+            curl = curl_b(sm, [pltpu.roll(v, 16, 1) for v in sm[1:]], y_down, sz_down)
+            sp = tuple(q - time_step * v for q, v in zip(sp, curl))
+            adjoint[STEPS - 2 - n] = sp
     for c in range(3):
         se_out[c] = se[c][0:16, 0:128] + se_own[c, 0:16]
         e_out[c] = E[c, base : base + cx, 0:16] + e_own[c]
-    s_grad = [sg[c][0:16] for c in range(3)]
-
+        sg_out[c] = sum(adjoint[n][c][0:16, 0:128] * (s_curls[n][c] + sc_own[n, c])[0:16] for n in range(STEPS))
+    yield
+
+
+def sums_kernel(PS, c_own, CD, sg, ids, s_out):
+    at = Place()
+    cx = ids.shape[0]
     acc = jnp.zeros((80, 128), F32)
     for x in range(cx):
         grads = []
         for c in range(3):
-            grads.append(at.with_seam(G[c, x], s_grad[c], x))
+            g = 0.0
+            for n in range(STEPS):
+                curl = c_own[n, c, x]
+                if x in LOW_E[n] or x - cx in HIGH_E[n]:
+                    curl = curl + CD[n, c, x]
+                g = g + PS[n, c, DEEP + x, 0:16] * curl
+            grads.append(at.with_seam(g, sg[c], x))
         lhs, rhs = [], []
         for r in range(2):
             g = jnp.concatenate([v[8 * r : 8 * r + 8] for v in grads], axis=0)
@@ -487,11 +494,16 @@
     s_out[...] = jnp.dot(parts, fold, precision=lax.Precision.HIGHEST, preferred_element_type=F32)
 
 
-def last_kernel(ip_in, sd_in, a_got, b_got, z_in, y1, yz, y2, c_own, a_sent, b_sent, a_in, b_in, e_own, sc_own, se_own, ids,
-                e_out, se_out, s_out, I, W, M, PS, E, H, G, i_ext, s_ext, p_own, g_own):
-    adjoint_kernel(ip_in, sd_in, a_got, b_got, z_in, y1, yz, y2, c_own, i_ext, s_ext, p_own, g_own, I, W, M, PS)
-    driven_kernel(sd_in, a_sent, b_sent, a_in, b_in, e_own, sc_own, se_own, i_ext, s_ext, p_own, g_own, ids,
-                  e_out, se_out, s_out, E, H, G)
+def last_kernel(ip_in, sd_in, a_got, b_got, z_in, y1, yz, y2, c_own, a_sent, b_sent, high_in, low_in, e_own, sc_own, se_own, ids,
+                e_out, se_out, s_out, I, W, M, PS, E, H, CD, s_ext, sg):
+    runs = (
+        adjoint_kernel(ip_in, sd_in, a_got, b_got, z_in, y1, yz, y2, s_ext, I, W, M, PS),
+        driven_kernel(a_sent, b_sent, high_in, low_in, e_own, sc_own, se_own, s_ext, I, e_out, se_out, sg, E, H, CD),
+    )
+    for _ in range(2 * STEPS + 1):
+        for run in runs:
+            next(run, None)
+    sums_kernel(PS, c_own, CD, sg, ids, s_out)
 
 
 def finish_kernel(e_in, se_in, e_out):
@@ -570,7 +582,6 @@
     )
     a_in = lax.ppermute(a_sent, "gx", a_pairs)
     b_in = lax.ppermute(b_sent, "gx", b_pairs)
-    a_got, b_got, _ = lax.optimization_barrier((a_got, b_got, a_sent))
     high_in = jnp.where(even == 1, a_in, b_in)
     low_in = jnp.where(even == 1, b_in, a_in)
     y2 = swap_y(jnp.concatenate([y_rows(v) for v in (a_got, b_got)], axis=0))
@@ -584,7 +595,7 @@
         [field] * 3
         + [tile(STEPS, 3, planes, 24, 128)]
         + [driven] * 2
-        + [own, tile(3, cx + 4, 24, 128), tile(6, 24, 256), tile(STEPS - 1, 3, cx, 16, 128), own],
+        + [tile(STEPS, 3, cx, 16, 128), tile(6, 24, 256), tile(3, 16, 128)],
         (inv_perm, adj_seed, a_got, b_got, z_got, y1, yz, y2, c_own, a_sent, b_sent, high_in, low_in, e_own, sc_own, se_own, region_ids),
         16,
     )

time: 28.5 us -> 27.6 us (0.968)
  starting transfers between devices: 16.1 us -> 15 us
    ppermute x1, starting transfers between devices: 5.74 us -> 4.66 us  [local(): total = sums + lax.ppermute(sums, 'gx', a_pairs)]
where the time goes in v6:
time: 27.6 us; the launch traced here: 27.2 us
  starting transfers between devices  15 us (54%)
  Pallas kernels  5.85 us (21%)
  waiting for transfers between devices  4.7 us (17%)
  other arithmetic  0.85 us (3%)
  between operations  0.82 us (3%)
    pallas_call x4, Pallas kernels, call(): pl.pallas_call(kernel, out_shape=outs, in_specs=specs or [vmem] * len(arg...  5.85 us
    ppermute x1, starting transfers between devices, local(): total = sums + lax.ppermute(sums, 'gx', a_pairs)  4.66 us
    ppermute x1, starting transfers between devices, local(): a_in = lax.ppermute(a_sent, 'gx', a_pairs)  4.34 us
    ppermute x1, waiting for transfers between devices, local(): a_in = lax.ppermute(a_sent, 'gx', a_pairs)  2.75 us
    ppermute x1, starting transfers between devices, local(): z_got = lax.ppermute(z_msg, 'gz', [(0, 1), (1, 0)])  2.59 us
    ppermute x1, starting transfers between devices, local(): a_got = lax.ppermute(a_msg, 'gx', a_pairs)  1.49 us
    ppermute x3, waiting for transfers between devices, swap_y(): return lax.ppermute(v, 'gy', [(0, 1), (1, 0)])  1.16 us
    ppermute x1, waiting for transfers between devices, local(): total = sums + lax.ppermute(sums, 'gx', a_pairs)  0.78 us
  transfers between devices with their start and end apart: 9, of which 3 were waited for; matrix products, arithmetic and copies ran while one was open for 1% of the time, Pallas kernels for 7%

profile of v6, /device:TPU:0, one launch (start us, length us, event | category | flops | bytes accessed | tf_op | source)
XLA Modules:
  0.0 27.2 jit_solution(13205174878861583373)
XLA Ops:
  0.7 1.6 %shard_map.68 = (f32[18,16,128]{2,1,0:T(8,128)S(1)}, f32[18,16,128]{2,1,0:T(8,128)S(1)}, f32[3,16,128]{2,1,0:T(8,128)S(1)}, f32[96,8,128]{2,1,0:T(8,128)S(1)}) custom-call(f32[3,8,16,128]{3,2,1,0:T(8,128)} %ip_in.3, f32[3,8,16,128]{3,2,1,0:T(8,128)} %sd_in.1, f32[3,8,16,128]{3,2,1,0:T(8,128)} %e_in.1, f32[3,8,16,128]{3,2,1,0:T(8,128)} %h_in.1), custom_call_target="tpu_custom_call" | custom-call | tf_op jit(solution)/shard_map/pallas_call | solution.py:542
  2.3 0.5 %collective-permute-start.3 = (f32[96,8,128]{2,1,0:T(8,128)S(1)}, f32[96,8,128]{2,1,0:T(8,128)S(1)}, u32[]{:S(2)}, u32[]{:S(2)}) collective-permute-start(f32[96,8,128]{2,1,0:T(8,128)S(1)} %get-tuple-element.18), channel_id=1, source_target_pairs={{0,2},{2,0},{1,3},{3,1},{4,6},{6,4},{5,7},{7,5},{8,10},{10,8},{9,1... | collective-permute-start | bytes 1179656 | tf_op jit(solution)/shard_map/ppermute | solution.py:535
  2.8 2.6 %collective-permute-start.2 = (f32[3,16,128]{2,1,0:T(8,128)S(1)}, f32[3,16,128]{2,1,0:T(8,128)S(1)}, u32[]{:S(2)}, u32[]{:S(2)}) collective-permute-start(f32[3,16,128]{2,1,0:T(8,128)S(1)} %get-tuple-element.17), channel_id=1, source_target_pairs={{0,1},{1,0},{2,3},{3,2},{4,5},{5,4},{6,7},{7,6},{8,9},{9,8},{10,11... | collective-permute-start | bytes 73736 | tf_op jit(solution)/shard_map/ppermute | solution.py:561
  5.4 1.5 %collective-permute-start = (f32[18,16,128]{2,1,0:T(8,128)S(1)}, f32[18,16,128]{2,1,0:T(8,128)S(1)}, u32[]{:S(2)}, u32[]{:S(2)}) collective-permute-start(f32[18,16,128]{2,1,0:T(8,128)S(1)} %get-tuple-element.15), channel_id=1, source_target_pairs={{0,4},{4,0},{8,12},{12,8},{16,20},{20,16},{24,28},{28,24},{1,5},{5... | collective-permute-start | bytes 442376 | tf_op jit(solution)/shard_map/ppermute | solution.py:563
  6.9 0.7 %collective-permute-start.1 = (f32[18,16,128]{2,1,0:T(8,128)S(1)}, f32[18,16,128]{2,1,0:T(8,128)S(1)}, u32[]{:S(2)}, u32[]{:S(2)}) collective-permute-start(f32[18,16,128]{2,1,0:T(8,128)S(1)} %get-tuple-element.16), channel_id=1, source_target_pairs={{4,8},{8,4},{12,16},{16,12},{20,24},{24,20},{5,9},{9,5},{13,17},{1... | collective-permute-start | bytes 442376 | tf_op jit(solution)/shard_map/ppermute | solution.py:564
  7.6 0.0 collective-permute-done.2.z_in
  7.6 0.1 slice_select_fusion.2
  7.6 0.0 collective-permute-start.4
  7.7 1.2 %collective-permute-done.4.yz = f32[3,8,128]{2,1,0:T(8,128)S(1)} collective-permute-done((f32[3,8,128]{2,1,0:T(8,128)S(1)}, f32[3,8,128]{2,1,0:T(8,128)S(1)}, u32[]{:S(2)}, u32[]{:S(2)}) %collective-permute-start.4) | collective-permute-done | bytes 12320 | tf_op jit(solution)/shard_map/ppermute | solution.py:535
  8.8 0.0 collective-permute-done.3.y1
  8.8 1.1 %shard_map.69 = (f32[10,24,128]{2,1,0:T(8,128)S(1)}, f32[10,24,128]{2,1,0:T(8,128)S(1)}, f32[4,3,8,16,128]{4,3,2,1,0:T(8,128)S(1)}, f32[3,8,16,128]{3,2,1,0:T(8,...) custom-call(f32[3,8,16,128]{3,2,1,0:T(8,128)S(1)} %copy-done, f32[3,8,16,128]{3,2,1,0:T(8,128)S(1)} %copy-done.2, ...), custom_call_target="tpu_custom_call" | custom-call | tf_op jit(solution)/shard_map/pallas_call | solution.py:542
  9.9 4.3 %collective-permute-start.6 = (f32[10,24,128]{2,1,0:T(8,128)S(1)}, f32[10,24,128]{2,1,0:T(8,128)S(1)}, u32[]{:S(2)}, u32[]{:S(2)}) collective-permute-start(f32[10,24,128]{2,1,0:T(8,128)S(1)} %get-tuple-element.20.a_sent), channel_id=1, source_target_pairs={{0,4},{4,0},{8,12},{12,8},{16,20},{20,16},{24,28},{28,24},{1,5},{5... | collective-permute-start | bytes 368648 | tf_op jit(solution)/shard_map/ppermute | solution.py:583
  14.3 0.7 %collective-permute-start.7 = (f32[10,24,128]{2,1,0:T(8,128)S(1)}, f32[10,24,128]{2,1,0:T(8,128)S(1)}, u32[]{:S(2)}, u32[]{:S(2)}) collective-permute-start(f32[10,24,128]{2,1,0:T(8,128)S(1)} %get-tuple-element.21.b_sent), channel_id=1, source_target_pairs={{4,8},{8,4},{12,16},{16,12},{20,24},{24,20},{5,9},{9,5},{13,17},{1... | collective-permute-start | bytes 368648 | tf_op jit(solution)/shard_map/ppermute | solution.py:584
  14.9 0.0 collective-permute-done.a_got
  14.9 0.1 slice_select_fusion.1
  15.0 0.0 copy-start.1
  15.1 0.0 copy-start.4
  15.1 0.1 collective-permute-start.5
  15.1 2.8 %collective-permute-done.6 = f32[10,24,128]{2,1,0:T(8,128)S(1)} collective-permute-done((f32[10,24,128]{2,1,0:T(8,128)S(1)}, f32[10,24,128]{2,1,0:T(8,128)S(1)}, u32[]{:S(2)}, u32[]{:S(2)}) %collective-permute-start.6) | collective-permute-done | bytes 122912 | tf_op jit(solution)/shard_map/ppermute | solution.py:583
  18.0 2.4 %shard_map.70 = (f32[3,8,16,128]{3,2,1,0:T(8,128)S(1)}, f32[3,16,128]{2,1,0:T(8,128)S(1)}, f32[8,128]{1,0:T(8,128)S(1)}) custom-call(f32[3,8,16,128]{3,2,1,0:T(8,128)S(1)} %copy-done, f32[3,8,16,128]{3,2,1,0:T(8,128)S(1)} %copy-done.1, f32[18,16,128]{2,1,0:T(8,128)S(1)} %collective-permute-done.a_got, f32[18,16,128]{2,1,0:T(8,128)S(1)} %collective-permute-done.1.b_got, ...), custom_call_target="tpu_custom_call" | custom-call | tf_op jit(solution)/shard_map/pallas_call | solution.py:542
  20.3 4.7 %collective-permute-start.8 = (f32[8,128]{1,0:T(8,128)S(1)}, f32[8,128]{1,0:T(8,128)S(1)}, u32[]{:S(2)}, u32[]{:S(2)}) collective-permute-start(f32[8,128]{1,0:T(8,128)S(1)} %get-tuple-element.27), channel_id=1, source_target_pairs={{0,4},{4,0},{8,12},{12,8},{16,20},{20,16},{24,28},{28,24},{1,5},{5... | collective-permute-start | bytes 12296 | tf_op jit(solution)/shard_map/ppermute | solution.py:603
  25.0 0.8 %shard_map.71 = f32[3,8,16,128]{3,2,1,0:T(8,128)} custom-call(f32[3,8,16,128]{3,2,1,0:T(8,128)S(1)} %get-tuple-element.25.e_in, f32[3,16,128]{2,1,0:T(8,128)S(1)} %get-tuple-element.26.se_in), custom_call_target="tpu_custom_call" | custom-call | tf_op jit(solution)/shard_map/pallas_call | solution.py:542
  25.8 0.8 %collective-permute-done.8 = f32[8,128]{1,0:T(8,128)S(1)} collective-permute-done((f32[8,128]{1,0:T(8,128)S(1)}, f32[8,128]{1,0:T(8,128)S(1)}, u32[]{:S(2)}, u32[]{:S(2)}) %collective-permute-start.8) | collective-permute-done | bytes 4128 | tf_op jit(solution)/shard_map/ppermute | solution.py:603
  26.6 0.7 %slice_select_fusion.3 = f32[3,8]{1,0:T(4,128)} fusion(f32[8,128]{1,0:T(8,128)S(1)} %add.12, pred[]{:T(512)S(6)} %eq.4), kind=kLoop, calls=%fused_computation.6 | loop fusion | flops 24 | bytes 289 | tf_op jit(solution)/shard_map/jit(_where)/select_n | solution.py:604
  (15 shorter events, 0.1 us)
Async XLA Ops:
  0.6 8.2 %copy-start = (f32[3,8,16,128]{3,2,1,0:T(8,128)S(1)}, f32[3,8,16,128]{3,2,1,0:T(8,128)}, u32[]{:S(2)}) copy-start(f32[3,8,16,128]{3,2,1,0:T(8,128)} %ip_in.3) | copy-start | bytes 589828
  0.6 8.2 %copy-start.2 = (f32[3,8,16,128]{3,2,1,0:T(8,128)S(1)}, f32[3,8,16,128]{3,2,1,0:T(8,128)}, u32[]{:S(2)}) copy-start(f32[3,8,16,128]{3,2,1,0:T(8,128)} %e_in.1) | copy-start | bytes 589828
  0.7 8.2 %copy-start.3 = (f32[3,8,16,128]{3,2,1,0:T(8,128)S(1)}, f32[3,8,16,128]{3,2,1,0:T(8,128)}, u32[]{:S(2)}) copy-start(f32[3,8,16,128]{3,2,1,0:T(8,128)} %h_in.1) | copy-start | bytes 589828
  2.3 6.6 %collective-permute-start.3 = (f32[96,8,128]{2,1,0:T(8,128)S(1)}, f32[96,8,128]{2,1,0:T(8,128)S(1)}, u32[]{:S(2)}, u32[]{:S(2)}) collective-permute-start(f32[96,8,128]{2,1,0:T(8,128)S(1)} %get-tuple-element.18), channel_id=1, source_target_pairs={{0,2},{2,0},{1,3},{3,1},{4,6},{6,4},{5,7},{7,5},{8,10},{10,8},{9,1... | collective-permute-start | bytes 1179656 | tf_op jit(solution)/shard_map/ppermute | solution.py:535
  2.8 4.8 %collective-permute-start.2 = (f32[3,16,128]{2,1,0:T(8,128)S(1)}, f32[3,16,128]{2,1,0:T(8,128)S(1)}, u32[]{:S(2)}, u32[]{:S(2)}) collective-permute-start(f32[3,16,128]{2,1,0:T(8,128)S(1)} %get-tuple-element.17), channel_id=1, source_target_pairs={{0,1},{1,0},{2,3},{3,2},{4,5},{5,4},{6,7},{7,6},{8,9},{9,8},{10,11... | collective-permute-start | bytes 73736 | tf_op jit(solution)/shard_map/ppermute | solution.py:561
  5.4 9.5 %collective-permute-start = (f32[18,16,128]{2,1,0:T(8,128)S(1)}, f32[18,16,128]{2,1,0:T(8,128)S(1)}, u32[]{:S(2)}, u32[]{:S(2)}) collective-permute-start(f32[18,16,128]{2,1,0:T(8,128)S(1)} %get-tuple-element.15), channel_id=1, source_target_pairs={{0,4},{4,0},{8,12},{12,8},{16,20},{20,16},{24,28},{28,24},{1,5},{5... | collective-permute-start | bytes 442376 | tf_op jit(solution)/shard_map/ppermute | solution.py:563
  6.9 8.1 %collective-permute-start.1 = (f32[18,16,128]{2,1,0:T(8,128)S(1)}, f32[18,16,128]{2,1,0:T(8,128)S(1)}, u32[]{:S(2)}, u32[]{:S(2)}) collective-permute-start(f32[18,16,128]{2,1,0:T(8,128)S(1)} %get-tuple-element.16), channel_id=1, source_target_pairs={{4,8},{8,4},{12,16},{16,12},{20,24},{24,20},{5,9},{9,5},{13,17},{1... | collective-permute-start | bytes 442376 | tf_op jit(solution)/shard_map/ppermute | solution.py:564
  7.6 1.2 %collective-permute-start.4 = (f32[3,8,128]{2,1,0:T(8,128)S(1)}, f32[3,8,128]{2,1,0:T(8,128)S(1)}, u32[]{:S(2)}, u32[]{:S(2)}) collective-permute-start(f32[3,8,128]{2,1,0:T(8,128)S(1)} %slice_select_fusion.2), channel_id=1, source_target_pairs={{0,2},{2,0},{1,3},{3,1},{4,6},{6,4},{5,7},{7,5},{8,10},{10,8},{9,1... | collective-permute-start | bytes 36872 | tf_op jit(solution)/shard_map/ppermute | solution.py:535
  9.9 8.0 %collective-permute-start.6 = (f32[10,24,128]{2,1,0:T(8,128)S(1)}, f32[10,24,128]{2,1,0:T(8,128)S(1)}, u32[]{:S(2)}, u32[]{:S(2)}) collective-permute-start(f32[10,24,128]{2,1,0:T(8,128)S(1)} %get-tuple-element.20.a_sent), channel_id=1, source_target_pairs={{0,4},{4,0},{8,12},{12,8},{16,20},{20,16},{24,28},{28,24},{1,5},{5... | collective-permute-start | bytes 368648 | tf_op jit(solution)/shard_map/ppermute | solution.py:583
  14.3 3.6 %collective-permute-start.7 = (f32[10,24,128]{2,1,0:T(8,128)S(1)}, f32[10,24,128]{2,1,0:T(8,128)S(1)}, u32[]{:S(2)}, u32[]{:S(2)}) collective-permute-start(f32[10,24,128]{2,1,0:T(8,128)S(1)} %get-tuple-element.21.b_sent), channel_id=1, source_target_pairs={{4,8},{8,4},{12,16},{16,12},{20,24},{24,20},{5,9},{9,5},{13,17},{1... | collective-permute-start | bytes 368648 | tf_op jit(solution)/shard_map/ppermute | solution.py:584
  15.0 2.9 %copy-start.1 = (f32[3,8,16,128]{3,2,1,0:T(8,128)S(1)}, f32[3,8,16,128]{3,2,1,0:T(8,128)}, u32[]{:S(2)}) copy-start(f32[3,8,16,128]{3,2,1,0:T(8,128)} %sd_in.1) | copy-start | bytes 589828
  15.1 2.9 %copy-start.4 = (s32[8,16,128]{2,1,0:T(8,128)S(1)}, s32[8,16,128]{2,1,0:T(8,128)}, u32[]{:S(2)}) copy-start(s32[8,16,128]{2,1,0:T(8,128)} %ids.1) | copy-start | bytes 196612
  15.1 2.9 %collective-permute-start.5 = (f32[36,8,128]{2,1,0:T(8,128)S(1)}, f32[36,8,128]{2,1,0:T(8,128)S(1)}, u32[]{:S(2)}, u32[]{:S(2)}) collective-permute-start(f32[36,8,128]{2,1,0:T(8,128)S(1)} %pad_maximum_fusion), channel_id=1, source_target_pairs={{0,2},{2,0},{1,3},{3,1},{4,6},{6,4},{5,7},{7,5},{8,10},{10,8},{9,1... | collective-permute-start | bytes 442376 | tf_op jit(solution)/shard_map/ppermute | solution.py:535
  20.3 6.2 %collective-permute-start.8 = (f32[8,128]{1,0:T(8,128)S(1)}, f32[8,128]{1,0:T(8,128)S(1)}, u32[]{:S(2)}, u32[]{:S(2)}) collective-permute-start(f32[8,128]{1,0:T(8,128)S(1)} %get-tuple-element.27), channel_id=1, source_target_pairs={{0,4},{4,0},{8,12},{12,8},{16,20},{20,16},{24,28},{28,24},{1,5},{5... | collective-permute-start | bytes 12296 | tf_op jit(solution)/shard_map/ppermute | solution.py:603

commit v7 on v6

--- a/solution.py
+++ b/solution.py
@@ -180,7 +180,7 @@
 
 
 def own_kernel(ip_in, e_in, h_in, y1, z_in, yz,
-               a_out, b_out, c_out, e_out, sc_out, se_out, I, E, H):
+               a_out, b_out, c_out, e_out, sc_out, se_out, si_out, I, E, H):
     at = Place()
     cx = e_in.shape[1]
     lane = at.lane
@@ -255,6 +255,7 @@
     for c in range(3):
         e_out[c] = E[c, 1 : cx + 1, 0:16]
     sput(se_out, se)
+    sput(si_out, si)
 
 
 def adjoint_kernel(ip_in, sd_in, a_in, b_in, z_in, y1, yz, y2,
@@ -284,7 +285,8 @@
             own = jnp.concatenate([z_in[t], at.y_part(yz[t])], axis=0)
             around = [X[c, DEEP + cx + k] for k in range(DEEP)] + [jnp.zeros((24, 128), F32)] * 2
             around += [X[c, k] for k in range(DEEP)]
-            s_out[q, :, 0:128] = at.strip_got(at.strip_own([X[c, DEEP + x] for x in range(cx)]), own, q)
+            if f == SEED:
+                s_out[q, :, 0:128] = at.strip_got(at.strip_own([X[c, DEEP + x] for x in range(cx)]), own, q)
             s_out[q, :, 128:256] = at.strip_own(around)
 
     def keep_at(x):
@@ -342,7 +344,7 @@
 HIGH_E = ([-1, 0], [-2, -1, 0, 1], [-3, -2, -1, 0], [-4, -3, -2, -1])
 
 
-def driven_kernel(a_sent, b_sent, high_in, low_in, e_own, sc_own, se_own, s_in, I, e_out, se_out, sg_out, E, H, CD):
+def driven_kernel(a_sent, b_sent, high_in, low_in, e_own, sc_own, se_own, si_own, s_in, I, e_out, se_out, sg_out, E, H, CD):
     at = Place()
     cx = e_own.shape[1]
     lane = at.lane
@@ -385,8 +387,9 @@
     strips = []
     for q in range(6):
         tile = at.strip_got(s_in[q, :, 128:256], edges[q // 4], q)
-        strips.append(jnp.concatenate([s_in[q, :, 0:128], tile], axis=1))
-    si = tuple(time_step * v for v in strips[0:3])
+        first = si_own[q] if q < 3 else s_in[q, :, 0:128]
+        strips.append(jnp.concatenate([first, time_step * tile if q < 3 else tile], axis=1))
+    si = tuple(strips[0:3])
     sp = tuple(strips[3:6])
     adjoint = [None] * (STEPS - 1) + [sp]
     sm = (0.0, 0.0, 0.0)
@@ -490,15 +493,19 @@
     sums = jnp.where(rows_of((24, 128)) % 8 == lanes_of((24, 128)) % 8, sums, 0.0)
     parts = [jnp.sum(sums[8 * c : 8 * c + 8], axis=0, keepdims=True) for c in range(3)]
     parts = jnp.concatenate(parts + [jnp.zeros((5, 128), F32)], axis=0)
-    fold = jnp.where(rows_of((128, 128)) // 8 == lanes_of((128, 128)), time_step * grad_scale, 0.0)
-    s_out[...] = jnp.dot(parts, fold, precision=lax.Precision.HIGHEST, preferred_element_type=F32)
-
-
-def last_kernel(ip_in, sd_in, a_got, b_got, z_in, y1, yz, y2, c_own, a_sent, b_sent, high_in, low_in, e_own, sc_own, se_own, ids,
+    one = parts.astype(jnp.bfloat16).astype(F32)
+    two = (parts - one).astype(jnp.bfloat16).astype(F32)
+    split = jnp.concatenate([one, two, (parts - one) - two, jnp.zeros((8, 128), F32)], axis=0).astype(jnp.bfloat16)
+    fold = jnp.where(rows_of((128, 128)) // 8 == lanes_of((128, 128)), 1.0, 0.0).astype(jnp.bfloat16)
+    folded = jnp.dot(split, fold, preferred_element_type=F32)
+    s_out[...] = (folded[0:8] + folded[8:16] + folded[16:24]) * (time_step * grad_scale)
+
+
+def last_kernel(ip_in, sd_in, a_got, b_got, z_in, y1, yz, y2, c_own, a_sent, b_sent, high_in, low_in, e_own, sc_own, se_own, si_own, ids,
                 e_out, se_out, s_out, I, W, M, PS, E, H, CD, s_ext, sg):
     runs = (
         adjoint_kernel(ip_in, sd_in, a_got, b_got, z_in, y1, yz, y2, s_ext, I, W, M, PS),
-        driven_kernel(a_sent, b_sent, high_in, low_in, e_own, sc_own, se_own, s_ext, I, e_out, se_out, sg, E, H, CD),
+        driven_kernel(a_sent, b_sent, high_in, low_in, e_own, sc_own, se_own, si_own, s_ext, I, e_out, se_out, sg, E, H, CD),
     )
     for _ in range(2 * STEPS + 1):
         for run in runs:
@@ -566,7 +573,7 @@
 
     n_msg = N_TRACES + 2
     field = tile(3, cx + 2, 24, 128)
-    a_sent, b_sent, c_own, e_own, sc_own, se_own = call(
+    a_sent, b_sent, c_own, e_own, sc_own, se_own, si_own = call(
         own_kernel,
         (
             shape(n_msg, 24, 128),
@@ -574,6 +581,7 @@
             shape(STEPS, 3, cx, 16, 128),
             shape(3, cx, 16, 128),
             shape(STEPS, 3, 24, 128),
+            shape(3, 24, 128),
             shape(3, 24, 128),
         ),
         [field] * 3,
@@ -596,7 +604,7 @@
         + [tile(STEPS, 3, planes, 24, 128)]
         + [driven] * 2
         + [tile(STEPS, 3, cx, 16, 128), tile(6, 24, 256), tile(3, 16, 128)],
-        (inv_perm, adj_seed, a_got, b_got, z_got, y1, yz, y2, c_own, a_sent, b_sent, high_in, low_in, e_own, sc_own, se_own, region_ids),
+        (inv_perm, adj_seed, a_got, b_got, z_got, y1, yz, y2, c_own, a_sent, b_sent, high_in, low_in, e_own, sc_own, se_own, si_own, region_ids),
         16,
     )
     (e_field,) = call(finish_kernel, (shape(*e_start.shape),), [], (e_main, e_strip), 4)

time: 27.6 us -> 27.4 us (level)
  no operation moved by 1% of the time
where the time goes in v7:
time: 27.4 us; the launch traced here: 27.1 us
  starting transfers between devices  15 us (55%)
  Pallas kernels  5.73 us (21%)
  waiting for transfers between devices  4.7 us (17%)
  other arithmetic  0.85 us (3%)
  between operations  0.82 us (3%)
    pallas_call x4, Pallas kernels, call(): pl.pallas_call(kernel, out_shape=outs, in_specs=specs or [vmem] * len(arg...  5.73 us
    ppermute x1, starting transfers between devices, local(): total = sums + lax.ppermute(sums, 'gx', a_pairs)  4.65 us
    ppermute x1, starting transfers between devices, local(): a_in = lax.ppermute(a_sent, 'gx', a_pairs)  4.34 us
    ppermute x1, waiting for transfers between devices, local(): a_in = lax.ppermute(a_sent, 'gx', a_pairs)  2.75 us
    ppermute x1, starting transfers between devices, local(): z_got = lax.ppermute(z_msg, 'gz', [(0, 1), (1, 0)])  2.59 us
    ppermute x1, starting transfers between devices, local(): a_got = lax.ppermute(a_msg, 'gx', a_pairs)  1.49 us
    ppermute x3, waiting for transfers between devices, swap_y(): return lax.ppermute(v, 'gy', [(0, 1), (1, 0)])  1.16 us
    ppermute x1, waiting for transfers between devices, local(): total = sums + lax.ppermute(sums, 'gx', a_pairs)  0.78 us
  transfers between devices with their start and end apart: 9, of which 3 were waited for; matrix products, arithmetic and copies ran while one was open for 1% of the time, Pallas kernels for 7%

profile of v7, /device:TPU:0, one launch (start us, length us, event | category | flops | bytes accessed | tf_op | source)
XLA Modules:
  0.0 27.1 jit_solution(5289178517974267126)
XLA Ops:
  0.7 1.6 %shard_map.68 = (f32[18,16,128]{2,1,0:T(8,128)S(1)}, f32[18,16,128]{2,1,0:T(8,128)S(1)}, f32[3,16,128]{2,1,0:T(8,128)S(1)}, f32[96,8,128]{2,1,0:T(8,128)S(1)}) custom-call(f32[3,8,16,128]{3,2,1,0:T(8,128)} %ip_in.3, f32[3,8,16,128]{3,2,1,0:T(8,128)} %sd_in.1, f32[3,8,16,128]{3,2,1,0:T(8,128)} %e_in.1, f32[3,8,16,128]{3,2,1,0:T(8,128)} %h_in.1), custom_call_target="tpu_custom_call" | custom-call | tf_op jit(solution)/shard_map/pallas_call | solution.py:549
  2.3 0.5 %collective-permute-start.3 = (f32[96,8,128]{2,1,0:T(8,128)S(1)}, f32[96,8,128]{2,1,0:T(8,128)S(1)}, u32[]{:S(2)}, u32[]{:S(2)}) collective-permute-start(f32[96,8,128]{2,1,0:T(8,128)S(1)} %get-tuple-element.19), channel_id=1, source_target_pairs={{0,2},{2,0},{1,3},{3,1},{4,6},{6,4},{5,7},{7,5},{8,10},{10,8},{9,1... | collective-permute-start | bytes 1179656 | tf_op jit(solution)/shard_map/ppermute | solution.py:542
  2.8 2.6 %collective-permute-start.2 = (f32[3,16,128]{2,1,0:T(8,128)S(1)}, f32[3,16,128]{2,1,0:T(8,128)S(1)}, u32[]{:S(2)}, u32[]{:S(2)}) collective-permute-start(f32[3,16,128]{2,1,0:T(8,128)S(1)} %get-tuple-element.18), channel_id=1, source_target_pairs={{0,1},{1,0},{2,3},{3,2},{4,5},{5,4},{6,7},{7,6},{8,9},{9,8},{10,11... | collective-permute-start | bytes 73736 | tf_op jit(solution)/shard_map/ppermute | solution.py:568
  5.4 1.5 %collective-permute-start = (f32[18,16,128]{2,1,0:T(8,128)S(1)}, f32[18,16,128]{2,1,0:T(8,128)S(1)}, u32[]{:S(2)}, u32[]{:S(2)}) collective-permute-start(f32[18,16,128]{2,1,0:T(8,128)S(1)} %get-tuple-element.16), channel_id=1, source_target_pairs={{0,4},{4,0},{8,12},{12,8},{16,20},{20,16},{24,28},{28,24},{1,5},{5... | collective-permute-start | bytes 442376 | tf_op jit(solution)/shard_map/ppermute | solution.py:570
  6.9 0.7 %collective-permute-start.1 = (f32[18,16,128]{2,1,0:T(8,128)S(1)}, f32[18,16,128]{2,1,0:T(8,128)S(1)}, u32[]{:S(2)}, u32[]{:S(2)}) collective-permute-start(f32[18,16,128]{2,1,0:T(8,128)S(1)} %get-tuple-element.17), channel_id=1, source_target_pairs={{4,8},{8,4},{12,16},{16,12},{20,24},{24,20},{5,9},{9,5},{13,17},{1... | collective-permute-start | bytes 442376 | tf_op jit(solution)/shard_map/ppermute | solution.py:571
  7.6 0.0 collective-permute-done.2.z_in
  7.6 0.1 slice_select_fusion.2
  7.6 0.0 collective-permute-start.4
  7.7 1.2 %collective-permute-done.4.yz = f32[3,8,128]{2,1,0:T(8,128)S(1)} collective-permute-done((f32[3,8,128]{2,1,0:T(8,128)S(1)}, f32[3,8,128]{2,1,0:T(8,128)S(1)}, u32[]{:S(2)}, u32[]{:S(2)}) %collective-permute-start.4) | collective-permute-done | bytes 12320 | tf_op jit(solution)/shard_map/ppermute | solution.py:542
  8.8 0.0 collective-permute-done.3.y1
  8.8 1.1 %shard_map.69 = (f32[10,24,128]{2,1,0:T(8,128)S(1)}, f32[10,24,128]{2,1,0:T(8,128)S(1)}, f32[4,3,8,16,128]{4,3,2,1,0:T(8,128)S(1)}, f32[3,8,16,128]{3,2,1,0:T(8,...) custom-call(f32[3,8,16,128]{3,2,1,0:T(8,128)S(1)} %copy-done, ...), custom_call_target="tpu_custom_call" | custom-call | tf_op jit(solution)/shard_map/pallas_call | solution.py:549
  9.9 4.3 %collective-permute-start.6 = (f32[10,24,128]{2,1,0:T(8,128)S(1)}, f32[10,24,128]{2,1,0:T(8,128)S(1)}, u32[]{:S(2)}, u32[]{:S(2)}) collective-permute-start(f32[10,24,128]{2,1,0:T(8,128)S(1)} %get-tuple-element.21.a_sent), channel_id=1, source_target_pairs={{0,4},{4,0},{8,12},{12,8},{16,20},{20,16},{24,28},{28,24},{1,5},{5... | collective-permute-start | bytes 368648 | tf_op jit(solution)/shard_map/ppermute | solution.py:591
  14.3 0.7 %collective-permute-start.7 = (f32[10,24,128]{2,1,0:T(8,128)S(1)}, f32[10,24,128]{2,1,0:T(8,128)S(1)}, u32[]{:S(2)}, u32[]{:S(2)}) collective-permute-start(f32[10,24,128]{2,1,0:T(8,128)S(1)} %get-tuple-element.22.b_sent), channel_id=1, source_target_pairs={{4,8},{8,4},{12,16},{16,12},{20,24},{24,20},{5,9},{9,5},{13,17},{1... | collective-permute-start | bytes 368648 | tf_op jit(solution)/shard_map/ppermute | solution.py:592
  14.9 0.0 collective-permute-done.a_got
  14.9 0.1 slice_select_fusion.1
  15.0 0.0 copy-start.1
  15.1 0.0 copy-start.4
  15.1 0.1 collective-permute-start.5
  15.1 2.8 %collective-permute-done.6 = f32[10,24,128]{2,1,0:T(8,128)S(1)} collective-permute-done((f32[10,24,128]{2,1,0:T(8,128)S(1)}, f32[10,24,128]{2,1,0:T(8,128)S(1)}, u32[]{:S(2)}, u32[]{:S(2)}) %collective-permute-start.6) | collective-permute-done | bytes 122912 | tf_op jit(solution)/shard_map/ppermute | solution.py:591
  18.0 2.3 %shard_map.70 = (f32[3,8,16,128]{3,2,1,0:T(8,128)S(1)}, f32[3,16,128]{2,1,0:T(8,128)S(1)}, f32[8,128]{1,0:T(8,128)S(1)}) custom-call(f32[3,8,16,128]{3,2,1,0:T(8,128)S(1)} %copy-done, f32[3,8,16,128]{3,2,1,0:T(8,128)S(1)} %copy-done.1, f32[18,16,128]{2,1,0:T(8,128)S(1)} %collective-permute-done.a_got, f32[18,16,128]{2,1,0:T(8,128)S(1)} %collective-permute-done.1.b_got, ...), custom_call_target="tpu_custom_call" | custom-call | tf_op jit(solution)/shard_map/pallas_call | solution.py:549
  20.2 4.7 %collective-permute-start.8 = (f32[8,128]{1,0:T(8,128)S(1)}, f32[8,128]{1,0:T(8,128)S(1)}, u32[]{:S(2)}, u32[]{:S(2)}) collective-permute-start(f32[8,128]{1,0:T(8,128)S(1)} %get-tuple-element.29), channel_id=1, source_target_pairs={{0,4},{4,0},{8,12},{12,8},{16,20},{20,16},{24,28},{28,24},{1,5},{5... | collective-permute-start | bytes 12296 | tf_op jit(solution)/shard_map/ppermute | solution.py:611
  24.9 0.8 %shard_map.71 = f32[3,8,16,128]{3,2,1,0:T(8,128)} custom-call(f32[3,8,16,128]{3,2,1,0:T(8,128)S(1)} %get-tuple-element.27.e_in, f32[3,16,128]{2,1,0:T(8,128)S(1)} %get-tuple-element.28.se_in), custom_call_target="tpu_custom_call" | custom-call | tf_op jit(solution)/shard_map/pallas_call | solution.py:549
  25.7 0.8 %collective-permute-done.8 = f32[8,128]{1,0:T(8,128)S(1)} collective-permute-done((f32[8,128]{1,0:T(8,128)S(1)}, f32[8,128]{1,0:T(8,128)S(1)}, u32[]{:S(2)}, u32[]{:S(2)}) %collective-permute-start.8) | collective-permute-done | bytes 4128 | tf_op jit(solution)/shard_map/ppermute | solution.py:611
  26.5 0.7 %slice_select_fusion.3 = f32[3,8]{1,0:T(4,128)} fusion(f32[8,128]{1,0:T(8,128)S(1)} %add.12, pred[]{:T(512)S(6)} %eq.4), kind=kLoop, calls=%fused_computation.6 | loop fusion | flops 24 | bytes 289 | tf_op jit(solution)/shard_map/jit(_where)/select_n | solution.py:612
  (15 shorter events, 0.1 us)
Async XLA Ops:
  0.6 8.2 %copy-start = (f32[3,8,16,128]{3,2,1,0:T(8,128)S(1)}, f32[3,8,16,128]{3,2,1,0:T(8,128)}, u32[]{:S(2)}) copy-start(f32[3,8,16,128]{3,2,1,0:T(8,128)} %ip_in.3) | copy-start | bytes 589828
  0.6 8.2 %copy-start.2 = (f32[3,8,16,128]{3,2,1,0:T(8,128)S(1)}, f32[3,8,16,128]{3,2,1,0:T(8,128)}, u32[]{:S(2)}) copy-start(f32[3,8,16,128]{3,2,1,0:T(8,128)} %e_in.1) | copy-start | bytes 589828
  0.7 8.2 %copy-start.3 = (f32[3,8,16,128]{3,2,1,0:T(8,128)S(1)}, f32[3,8,16,128]{3,2,1,0:T(8,128)}, u32[]{:S(2)}) copy-start(f32[3,8,16,128]{3,2,1,0:T(8,128)} %h_in.1) | copy-start | bytes 589828
  2.3 6.6 %collective-permute-start.3 = (f32[96,8,128]{2,1,0:T(8,128)S(1)}, f32[96,8,128]{2,1,0:T(8,128)S(1)}, u32[]{:S(2)}, u32[]{:S(2)}) collective-permute-start(f32[96,8,128]{2,1,0:T(8,128)S(1)} %get-tuple-element.19), channel_id=1, source_target_pairs={{0,2},{2,0},{1,3},{3,1},{4,6},{6,4},{5,7},{7,5},{8,10},{10,8},{9,1... | collective-permute-start | bytes 1179656 | tf_op jit(solution)/shard_map/ppermute | solution.py:542
  2.8 4.8 %collective-permute-start.2 = (f32[3,16,128]{2,1,0:T(8,128)S(1)}, f32[3,16,128]{2,1,0:T(8,128)S(1)}, u32[]{:S(2)}, u32[]{:S(2)}) collective-permute-start(f32[3,16,128]{2,1,0:T(8,128)S(1)} %get-tuple-element.18), channel_id=1, source_target_pairs={{0,1},{1,0},{2,3},{3,2},{4,5},{5,4},{6,7},{7,6},{8,9},{9,8},{10,11... | collective-permute-start | bytes 73736 | tf_op jit(solution)/shard_map/ppermute | solution.py:568
  5.4 9.5 %collective-permute-start = (f32[18,16,128]{2,1,0:T(8,128)S(1)}, f32[18,16,128]{2,1,0:T(8,128)S(1)}, u32[]{:S(2)}, u32[]{:S(2)}) collective-permute-start(f32[18,16,128]{2,1,0:T(8,128)S(1)} %get-tuple-element.16), channel_id=1, source_target_pairs={{0,4},{4,0},{8,12},{12,8},{16,20},{20,16},{24,28},{28,24},{1,5},{5... | collective-permute-start | bytes 442376 | tf_op jit(solution)/shard_map/ppermute | solution.py:570
  6.9 8.1 %collective-permute-start.1 = (f32[18,16,128]{2,1,0:T(8,128)S(1)}, f32[18,16,128]{2,1,0:T(8,128)S(1)}, u32[]{:S(2)}, u32[]{:S(2)}) collective-permute-start(f32[18,16,128]{2,1,0:T(8,128)S(1)} %get-tuple-element.17), channel_id=1, source_target_pairs={{4,8},{8,4},{12,16},{16,12},{20,24},{24,20},{5,9},{9,5},{13,17},{1... | collective-permute-start | bytes 442376 | tf_op jit(solution)/shard_map/ppermute | solution.py:571
  7.6 1.2 %collective-permute-start.4 = (f32[3,8,128]{2,1,0:T(8,128)S(1)}, f32[3,8,128]{2,1,0:T(8,128)S(1)}, u32[]{:S(2)}, u32[]{:S(2)}) collective-permute-start(f32[3,8,128]{2,1,0:T(8,128)S(1)} %slice_select_fusion.2), channel_id=1, source_target_pairs={{0,2},{2,0},{1,3},{3,1},{4,6},{6,4},{5,7},{7,5},{8,10},{10,8},{9,1... | collective-permute-start | bytes 36872 | tf_op jit(solution)/shard_map/ppermute | solution.py:542
  9.9 8.0 %collective-permute-start.6 = (f32[10,24,128]{2,1,0:T(8,128)S(1)}, f32[10,24,128]{2,1,0:T(8,128)S(1)}, u32[]{:S(2)}, u32[]{:S(2)}) collective-permute-start(f32[10,24,128]{2,1,0:T(8,128)S(1)} %get-tuple-element.21.a_sent), channel_id=1, source_target_pairs={{0,4},{4,0},{8,12},{12,8},{16,20},{20,16},{24,28},{28,24},{1,5},{5... | collective-permute-start | bytes 368648 | tf_op jit(solution)/shard_map/ppermute | solution.py:591
  14.3 3.6 %collective-permute-start.7 = (f32[10,24,128]{2,1,0:T(8,128)S(1)}, f32[10,24,128]{2,1,0:T(8,128)S(1)}, u32[]{:S(2)}, u32[]{:S(2)}) collective-permute-start(f32[10,24,128]{2,1,0:T(8,128)S(1)} %get-tuple-element.22.b_sent), channel_id=1, source_target_pairs={{4,8},{8,4},{12,16},{16,12},{20,24},{24,20},{5,9},{9,5},{13,17},{1... | collective-permute-start | bytes 368648 | tf_op jit(solution)/shard_map/ppermute | solution.py:592
  15.0 2.9 %copy-start.1 = (f32[3,8,16,128]{3,2,1,0:T(8,128)S(1)}, f32[3,8,16,128]{3,2,1,0:T(8,128)}, u32[]{:S(2)}) copy-start(f32[3,8,16,128]{3,2,1,0:T(8,128)} %sd_in.1) | copy-start | bytes 589828
  15.1 2.9 %copy-start.4 = (s32[8,16,128]{2,1,0:T(8,128)S(1)}, s32[8,16,128]{2,1,0:T(8,128)}, u32[]{:S(2)}) copy-start(s32[8,16,128]{2,1,0:T(8,128)} %ids.1) | copy-start | bytes 196612
  15.1 2.9 %collective-permute-start.5 = (f32[36,8,128]{2,1,0:T(8,128)S(1)}, f32[36,8,128]{2,1,0:T(8,128)S(1)}, u32[]{:S(2)}, u32[]{:S(2)}) collective-permute-start(f32[36,8,128]{2,1,0:T(8,128)S(1)} %pad_maximum_fusion), channel_id=1, source_target_pairs={{0,2},{2,0},{1,3},{3,1},{4,6},{6,4},{5,7},{7,5},{8,10},{10,8},{9,1... | collective-permute-start | bytes 442376 | tf_op jit(solution)/shard_map/ppermute | solution.py:542
  20.2 6.2 %collective-permute-start.8 = (f32[8,128]{1,0:T(8,128)S(1)}, f32[8,128]{1,0:T(8,128)S(1)}, u32[]{:S(2)}, u32[]{:S(2)}) collective-permute-start(f32[8,128]{1,0:T(8,128)S(1)} %get-tuple-element.29), channel_id=1, source_target_pairs={{0,4},{4,0},{8,12},{12,8},{16,20},{20,16},{24,28},{28,24},{1,5},{5... | collective-permute-start | bytes 12296 | tf_op jit(solution)/shard_map/ppermute | solution.py:611
